TPU v7x, 512 devices: a whole 4x4x16 slice. The times are simulated.
512 devices in a mesh: comp: 8 (over y, core), tile: 64 (over x, z).
Axes of the slice: x: 4, y: 4, z: 16, core: 2. Of those that a mesh axis runs over, the one named last changes fastest.
Arguments:
- spectrum: float32 [1296, 256, 512], P('comp', 'tile'), may hold values from 0.05 to 1
- sea_mask: int32 [256, 512], P('tile'), may hold values 0 or 1
- quad_bins: int32 [4, 1296], replicated, may hold values from 0 to 1295
- coupling: float32 [1296], replicated, may hold values from 0.05 to 0.5
- growth: float32 [1296], replicated, may hold values from -0.2 to 0.4
Outputs:
- updated: float32 [1296, 256, 512], P('comp', 'tile')
All inputs are finite; a program needn't handle non-finite values. No bound on the sum of `sea_mask` on one device may be relied on, other than what follows from the above.
Results may differ from a plain program's by a relative error of at most 0.0001.
Values sent between devices are 32-bit elements; how exact they have to be, the bound alone decides.
No kernel may reach another device: no remote copies, remote signals or barrier semaphores. Data moves between devices by JAX's collectives and lax.ppermute only.
A program may use at most 192 MiB of HBM per device.

v0:
```python
import math

import jax
import jax.numpy as jnp
from jax import lax
from jax.sharding import PartitionSpec as P

NDIR = 36
NFREQ = 36
SUB = 4


w_plus = 0.4096
w_minus = 3.1605
w_cross = 1.2945
time_step = 0.5


def extended_2(shard, sides, width):
    for axis, dim in sides:
        count, length = (lax.axis_size(axis), shard.shape[dim])
        up = [(i, (i + 1) % count) for i in range(count - 1)]
        down = [(j, i) for i, j in up]
        last = lax.slice_in_dim(shard, length - width, length, axis=dim)
        first = lax.slice_in_dim(shard, 0, width, axis=dim)
        before = lax.ppermute(last, axis, up)
        after = lax.ppermute(first, axis, down)
        shard = jnp.concatenate([before, shard, after], axis=dim)
    return shard


def courant_numbers(index):
    direction = (index // NFREQ).astype(jnp.float32)
    level = (index % NFREQ).astype(jnp.float32)
    angle = 2.0 * math.pi * direction / NDIR
    magnitude = 0.7 * jnp.power(jnp.float32(0.93), level)
    return (magnitude * jnp.cos(angle), magnitude * jnp.sin(angle))


def advect(extended, along_x, along_y, mask):
    center = extended[:, 1:-1, :]
    west = extended[:, :-2, :]
    east = extended[:, 2:, :]
    padded_y = jnp.pad(center, ((0, 0), (0, 0), (1, 1)))
    south = padded_y[:, :, :-2]
    north = padded_y[:, :, 2:]
    pos_x = jnp.maximum(along_x, 0.0)[:, None, None]
    neg_x = jnp.minimum(along_x, 0.0)[:, None, None]
    pos_y = jnp.maximum(along_y, 0.0)[:, None, None]
    neg_y = jnp.minimum(along_y, 0.0)[:, None, None]
    moved = center - pos_x * (center - west) - neg_x * (east - center)
    moved = moved - pos_y * (center - south) - neg_y * (north - center)
    return moved * mask


def settle(energy, quad_bins, coupling, growth):
    count = energy.shape[0]
    total = growth[:, None] * energy
    for mirror in range(2):
        plus_bins = quad_bins[2 * mirror]
        minus_bins = quad_bins[2 * mirror + 1]
        plus_energy = jnp.take(energy, plus_bins, axis=0)
        minus_energy = jnp.take(energy, minus_bins, axis=0)
        delta = coupling[:, None] * (
            energy * energy * (w_plus * plus_energy + w_minus * minus_energy)
            - 2.0 * w_cross * energy * plus_energy * minus_energy
        )
        total = total - 2.0 * delta
        total = total + jax.ops.segment_sum(delta, plus_bins, num_segments=count)
        total = total + jax.ops.segment_sum(delta, minus_bins, num_segments=count)
    return energy + time_step * total


def per_device(spectrum, sea_mask, quad_bins, coupling, growth):
    comp_dev, width, height = spectrum.shape
    groups = lax.axis_size("comp")
    first = lax.axis_index("comp") * comp_dev
    along_x, along_y = courant_numbers(first + jnp.arange(comp_dev, dtype=jnp.int32))
    mask = sea_mask.astype(jnp.float32)[None]
    field = spectrum
    for step in range(SUB):
        extended = extended_2(field, (("tile", 1),), 1)
        field = advect(extended, along_x, along_y, mask)
    cells = width * height
    pieces = field.reshape(comp_dev, groups, cells // groups)
    fresh = settle(
        lax.all_to_all(pieces, "comp", split_axis=1, concat_axis=0, tiled=True)[:, 0, :],
        quad_bins,
        coupling,
        growth,
    )
    result = lax.all_to_all(fresh[:, None, :], "comp", split_axis=0, concat_axis=1, tiled=True)
    return result.reshape(comp_dev, width, height)


def solution(mesh):
    return jax.shard_map(
        per_device,
        mesh=mesh,
        in_specs=(P("comp", "tile", None), P("tile", None), P(), P(), P()),
        out_specs=P("comp", "tile", None),
        check_vma=False,
    )
```

profile of v0, /device:TPU:7, one launch (start us, length us, event | category | flops | bytes accessed | tf_op | source)
XLA Modules:
  0.0 198.9 jit_solution(6207487047705108573)
XLA Ops:
  0.0 1.8 copy.40
  1.8 3.5 %collective-permute-start = (f32[162,1,512]{2,0,1:T(8,128)S(1)}, f32[162,1,512]{2,0,1:T(8,128)S(1)}, u32[]{:S(2)}, u32[]{:S(2)}) collective-permute-start(f32[162,1,512]{2,0,1:T(8,128)S(1)} %get-tuple-element.20), channel_id=1, source_target_pairs={{0,1},{1,2},{2,3},{3,4},{4,5},{5,6},{6,7},{7,8},{8,9},{9,10},{10,1... | collective-permute-start | bytes 995336 | tf_op jit(solution)/shard_map/ppermute | solution.py:26
  5.4 9.8 %collective-permute-start.1 = (f32[162,1,512]{2,0,1:T(8,128)S(1)}, f32[162,1,512]{2,0,1:T(8,128)S(1)}, u32[]{:S(2)}, u32[]{:S(2)}) collective-permute-start(f32[162,1,512]{2,0,1:T(8,128)S(1)} %get-tuple-element.21), channel_id=1, source_target_pairs={{1,0},{2,1},{3,2},{4,3},{5,4},{6,5},{7,6},{8,7},{9,8},{10,9},{11,1... | collective-permute-start | bytes 995336 | tf_op jit(solution)/shard_map/ppermute | solution.py:27
  15.2 0.1 broadcast_minimum_fusion
  15.2 0.1 broadcast_minimum_fusion.1
  15.3 5.7 %collective-permute-done = f32[162,1,512]{2,0,1:T(8,128)S(1)} collective-permute-done((f32[162,1,512]{2,0,1:T(8,128)S(1)}, f32[162,1,512]{2,0,1:T(8,128)S(1)}, u32[]{:S(2)}, u32[]{:S(2)}) %collective-permute-start) | collective-permute-done | bytes 331808 | tf_op jit(solution)/shard_map/ppermute | solution.py:26
  21.0 0.9 collective-permute-done.1
  21.9 1.0 fusion.4
  22.9 1.9 collective-permute-start.2
  24.8 6.2 %collective-permute-start.3 = (f32[162,1,512]{2,0,1:T(8,128)S(1)}, f32[162,1,512]{2,0,1:T(8,128)S(1)}, u32[]{:S(2)}, u32[]{:S(2)}) collective-permute-start(f32[162,1,512]{2,0,1:T(8,128)S(1)} %get-tuple-element.19), channel_id=1, source_target_pairs={{1,0},{2,1},{3,2},{4,3},{5,4},{6,5},{7,6},{8,7},{9,8},{10,9},{11,1... | collective-permute-start | bytes 995336 | tf_op jit(solution)/shard_map/ppermute | solution.py:27
  31.1 4.9 %collective-permute-done.2 = f32[162,1,512]{2,0,1:T(8,128)S(1)} collective-permute-done((f32[162,1,512]{2,0,1:T(8,128)S(1)}, f32[162,1,512]{2,0,1:T(8,128)S(1)}, u32[]{:S(2)}, u32[]{:S(2)}) %collective-permute-start.2) | collective-permute-done | bytes 331808 | tf_op jit(solution)/shard_map/ppermute | solution.py:26
  36.0 0.9 collective-permute-done.3
  36.9 1.0 fusion.11
  37.9 1.9 collective-permute-start.4
  39.8 6.2 %collective-permute-start.5 = (f32[162,1,512]{2,0,1:T(8,128)S(1)}, f32[162,1,512]{2,0,1:T(8,128)S(1)}, u32[]{:S(2)}, u32[]{:S(2)}) collective-permute-start(f32[162,1,512]{2,0,1:T(8,128)S(1)} %get-tuple-element.17), channel_id=1, source_target_pairs={{1,0},{2,1},{3,2},{4,3},{5,4},{6,5},{7,6},{8,7},{9,8},{10,9},{11,1... | collective-permute-start | bytes 995336 | tf_op jit(solution)/shard_map/ppermute | solution.py:27
  46.1 4.0 %collective-permute-done.4 = f32[162,1,512]{2,0,1:T(8,128)S(1)} collective-permute-done((f32[162,1,512]{2,0,1:T(8,128)S(1)}, f32[162,1,512]{2,0,1:T(8,128)S(1)}, u32[]{:S(2)}, u32[]{:S(2)}) %collective-permute-start.4) | collective-permute-done | bytes 331808 | tf_op jit(solution)/shard_map/ppermute | solution.py:26
  50.0 0.9 collective-permute-done.5
  50.9 1.0 fusion.18
  51.9 0.0 copy-start.2
  52.0 1.9 collective-permute-start.6
  53.9 6.2 %collective-permute-start.7 = (f32[162,1,512]{2,0,1:T(8,128)S(1)}, f32[162,1,512]{2,0,1:T(8,128)S(1)}, u32[]{:S(2)}, u32[]{:S(2)}) collective-permute-start(f32[162,1,512]{2,0,1:T(8,128)S(1)} %get-tuple-element.15), channel_id=1, source_target_pairs={{1,0},{2,1},{3,2},{4,3},{5,4},{6,5},{7,6},{8,7},{9,8},{10,9},{11,1... | collective-permute-start | bytes 995336 | tf_op jit(solution)/shard_map/ppermute | solution.py:27
  60.2 0.1 slice_reduce_fusion.3
  60.2 3.0 %collective-permute-done.6 = f32[162,1,512]{2,0,1:T(8,128)S(1)} collective-permute-done((f32[162,1,512]{2,0,1:T(8,128)S(1)}, f32[162,1,512]{2,0,1:T(8,128)S(1)}, u32[]{:S(2)}, u32[]{:S(2)}) %collective-permute-start.6) | collective-permute-done | bytes 331808 | tf_op jit(solution)/shard_map/ppermute | solution.py:26
  63.2 1.1 collective-permute-done.7
  64.3 1.0 fusion.25
  65.3 0.9 copy.47
  66.2 0.5 reshape.51
  66.7 1.5 copy.48
  68.2 8.7 %all-to-all-start = ((f32[162,8,256]{2,0,1:T(8,128)}), f32[162,8,256]{2,0,1:T(8,128)S(1)}, u32[]{:S(2)}, u32[]{:S(2)}) async-start(f32[162,8,256]{2,0,1:T(8,128)} %copy.48), calls=%async_computation | async-start | bytes 2752512 | tf_op jit(solution)/shard_map/all_to_all | solution.py:87
  77.0 18.5 %all-to-all-done = f32[162,8,256]{2,0,1:T(8,128)S(1)} async-done(((f32[162,8,256]{2,0,1:T(8,128)}), f32[162,8,256]{2,0,1:T(8,128)S(1)}, u32[]{:S(2)}, u32[]{:S(2)}) %all-to-all-start) | async-done | bytes 1327136 | tf_op jit(solution)/shard_map/all_to_all | solution.py:87
  95.6 0.2 squeeze.15
  95.7 4.5 %gather_fusion = f32[1296,256]{1,0:T(8,128)} fusion(f32[1296,256]{1,0:T(8,128)S(1)} %squeeze.15, s32[2048]{0:T(1024)S(1)} %pad_clamp_fusion.3), kind=kCustom, calls=%fused_computation.clone | custom fusion | bytes 2659392 | tf_op jit(solution)/shard_map/jit(_take)/gather | solution.py:62
  100.2 4.5 %gather_fusion.1 = f32[1296,256]{1,0:T(8,128)} fusion(f32[1296,256]{1,0:T(8,128)S(1)} %squeeze.15, s32[2048]{0:T(1024)S(1)} %pad_clamp_fusion.2), kind=kCustom, calls=%fused_computation.1.clone | custom fusion | bytes 2659392 | tf_op jit(solution)/shard_map/jit(_take)/gather | solution.py:63
  104.8 4.1 %multiply_subtract_fusion.1 = (f32[1296,256]{1,0:T(8,128)S(1)}, f32[1296,256]{1,0:T(8,128)}) fusion(f32[1296,256]{1,0:T(8,128)S(1)} %squeeze.15, f32[1296]{0:T(1024)S(1)} %copy-done.3, f32[1296,256]{1,0:T(8,128)} %gather_fusion.1, pred[1296]{0:T(1024)(128)(4,1)S(1)} %get-tuple-element.32, f32[1296,256]{1,0:T(8,128)} %gather_fusion, ...), kind=kLoop, calls=%fused_computation.79 | loop fusion | flops 4976640 | bytes 6648480 | tf_op jit(solution)/shard_map/sub | solution.py:68
  108.9 9.6 %scatter_custom_fusion.1 = f32[1296,256]{1,0:T(8,128)} fusion(s32[1296]{0:T(1024)S(1)} %get-tuple-element.7, f32[1296,256]{1,0:T(8,128)} %get-tuple-element.13, f32[]{:T(128)} %constant.56.clone.1), kind=kCustom, calls=%fused_computation.83 | custom fusion | flops 331776 | bytes 1327616 | tf_op jit(solution)/shard_map/scatter-add | solution.py:70
  118.5 9.7 %scatter_fusion = f32[1296,256]{1,0:T(8,128)S(1)} fusion(f32[1296,256]{1,0:T(8,128)S(1)} %get-tuple-element.12, s32[1296]{0:T(1024)S(1)} %get-tuple-element.6, f32[1296,256]{1,0:T(8,128)} %get-tuple-element.13), kind=kCustom, calls=%fused_computation.4 | custom fusion | flops 331776 | bytes 3986496 | tf_op jit(solution)/shard_map/scatter-add | solution.py:69
  128.2 4.5 %gather_fusion.2 = f32[1296,256]{1,0:T(8,128)} fusion(f32[1296,256]{1,0:T(8,128)S(1)} %squeeze.15, s32[2048]{0:T(1024)S(1)} %pad_clamp_fusion.1), kind=kCustom, calls=%fused_computation.2.clone | custom fusion | bytes 2659392 | tf_op jit(solution)/shard_map/jit(_take)/gather | solution.py:62
  132.8 4.6 %gather_fusion.3 = f32[1296,256]{1,0:T(8,128)} fusion(f32[1296,256]{1,0:T(8,128)S(1)} %squeeze.15, s32[2048]{0:T(1024)S(1)} %pad_clamp_fusion), kind=kCustom, calls=%fused_computation.3.clone | custom fusion | bytes 2659392 | tf_op jit(solution)/shard_map/jit(_take)/gather | solution.py:63
  137.3 3.9 %multiply_subtract_fusion = (f32[1296,256]{1,0:T(8,128)S(1)}, f32[1296,256]{1,0:T(8,128)}) fusion(f32[1296,256]{1,0:T(8,128)} %copy-done, f32[1296,256]{1,0:T(8,128)} %scatter_custom_fusion.1, f32[1296,256]{1,0:T(8,128)S(1)} %squeeze.15, f32[1296,256]{1,0:T(8,128)} %gather_fusion.3, pred[1296]{0:T(1024)(128)(4,1)S(1)} %get-tuple-element.30, ...), kind=kLoop, calls=%fused_computation.77 | loop fusion | flops 4976640 | bytes 9297504 | tf_op jit(solution)/shard_map/sub | solution.py:68
  141.3 9.6 %scatter_custom_fusion.3 = f32[1296,256]{1,0:T(8,128)} fusion(s32[1296]{0:T(1024)S(1)} %get-tuple-element.8, f32[1296,256]{1,0:T(8,128)} %get-tuple-element.11, f32[]{:T(128)} %constant.56.clone.1), kind=kCustom, calls=%fused_computation.81 | custom fusion | flops 331776 | bytes 1327616 | tf_op jit(solution)/shard_map/scatter-add | solution.py:70
  150.9 9.7 %scatter_fusion.1 = f32[1296,256]{1,0:T(8,128)S(1)} fusion(f32[1296,256]{1,0:T(8,128)S(1)} %get-tuple-element.10, s32[1296]{0:T(1024)S(1)} %get-tuple-element.9, f32[1296,256]{1,0:T(8,128)} %get-tuple-element.11), kind=kCustom, calls=%fused_computation.6 | custom fusion | flops 331776 | bytes 3986496 | tf_op jit(solution)/shard_map/scatter-add | solution.py:69
  160.6 1.6 add_bitcast_fusion
  162.2 5.7 %copy.49 = f32[1296,1,256]{2,1,0:T(1,128)S(1)} copy(f32[1296,1,256]{2,0,1:T(8,128)S(1)} %add_bitcast_fusion) | data formatting | bytes 2654208 | tf_op jit(solution)/shard_map/broadcast_in_dim | solution.py:92
  167.9 21.9 %all_to_all.30 = f32[1296,1,256]{2,1,0:T(1,128)S(1)} all-to-all(f32[1296,1,256]{2,1,0:T(1,128)S(1)} %copy.49), channel_id=1, replica_groups=mesh['comp'=8,'tile'=64] {'comp'}, dimensions={0} | all-to-all | bytes 2654208 | tf_op jit(solution)/shard_map/all_to_all | solution.py:92
  189.8 6.9 %reduce.4 = f32[1296,256]{1,0:T(8,128)S(1)} reduce(f32[1296,1,256]{2,1,0:T(1,128)S(1)} %all_to_all.30, f32[]{:T(128)} %constant.76), dimensions={1}, to_apply=%all_to_all.25.reduce_sub_computation | reduce | bytes 2654212 | tf_op jit(solution)/shard_map/all_to_all | solution.py:92
  196.7 0.2 all_to_all.26
  196.8 0.4 copy.50
  197.3 1.7 reshape.52
  (22 shorter events, 0.3 us)
Async XLA Ops:
  0.0 15.2 %copy-start.4 = (s32[4,512]{1,0:T(4,128)S(1)}, s32[4,512]{1,0:T(4,128)}, u32[]{:S(2)}) copy-start(s32[4,512]{1,0:T(4,128)} %param.8) | copy-start | bytes 24580
  1.8 19.2 %collective-permute-start = (f32[162,1,512]{2,0,1:T(8,128)S(1)}, f32[162,1,512]{2,0,1:T(8,128)S(1)}, u32[]{:S(2)}, u32[]{:S(2)}) collective-permute-start(f32[162,1,512]{2,0,1:T(8,128)S(1)} %get-tuple-element.20), channel_id=1, source_target_pairs={{0,1},{1,2},{2,3},{3,4},{4,5},{5,6},{6,7},{7,8},{8,9},{9,10},{10,1... | collective-permute-start | bytes 995336 | tf_op jit(solution)/shard_map/ppermute | solution.py:26
  5.4 16.5 %collective-permute-start.1 = (f32[162,1,512]{2,0,1:T(8,128)S(1)}, f32[162,1,512]{2,0,1:T(8,128)S(1)}, u32[]{:S(2)}, u32[]{:S(2)}) collective-permute-start(f32[162,1,512]{2,0,1:T(8,128)S(1)} %get-tuple-element.21), channel_id=1, source_target_pairs={{1,0},{2,1},{3,2},{4,3},{5,4},{6,5},{7,6},{8,7},{9,8},{10,9},{11,1... | collective-permute-start | bytes 995336 | tf_op jit(solution)/shard_map/ppermute | solution.py:27
  22.9 13.0 %collective-permute-start.2 = (f32[162,1,512]{2,0,1:T(8,128)S(1)}, f32[162,1,512]{2,0,1:T(8,128)S(1)}, u32[]{:S(2)}, u32[]{:S(2)}) collective-permute-start(f32[162,1,512]{2,0,1:T(8,128)S(1)} %get-tuple-element.18), channel_id=1, source_target_pairs={{0,1},{1,2},{2,3},{3,4},{4,5},{5,6},{6,7},{7,8},{8,9},{9,10},{10,1... | collective-permute-start | bytes 995336 | tf_op jit(solution)/shard_map/ppermute | solution.py:26
  24.8 12.0 %collective-permute-start.3 = (f32[162,1,512]{2,0,1:T(8,128)S(1)}, f32[162,1,512]{2,0,1:T(8,128)S(1)}, u32[]{:S(2)}, u32[]{:S(2)}) collective-permute-start(f32[162,1,512]{2,0,1:T(8,128)S(1)} %get-tuple-element.19), channel_id=1, source_target_pairs={{1,0},{2,1},{3,2},{4,3},{5,4},{6,5},{7,6},{8,7},{9,8},{10,9},{11,1... | collective-permute-start | bytes 995336 | tf_op jit(solution)/shard_map/ppermute | solution.py:27
  37.9 12.1 %collective-permute-start.4 = (f32[162,1,512]{2,0,1:T(8,128)S(1)}, f32[162,1,512]{2,0,1:T(8,128)S(1)}, u32[]{:S(2)}, u32[]{:S(2)}) collective-permute-start(f32[162,1,512]{2,0,1:T(8,128)S(1)} %get-tuple-element.16), channel_id=1, source_target_pairs={{0,1},{1,2},{2,3},{3,4},{4,5},{5,6},{6,7},{7,8},{8,9},{9,10},{10,1... | collective-permute-start | bytes 995336 | tf_op jit(solution)/shard_map/ppermute | solution.py:26
  39.8 11.1 %collective-permute-start.5 = (f32[162,1,512]{2,0,1:T(8,128)S(1)}, f32[162,1,512]{2,0,1:T(8,128)S(1)}, u32[]{:S(2)}, u32[]{:S(2)}) collective-permute-start(f32[162,1,512]{2,0,1:T(8,128)S(1)} %get-tuple-element.17), channel_id=1, source_target_pairs={{1,0},{2,1},{3,2},{4,3},{5,4},{6,5},{7,6},{8,7},{9,8},{10,9},{11,1... | collective-permute-start | bytes 995336 | tf_op jit(solution)/shard_map/ppermute | solution.py:27
  51.9 8.2 %copy-start.2 = (s32[4,1296]{1,0:T(4,128)S(1)}, s32[4,1296]{1,0:T(4,128)}, u32[]{:S(2)}) copy-start(s32[4,1296]{1,0:T(4,128)} %param.9) | copy-start | bytes 62212
  52.0 11.2 %collective-permute-start.6 = (f32[162,1,512]{2,0,1:T(8,128)S(1)}, f32[162,1,512]{2,0,1:T(8,128)S(1)}, u32[]{:S(2)}, u32[]{:S(2)}) collective-permute-start(f32[162,1,512]{2,0,1:T(8,128)S(1)} %get-tuple-element.14), channel_id=1, source_target_pairs={{0,1},{1,2},{2,3},{3,4},{4,5},{5,6},{6,7},{7,8},{8,9},{9,10},{10,1... | collective-permute-start | bytes 995336 | tf_op jit(solution)/shard_map/ppermute | solution.py:26
  53.9 10.4 %collective-permute-start.7 = (f32[162,1,512]{2,0,1:T(8,128)S(1)}, f32[162,1,512]{2,0,1:T(8,128)S(1)}, u32[]{:S(2)}, u32[]{:S(2)}) collective-permute-start(f32[162,1,512]{2,0,1:T(8,128)S(1)} %get-tuple-element.15), channel_id=1, source_target_pairs={{1,0},{2,1},{3,2},{4,3},{5,4},{6,5},{7,6},{8,7},{9,8},{10,9},{11,1... | collective-permute-start | bytes 995336 | tf_op jit(solution)/shard_map/ppermute | solution.py:27
  68.2 27.3 %all-to-all-start = ((f32[162,8,256]{2,0,1:T(8,128)}), f32[162,8,256]{2,0,1:T(8,128)S(1)}, u32[]{:S(2)}, u32[]{:S(2)}) async-start(f32[162,8,256]{2,0,1:T(8,128)} %copy.48), calls=%async_computation | async-start | bytes 2752512 | tf_op jit(solution)/shard_map/all_to_all | solution.py:87
  100.2 4.6 %copy-start.1 = (f32[1296]{0:T(1024)S(1)}, f32[1296]{0:T(1024)}, u32[]{:S(2)}) copy-start(f32[1296]{0:T(1024)} %param.10) | copy-start | bytes 15556
  100.2 4.6 %copy-start.3 = (f32[1296]{0:T(1024)S(1)}, f32[1296]{0:T(1024)}, u32[]{:S(2)}) copy-start(f32[1296]{0:T(1024)} %param.11) | copy-start | bytes 15556
  128.2 4.6 %copy-start = (f32[1296,256]{1,0:T(8,128)}, f32[1296,256]{1,0:T(8,128)S(1)}, u32[]{:S(2)}) copy-start(f32[1296,256]{1,0:T(8,128)S(1)} %scatter_fusion) | copy-start | bytes 3981316
where the time goes:
time: 200 us; the launch traced here: 199 us
  other arithmetic  59.3 us (30%)
  starting transfers between devices  46.4 us (23%)
  waiting for transfers between devices  39.8 us (20%)
  local copies, waits for them, and re-layouts  31.2 us (16%)
  blocking collectives  21.9 us (11%)
    ppermute x4, starting transfers between devices, extended_2(): after = lax.ppermute(first, axis, down)  28.4 us
    all_to_all x1, blocking collectives, per_device(): lax.all_to_all(fresh[:, None, :], 'comp', split_axis=0, concat_axis=1, ti...  21.9 us
    scatter-add x2, other arithmetic, settle(): total = total + jax.ops.segment_sum(delta, plus_bins, num_segments=count)  19.4 us
    scatter-add x2, other arithmetic, settle(): total = total + jax.ops.segment_sum(delta, minus_bins, num_segments=count)  19.2 us
    all_to_all x1, waiting for transfers between devices, per_device(): lax.all_to_all(pieces, 'comp', split_axis=1, concat_axis=0, tiled=True)  18.5 us
    ppermute x4, waiting for transfers between devices, extended_2(): before = lax.ppermute(last, axis, up)  17.5 us
    ppermute x4, starting transfers between devices, extended_2(): before = lax.ppermute(last, axis, up)  9.31 us
    gather x2, local copies, waits for them, and re-layouts, settle(): minus_energy = jnp.take(energy, minus_bins, axis=0)  9.11 us
  transfers between devices with their start and end apart: 9, of which 9 were waited for; matrix products, arithmetic and copies ran while one was open for 0% of the time, Pallas kernels for 0%

commit v1 on v0

v1 whole, which is shorter than its diff:
```python
import math

import jax
import jax.numpy as jnp
import numpy as np
from jax import lax
from jax.experimental import pallas as pl
from jax.experimental.pallas import tpu as pltpu
from jax.sharding import PartitionSpec as P

NDIR = 36
NFREQ = 36
SUB = 4

w_plus = 0.4096
w_minus = 3.1605
w_cross = 1.2945
time_step = 0.5

ROW_TILES = 4
STEP = 18


def courant_table():
    d = np.repeat(np.arange(NDIR), NFREQ)
    level = np.tile(np.arange(NFREQ), NDIR)
    angle = 2.0 * math.pi * d / NDIR
    size = 0.7 * 0.93**level
    cos = np.where(d % (NDIR // 2) == NDIR // 4, 0.0, np.cos(angle))
    sin = np.where(d % (NDIR // 2) == 0, 0.0, np.sin(angle))
    along_x, along_y = np.abs(size * cos), np.abs(size * sin)
    return np.stack([1.0 - along_x - along_y, along_x, along_y]).astype(np.float32)


def upwind_pairs(groups, tiles):
    pairs = []
    for c in range(groups):
        east = c * 4 // groups in (0, 3)
        for t in range(tiles):
            to = t + 1 if east else t - 1
            if 0 <= to < tiles:
                pairs.append((c * tiles + t, c * tiles + to))
    return pairs


def propagate_kernel(quarter_ref, coef_ref, own_ref, halo_ref, own_mask_ref, halo_mask_ref, out_ref):
    first = pl.program_id(0) * STEP
    quarter = quarter_ref[0]
    lane = lax.broadcasted_iota(jnp.int32, (8, 128), 1)

    def run(east, north):
        def rows(own, halo):
            both = [halo, own] if east else [own, halo]
            whole = jnp.concatenate(both, axis=0)
            return [whole[:, 128 * i : 128 * (i + 1)] for i in range(ROW_TILES)]

        mask = rows(own_mask_ref[...], halo_mask_ref[...])
        edge = lane == (0 if north else 127)
        base = 4 if east else 0

        def component(k, carry):
            stay, side, row = (coef_ref[i, first + k] for i in range(3))
            field = rows(own_ref[k], halo_ref[k])
            for _ in range(SUB):
                turned = [pltpu.roll(v, 1 if north else 127, 1) for v in field]
                fresh = []
                for i, v in enumerate(field):
                    j = i - 1 if north else i + 1
                    over = turned[j] if 0 <= j < ROW_TILES else 0.0
                    upwind_row = jnp.where(edge, over, turned[i])
                    upwind_col = pltpu.roll(v, 1 if east else 7, 0)
                    fresh.append(mask[i] * (stay * v + side * upwind_col + row * upwind_row))
                field = fresh
            for i, v in enumerate(field):
                for pair in range(2):
                    at = base + 2 * pair
                    out_ref[pair * ROW_TILES + i, k] = v[at : at + 2, :]
            return carry

        lax.fori_loop(0, STEP, component, 0, unroll=3)

    for value, (east, north) in enumerate(((True, True), (False, True), (False, False), (True, False))):
        pl.when(quarter == value)(lambda east=east, north=north: run(east, north))


def settle_kernel(bins_ref, coupling_ref, growth_ref, energy_ref, out_ref, a_ref, b_ref, c_ref, d_ref):
    count = energy_ref.shape[0]
    parts = (a_ref, b_ref, c_ref, d_ref)

    def clear(k, carry):
        for ref in parts:
            ref[k] = jnp.zeros(ref.shape[1:], ref.dtype)
        return carry

    lax.fori_loop(0, count, clear, 0, unroll=16)

    def one(k, carry):
        energy = energy_ref[k]
        scaled = (coupling_ref[k] * time_step) * energy
        total = (1.0 + time_step * growth_ref[k]) * energy
        for mirror in range(2):
            p, q = bins_ref[2 * mirror, k], bins_ref[2 * mirror + 1, k]
            plus, minus = energy_ref[p], energy_ref[q]
            delta = scaled * (energy * (w_plus * plus + w_minus * minus) - (2.0 * w_cross) * plus * minus)
            total = total - 2.0 * delta
            parts[2 * mirror][p] = parts[2 * mirror][p] + delta
            parts[2 * mirror + 1][q] = parts[2 * mirror + 1][q] + delta
        out_ref[k] = total
        return carry

    lax.fori_loop(0, count, one, 0, unroll=8)

    def gather(k, carry):
        out_ref[k] = out_ref[k] + ((a_ref[k] + b_ref[k]) + (c_ref[k] + d_ref[k]))
        return carry

    lax.fori_loop(0, count, gather, 0, unroll=16)


def unpack_kernel(in_ref, out_ref):
    def component(k, carry):
        for i in range(ROW_TILES):
            both = [in_ref[pair * ROW_TILES + i, k] for pair in range(2)]
            out_ref[k, :, 128 * i : 128 * (i + 1)] = jnp.concatenate(both, axis=0)
        return carry

    lax.fori_loop(0, STEP, component, 0, unroll=3)


def per_device(spectrum, sea_mask, quad_bins, coupling, growth):
    comp_dev, width, height = spectrum.shape
    groups, tiles = lax.axis_size("comp"), lax.axis_size("tile")
    mine = lax.axis_index("comp")
    count = comp_dev * groups
    pairs = upwind_pairs(groups, tiles)
    halo_mask = lax.ppermute(sea_mask, ("comp", "tile"), pairs).astype(jnp.float32)
    halo = lax.ppermute(spectrum, ("comp", "tile"), pairs)
    mask = sea_mask.astype(jnp.float32)
    table = lax.dynamic_slice(jnp.asarray(courant_table()), (0, mine * comp_dev), (3, comp_dev))
    quarter = (mine * 4 // groups).reshape(1).astype(jnp.int32)

    smem = pl.BlockSpec(memory_space=pltpu.SMEM)
    whole = pl.BlockSpec((width, height), lambda i: (0, 0))
    wide = pl.BlockSpec((STEP, width, height), lambda i: (i, 0, 0))
    packed = pl.BlockSpec((groups, STEP, 2, 128), lambda i: (0, i, 0, 0))
    pieces = pl.pallas_call(
        propagate_kernel,
        grid=(comp_dev // STEP,),
        in_specs=[smem, smem, wide, wide, whole, whole],
        out_specs=packed,
        out_shape=jax.ShapeDtypeStruct((groups, comp_dev, 2, 128), jnp.float32),
        name="propagate",
    )(quarter, table, spectrum, halo, mask, halo_mask)

    energy = lax.all_to_all(pieces, "comp", split_axis=0, concat_axis=0, tiled=True).reshape(count, 2, 128)
    vmem = pl.BlockSpec(memory_space=pltpu.VMEM)
    fresh = pl.pallas_call(
        settle_kernel,
        in_specs=[smem, smem, smem, vmem],
        out_specs=vmem,
        out_shape=jax.ShapeDtypeStruct((count, 2, 128), jnp.float32),
        scratch_shapes=[pltpu.VMEM((count, 2, 128), jnp.float32)] * 4,
        compiler_params=pltpu.CompilerParams(vmem_limit_bytes=40 << 20),
        name="settle",
    )(quad_bins, coupling, growth, energy)

    back = lax.all_to_all(
        fresh.reshape(groups, comp_dev, 2, 128), "comp", split_axis=0, concat_axis=0, tiled=True
    )
    return pl.pallas_call(
        unpack_kernel,
        grid=(comp_dev // STEP,),
        in_specs=[packed],
        out_specs=wide,
        out_shape=jax.ShapeDtypeStruct((comp_dev, width, height), jnp.float32),
        name="unpack",
    )(back)


def solution(mesh):
    return jax.shard_map(
        per_device,
        mesh=mesh,
        in_specs=(P("comp", "tile", None), P("tile", None), P(), P(), P()),
        out_specs=P("comp", "tile", None),
        check_vma=False,
    )
```

time: 200 us -> 131 us (0.66)
  other arithmetic: 59.3 us -> 1.88 us
  Pallas kernels: 0 us -> 41.6 us
  starting transfers between devices: 46.4 us -> 7.08 us
  local copies, waits for them, and re-layouts: 31.2 us -> 2.44 us
  blocking collectives: 21.9 us -> 46.7 us
  waiting for transfers between devices: 39.8 us -> 30.9 us
    pallas_call x0 -> x3, Pallas kernels: none -> 41.6 us  [the longest x1 18.5 us: per_device(): pl.pallas_call(propagate_kernel, grid=(comp_dev // STEP,), in_specs=[smem...]
    scatter-add x4 -> x0, other arithmetic: 38.6 us -> none  [the longest x2 19.4 us: settle(): total = total + jax.ops.segment_sum(delta, plus_bins, num_segments=count)]
    ppermute x8 -> x2, starting transfers between devices: 37.7 us -> 7.08 us  [the longest x1 3.55 us: per_device(): lax.ppermute(sea_mask, ('comp', 'tile'), pairs).astype(jnp.float32)]
    all_to_all x1 -> x2, blocking collectives: 21.9 us -> 46.7 us  [the longest x1 24.5 us: per_device(): lax.all_to_all(pieces, 'comp', split_axis=0, concat_axis=0, tiled=True)]
    all_to_all x1 -> x0, waiting for transfers between devices: 18.5 us -> none  [per_device(): lax.all_to_all(pieces, 'comp', split_axis=1, concat_axis=0, tiled=True)]
    gather x4 -> x0, local copies, waits for them, and re-layouts: 18.2 us -> none  [the longest x2 9.11 us: settle(): minus_energy = jnp.take(energy, minus_bins, axis=0)]
    ppermute x8 -> x2, waiting for transfers between devices: 21.3 us -> 30.9 us  [the longest x1 30.8 us: per_device(): lax.ppermute(sea_mask, ('comp', 'tile'), pairs).astype(jnp.float32)]
    all_to_all x1 -> x0, starting transfers between devices: 8.71 us -> none  [per_device(): lax.all_to_all(pieces, 'comp', split_axis=1, concat_axis=0, tiled=True)]
  transfers between devices with their start and end apart: 9 -> 2, of which waited for: 9 -> 1; matrix products, arithmetic and copies ran while one was open for 0% -> 2% of each run, Pallas kernels for 0% -> 0%
where the time goes in v1:
time: 131 us
  blocking collectives  46.7 us (36%)
  Pallas kernels  41.6 us (32%)
  waiting for transfers between devices  30.9 us (24%)
  starting transfers between devices  7.08 us (5%)
  local copies, waits for them, and re-layouts  2.44 us (2%)
  other arithmetic  1.88 us (1%)
    ppermute x1, waiting for transfers between devices, per_device(): lax.ppermute(sea_mask, ('comp', 'tile'), pairs).astype(jnp.float32)  30.8 us
    all_to_all x1, blocking collectives, per_device(): lax.all_to_all(pieces, 'comp', split_axis=0, concat_axis=0, tiled=True)  24.5 us
    all_to_all x1, blocking collectives, per_device(): lax.all_to_all(fresh.reshape(groups, comp_dev, 2, 128), 'comp', split_axi...  22.3 us
    pallas_call x1, Pallas kernels, per_device(): pl.pallas_call(propagate_kernel, grid=(comp_dev // STEP,), in_specs=[smem...  18.5 us
    pallas_call x1, Pallas kernels, per_device(): pl.pallas_call(settle_kernel, in_specs=[smem, smem, smem, vmem], out_spec...  17 us
    pallas_call x1, Pallas kernels, per_device(): pl.pallas_call(unpack_kernel, grid=(comp_dev // STEP,), in_specs=[packed]...  6.04 us
    ppermute x1, starting transfers between devices, per_device(): lax.ppermute(sea_mask, ('comp', 'tile'), pairs).astype(jnp.float32)  3.55 us
    ppermute x1, starting transfers between devices, per_device(): halo = lax.ppermute(spectrum, ('comp', 'tile'), pairs)  3.54 us
  transfers between devices with their start and end apart: 2, of which 1 were waited for; matrix products, arithmetic and copies ran while one was open for 2% of the time, Pallas kernels for 0%

profile of v1, /device:TPU:7, one launch (start us, length us, event | category | flops | bytes accessed | tf_op | source)
XLA Modules:
  0.0 130.6 jit_solution(12626193463989963720)
XLA Ops:
  0.0 3.5 %collective-permute-start = (f32[162,4,512]{2,1,0:T(4,128)}, f32[162,4,512]{2,1,0:T(4,128)S(1)}, u32[]{:S(2)}, u32[]{:S(2)}) collective-permute-start(f32[162,4,512]{2,1,0:T(4,128)} %own_ref.1), channel_id=1, source_target_pairs={{0,1},{1,2},{2,3},{3,4},{4,5},{5,6},{6,7},{7,8},{8,9},{9,10},{10,1... | collective-permute-start | bytes 3981320 | tf_op jit(solution)/shard_map/ppermute | solution.py:137
  3.5 3.5 %collective-permute-start.1 = (s32[4,512]{1,0:T(4,128)}, s32[4,512]{1,0:T(4,128)S(1)}, u32[]{:S(2)}, u32[]{:S(2)}) collective-permute-start(s32[4,512]{1,0:T(4,128)} %param.7), channel_id=1, source_target_pairs={{0,1},{1,2},{2,3},{3,4},{4,5},{5,6},{6,7},{7,8},{8,9},{9,10},{10,1... | collective-permute-start | bytes 24584 | tf_op jit(solution)/shard_map/ppermute | solution.py:136
  7.1 1.4 %constant_dynamic-slice_fusion.coef_ref = f32[3,162]{1,0:T(4,128)} fusion(f32[3,1296]{1,0:T(4,128)} %constant.31.clone, s32[]{:T(128)S(6)} %select_n.9), kind=kLoop, calls=%fused_computation | loop fusion | bytes 3892 | tf_op jit(solution)/shard_map/dynamic_slice | solution.py:139
  8.5 1.3 convert_element_type.6.own_mask_ref
  9.8 30.8 %collective-permute-done.1 = s32[4,512]{1,0:T(4,128)S(1)} collective-permute-done((s32[4,512]{1,0:T(4,128)}, s32[4,512]{1,0:T(4,128)S(1)}, u32[]{:S(2)}, u32[]{:S(2)}) %collective-permute-start.1) | collective-permute-done | bytes 8224 | tf_op jit(solution)/shard_map/ppermute | solution.py:136
  40.6 0.6 convert_element_type.7.halo_mask_ref
  41.2 0.0 collective-permute-done.halo_ref
  41.2 0.0 copy-start.3
  41.2 1.1 copy-done.3
  42.3 18.5 %propagate.1 = f32[8,162,2,128]{3,2,1,0:T(2,128)} custom-call(s32[1]{0:T(128)} %bitcast.quarter_ref, f32[3,162]{1,0:T(4,128)} %constant_dynamic-slice_fusion.coef_ref, f32[162,4,512]{2,1,0:T(4,128)} %own_ref.1, f32[162,4,512]{2,1,0:T(4,128)} %copy-done.3, f32[4,512]{1,0:T(4,128)} %convert_element_type.6.own_mask_ref, f32[4,512]{1,0:T(4,128)} %convert_element_type.7.halo_mask_ref), custom_call_target="tpu_custom_call" | custom-call | tf_op jit(solution)/shard_map/propagate/pallas_call | solution.py:146
  60.8 0.0 copy-start
  60.8 0.0 copy-start.1
  60.8 0.0 copy-start.2
  60.8 24.5 %all_to_all.10 = f32[8,162,2,128]{3,2,1,0:T(2,128)S(1)} all-to-all(f32[8,162,2,128]{3,2,1,0:T(2,128)} %propagate.1), channel_id=1, replica_groups=mesh['comp'=8,'tile'=64] {'comp'}, dimensions={0} | all-to-all | bytes 2654208 | tf_op jit(solution)/shard_map/all_to_all | solution.py:155
  85.3 0.0 copy-done
  85.3 0.0 copy-done.1
  85.3 0.0 copy-done.2
  85.3 17.0 %settle.1 = f32[1296,2,128]{2,1,0:T(2,128)S(1)} custom-call(s32[4,1296]{1,0:T(4,128)S(1)} %copy-done, f32[1296]{0:T(1024)S(1)} %copy-done.1, f32[1296]{0:T(1024)S(1)} %copy-done.2, f32[1296,2,128]{2,1,0:T(2,128)S(1)} %bitcast.3), custom_call_target="tpu_custom_call" | custom-call | tf_op jit(solution)/shard_map/settle/pallas_call | solution.py:157
  102.3 22.3 %all_to_all.11.in_ref = f32[8,162,2,128]{3,2,1,0:T(2,128)} all-to-all(f32[8,162,2,128]{3,2,1,0:T(2,128)S(1)} %bitcast.4), channel_id=1, replica_groups=mesh['comp'=8,'tile'=64] {'comp'}, dimensions={0} | all-to-all | bytes 2654208 | tf_op jit(solution)/shard_map/all_to_all | solution.py:167
  124.6 6.0 %unpack.1 = f32[162,4,512]{2,1,0:T(4,128)} custom-call(f32[8,162,2,128]{3,2,1,0:T(2,128)} %all_to_all.11.in_ref), custom_call_target="tpu_custom_call" | custom-call | tf_op jit(solution)/shard_map/unpack/pallas_call | solution.py:170
Async XLA Ops:
  0.0 41.2 %collective-permute-start = (f32[162,4,512]{2,1,0:T(4,128)}, f32[162,4,512]{2,1,0:T(4,128)S(1)}, u32[]{:S(2)}, u32[]{:S(2)}) collective-permute-start(f32[162,4,512]{2,1,0:T(4,128)} %own_ref.1), channel_id=1, source_target_pairs={{0,1},{1,2},{2,3},{3,4},{4,5},{5,6},{6,7},{7,8},{8,9},{9,10},{10,1... | collective-permute-start | bytes 3981320 | tf_op jit(solution)/shard_map/ppermute | solution.py:137
  3.5 37.1 %collective-permute-start.1 = (s32[4,512]{1,0:T(4,128)}, s32[4,512]{1,0:T(4,128)S(1)}, u32[]{:S(2)}, u32[]{:S(2)}) collective-permute-start(s32[4,512]{1,0:T(4,128)} %param.7), channel_id=1, source_target_pairs={{0,1},{1,2},{2,3},{3,4},{4,5},{5,6},{6,7},{7,8},{8,9},{9,10},{10,1... | collective-permute-start | bytes 24584 | tf_op jit(solution)/shard_map/ppermute | solution.py:136
  41.2 1.1 copy-start.3
  60.8 24.5 %copy-start = (s32[4,1296]{1,0:T(4,128)S(1)}, s32[4,1296]{1,0:T(4,128)}, u32[]{:S(2)}) copy-start(s32[4,1296]{1,0:T(4,128)} %bins_ref.1) | copy-start | bytes 62212
  60.8 24.5 %copy-start.1 = (f32[1296]{0:T(1024)S(1)}, f32[1296]{0:T(1024)}, u32[]{:S(2)}) copy-start(f32[1296]{0:T(1024)} %coupling_ref.1) | copy-start | bytes 15556
  60.8 24.5 %copy-start.2 = (f32[1296]{0:T(1024)S(1)}, f32[1296]{0:T(1024)}, u32[]{:S(2)}) copy-start(f32[1296]{0:T(1024)} %growth_ref.1) | copy-start | bytes 15556

commit v2 on v1

v2 whole, which is shorter than its diff:
```python
import functools
import math

import jax
import jax.numpy as jnp
import numpy as np
from jax import lax
from jax.experimental import pallas as pl
from jax.experimental.pallas import tpu as pltpu
from jax.sharding import PartitionSpec as P

NDIR = 36
NFREQ = 36
SUB = 4

w_plus = 0.4096
w_minus = 3.1605
w_cross = 1.2945
time_step = 0.5

ROW_TILES = 4
CHUNKS = (84, 78)
TOGETHER = 28
VMEM_LIMIT = 40 << 20


def courant_table():
    d = np.repeat(np.arange(NDIR), NFREQ)
    level = np.tile(np.arange(NFREQ), NDIR)
    angle = 2.0 * math.pi * d / NDIR
    size = 0.7 * 0.93**level
    cos = np.where(d % (NDIR // 2) == NDIR // 4, 0.0, np.cos(angle))
    sin = np.where(d % (NDIR // 2) == 0, 0.0, np.sin(angle))
    along_x, along_y = np.abs(size * cos), np.abs(size * sin)
    return np.stack([1.0 - along_x - along_y, along_x, along_y], axis=1).astype(np.float32)


def upwind_pairs(groups, tiles):
    pairs = []
    for c in range(groups):
        east = c * 4 // groups in (0, 3)
        for t in range(tiles):
            to = t + 1 if east else t - 1
            if 0 <= to < tiles:
                pairs.append((c * tiles + t, c * tiles + to))
    return pairs


def rows_of(size):
    return -(-2 * size // 8) * 8


def pair_of(row):
    return pl.ds(pl.multiple_of(row, 2), 2)


def propagate_kernel(first, quarter_ref, coef_ref, own_ref, halo_ref, own_mask_ref, halo_mask_ref, out_ref):
    size = own_ref.shape[0]
    side_by_side = max(n for n in range(1, TOGETHER + 1) if size % n == 0)
    quarter = quarter_ref[0]
    lane = lax.broadcasted_iota(jnp.int32, (8, 128), 1)
    extra = out_ref.shape[1] - 2 * size
    if extra:
        for piece in range(out_ref.shape[0]):
            out_ref[piece, 2 * size :, :] = jnp.zeros((extra, 128), jnp.float32)

    def run(east, north):
        def rows(own, halo):
            whole = jnp.concatenate([halo, own] if east else [own, halo], axis=0)
            return [whole[:, 128 * i : 128 * (i + 1)] for i in range(ROW_TILES)]

        mask = rows(own_mask_ref[...].astype(jnp.float32), halo_mask_ref[...].astype(jnp.float32))
        edge = lane == (0 if north else 127)
        base = 4 if east else 0

        def several(step, carry):
            which = [step * side_by_side + u for u in range(side_by_side)]
            coefs = [[coef_ref[3 * (first + k) + i] for i in range(3)] for k in which]
            fields = [rows(own_ref[k], halo_ref[k]) for k in which]
            for _ in range(SUB):
                turned = [[pltpu.roll(v, 1 if north else 127, 1) for v in field] for field in fields]
                cols = [[pltpu.roll(v, 1 if east else 7, 0) for v in field] for field in fields]
                fresh = []
                for u, (stay, side, along) in enumerate(coefs):
                    field = []
                    for i in range(ROW_TILES):
                        j = i - 1 if north else i + 1
                        over = turned[u][j] if 0 <= j < ROW_TILES else 0.0
                        upwind_row = jnp.where(edge, over, turned[u][i])
                        field.append(mask[i] * (stay * fields[u][i] + side * cols[u][i] + along * upwind_row))
                    fresh.append(field)
                fields = fresh
            for u, k in enumerate(which):
                for i, v in enumerate(fields[u]):
                    for pair in range(2):
                        at = base + 2 * pair
                        out_ref[pair * ROW_TILES + i, pair_of(2 * k), :] = v[at : at + 2, :]
            return carry

        lax.fori_loop(0, size // side_by_side, several, 0)

    for value, (east, north) in enumerate(((True, True), (False, True), (False, False), (True, False))):
        pl.when(quarter == value)(functools.partial(run, east, north))


def settle_kernel(bins_ref, coupling_ref, growth_ref, *refs):
    pieces, (out_ref, energy_ref, a_ref, b_ref, c_ref, d_ref, sems) = refs[: len(CHUNKS)], refs[len(CHUNKS) :]
    parts = (a_ref, b_ref, c_ref, d_ref)
    total_rows = energy_ref.shape[0]
    groups = pieces[0].shape[0]
    copies = []
    start = 0
    for piece in pieces:
        rows = piece.shape[1]
        for g in range(groups):
            place = energy_ref.at[pl.ds(g * (total_rows // groups) + start, rows), :]
            copies.append(pltpu.make_async_copy(piece.at[g], place, sems.at[len(copies)]))
        start += rows
    for copy in copies:
        copy.start()

    def tile_of(t):
        return pl.ds(pl.multiple_of(8 * t, 8), 8)

    def clear(t, carry):
        for ref in parts:
            ref[tile_of(t), :] = jnp.zeros((8, 128), jnp.float32)
        return carry

    lax.fori_loop(0, total_rows // 8, clear, 0, unroll=4)
    for copy in copies:
        copy.wait()

    def one(k, carry):
        rows = [pair_of(bins_ref[4 * k + j]) for j in range(4)]
        here = pair_of(2 * k)
        energy = energy_ref[here, :]
        scaled = coupling_ref[k] * energy
        total = growth_ref[k] * energy
        for mirror in range(2):
            p, q = rows[2 * mirror], rows[2 * mirror + 1]
            plus, minus = energy_ref[p, :], energy_ref[q, :]
            delta = scaled * (energy * (w_plus * plus + w_minus * minus) - (2.0 * w_cross) * plus * minus)
            total = total - 2.0 * delta
            for ref, row in ((parts[2 * mirror], p), (parts[2 * mirror + 1], q)):
                ref[row, :] = ref[row, :] + delta
        out_ref[here, :] = total
        return carry

    lax.fori_loop(0, total_rows // 2, one, 0, unroll=16)

    def gather(t, carry):
        s = tile_of(t)
        out_ref[s, :] = out_ref[s, :] + ((a_ref[s, :] + b_ref[s, :]) + (c_ref[s, :] + d_ref[s, :]))
        return carry

    lax.fori_loop(0, total_rows // 8, gather, 0, unroll=4)


def unpack_kernel(in_ref, out_ref):
    step_size = 9

    def several(step, carry):
        which = [step * step_size + u for u in range(step_size)]
        both = [
            [[in_ref[pair * ROW_TILES + i, pair_of(2 * k), :] for pair in range(2)] for i in range(ROW_TILES)]
            for k in which
        ]
        for u, k in enumerate(which):
            for i in range(ROW_TILES):
                out_ref[k, :, 128 * i : 128 * (i + 1)] = jnp.concatenate(both[u][i], axis=0)
        return carry

    lax.fori_loop(0, out_ref.shape[0] // step_size, several, 0)


def per_device(spectrum, sea_mask, quad_bins, coupling, growth):
    comp_dev, width, height = spectrum.shape
    groups, tiles = lax.axis_size("comp"), lax.axis_size("tile")
    mine = lax.axis_index("comp")
    count = comp_dev * groups
    group_rows = sum(rows_of(size) for size in CHUNKS)
    pairs = upwind_pairs(groups, tiles)
    table = lax.dynamic_slice(jnp.asarray(courant_table().reshape(-1)), (3 * mine * comp_dev,), (3 * comp_dev,))
    quarter = (mine * 4 // groups).reshape(1).astype(jnp.int32)

    smem = pl.BlockSpec(memory_space=pltpu.SMEM)
    vmem = pl.BlockSpec(memory_space=pltpu.VMEM)
    params = pltpu.CompilerParams(vmem_limit_bytes=VMEM_LIMIT)

    starts = [sum(CHUNKS[:i]) for i in range(len(CHUNKS))]
    owns = [lax.slice_in_dim(spectrum, s, s + n, axis=0) for s, n in zip(starts, CHUNKS)]
    halos = [lax.ppermute(owns[0], ("comp", "tile"), pairs)]
    halo_mask = lax.ppermute(sea_mask, ("comp", "tile"), pairs)
    halos += [lax.ppermute(own, ("comp", "tile"), pairs) for own in owns[1:]]

    spare = group_rows // 2 - comp_dev
    own_rows = np.arange(groups)[:, None] * group_rows + 2 * (comp_dev + np.arange(spare))[None]
    where = 2 * quad_bins.T + (group_rows - 2 * comp_dev) * (quad_bins.T // comp_dev)
    fill = jnp.asarray(np.repeat(own_rows[:, :, None], 4, axis=2).astype(np.int32))
    where = jnp.concatenate([where.reshape(groups, comp_dev, 4), fill], axis=1).reshape(-1)
    pad = lambda v: jnp.pad(v.reshape(groups, comp_dev), ((0, 0), (0, spare))).reshape(-1)
    strength, kept = pad(time_step * coupling), pad(1.0 + time_step * growth)

    pieces = []
    for i, (start, size) in enumerate(zip(starts, CHUNKS)):
        moved = pl.pallas_call(
            functools.partial(propagate_kernel, start),
            in_specs=[smem, smem, vmem, vmem, vmem, vmem],
            out_specs=vmem,
            out_shape=jax.ShapeDtypeStruct((groups, rows_of(size), 128), jnp.float32),
            compiler_params=params,
            cost_estimate=pl.CostEstimate(flops=100 * size * 2048, bytes_accessed=12 * size * 2048, transcendentals=0),
            name=f"propagate_{i}",
        )(quarter, table, owns[i], halos[i], sea_mask, halo_mask)
        pieces.append(lax.all_to_all(moved, "comp", split_axis=0, concat_axis=0, tiled=True))

    total_rows = groups * group_rows
    fresh = pl.pallas_call(
        settle_kernel,
        in_specs=[smem, smem, smem] + [pl.BlockSpec(memory_space=pl.ANY)] * len(CHUNKS),
        out_specs=vmem,
        out_shape=jax.ShapeDtypeStruct((total_rows, 128), jnp.float32),
        scratch_shapes=[pltpu.VMEM((total_rows, 128), jnp.float32)] * 5
        + [pltpu.SemaphoreType.DMA((len(CHUNKS) * groups,))],
        compiler_params=params,
        name="settle",
    )(where, strength, kept, *pieces)

    back = lax.all_to_all(fresh.reshape(groups, group_rows, 128), "comp", split_axis=0, concat_axis=0, tiled=True)
    return pl.pallas_call(
        unpack_kernel,
        in_specs=[vmem],
        out_specs=vmem,
        out_shape=jax.ShapeDtypeStruct((comp_dev, width, height), jnp.float32),
        compiler_params=params,
        name="unpack",
    )(back)


def solution(mesh):
    return jax.shard_map(
        per_device,
        mesh=mesh,
        in_specs=(P("comp", "tile", None), P("tile", None), P(), P(), P()),
        out_specs=P("comp", "tile", None),
        check_vma=False,
    )
```

time: 131 us -> 114 us (0.87)
  blocking collectives: 46.7 us -> 22 us
  Pallas kernels: 41.6 us -> 20.7 us
  waiting for transfers between devices: 30.9 us -> 45.5 us
  starting transfers between devices: 7.08 us -> 20.5 us
  other arithmetic: 1.88 us -> 0.12 us
  local copies, waits for them, and re-layouts: 2.44 us -> 4.1 us
    all_to_all x2 -> x1, blocking collectives: 46.7 us -> 22 us  [per_device(): lax.all_to_all(fresh.reshape(groups, group_rows, 128), 'comp', split_axis...]
    pallas_call x3 -> x4, Pallas kernels: 41.6 us -> 20.7 us  [the longest x1 12.9 us: per_device(): pl.pallas_call(settle_kernel, in_specs=[smem, smem, smem] + [pl.BlockSpec...]
    all_to_all x0 -> x2, waiting for transfers between devices: none -> 17.7 us  [per_device(): lax.all_to_all(moved, 'comp', split_axis=0, concat_axis=0, tiled=True)]
    all_to_all x0 -> x2, starting transfers between devices: none -> 9.84 us  [per_device(): lax.all_to_all(moved, 'comp', split_axis=0, concat_axis=0, tiled=True)]
    ppermute x2 -> x3, starting transfers between devices: 7.08 us -> 10.6 us  [the longest x1 3.55 us: per_device(): halos += [lax.ppermute(own, ('comp', 'tile'), pairs) for own in owns[1:]]]
    ppermute x2 -> x3, waiting for transfers between devices: 30.9 us -> 27.8 us  [the longest x1 27.8 us: per_device(): halo_mask = lax.ppermute(sea_mask, ('comp', 'tile'), pairs)]
    slice x0 -> x2, local copies, waits for them, and re-layouts: none -> 2.28 us  [per_device(): lax.slice_in_dim(spectrum, s, s + n, axis=0)]
    convert_element_type x2 -> x0, other arithmetic: 1.88 us -> none  [the longest x1 1.29 us: per_device(): mask = sea_mask.astype(jnp.float32)]
  transfers between devices with their start and end apart: 2 -> 5, of which waited for: 1 -> 3; matrix products, arithmetic and copies ran while one was open for 2% -> 3% of each run, Pallas kernels for 0% -> 6%
where the time goes in v2:
time: 114 us; the launch traced here: 113 us
  waiting for transfers between devices  45.5 us (40%)
  blocking collectives  22 us (19%)
  Pallas kernels  20.7 us (18%)
  starting transfers between devices  20.5 us (18%)
  local copies, waits for them, and re-layouts  4.1 us (4%)
    ppermute x1, waiting for transfers between devices, per_device(): halo_mask = lax.ppermute(sea_mask, ('comp', 'tile'), pairs)  27.8 us
    all_to_all x1, blocking collectives, per_device(): lax.all_to_all(fresh.reshape(groups, group_rows, 128), 'comp', split_axis...  22 us
    all_to_all x2, waiting for transfers between devices, per_device(): lax.all_to_all(moved, 'comp', split_axis=0, concat_axis=0, tiled=True)  17.7 us
    pallas_call x1, Pallas kernels, per_device(): pl.pallas_call(settle_kernel, in_specs=[smem, smem, smem] + [pl.BlockSpec...  12.9 us
    all_to_all x2, starting transfers between devices, per_device(): lax.all_to_all(moved, 'comp', split_axis=0, concat_axis=0, tiled=True)  9.84 us
    pallas_call x2, Pallas kernels, per_device(): pl.pallas_call(functools.partial(propagate_kernel, start), in_specs=[smem...  6.25 us
    ppermute x1, starting transfers between devices, per_device(): halos += [lax.ppermute(own, ('comp', 'tile'), pairs) for own in owns[1:]]  3.55 us
    ppermute x1, starting transfers between devices, per_device(): halos = [lax.ppermute(owns[0], ('comp', 'tile'), pairs)]  3.55 us
  transfers between devices with their start and end apart: 5, of which 3 were waited for; matrix products, arithmetic and copies ran while one was open for 3% of the time, Pallas kernels for 6%

profile of v2, /device:TPU:7, one launch (start us, length us, event | category | flops | bytes accessed | tf_op | source)
XLA Modules:
  0.0 113.1 jit_solution(966649430470568153)
XLA Ops:
  0.0 0.0 copy-start
  0.0 1.1 %slice.7.own_ref = f32[78,4,512]{2,1,0:T(4,128)S(1)} slice(f32[162,4,512]{2,1,0:T(4,128)} %param.7), slice={[84:162], [0:4], [0:512]} | slice | bytes 1277952 | tf_op jit(solution)/shard_map/slice | solution.py:192
  1.1 3.5 %collective-permute-start.2 = (f32[78,4,512]{2,1,0:T(4,128)S(1)}, f32[78,4,512]{2,1,0:T(4,128)S(1)}, u32[]{:S(2)}, u32[]{:S(2)}) collective-permute-start(f32[78,4,512]{2,1,0:T(4,128)S(1)} %slice.7.own_ref), channel_id=1, source_target_pairs={{0,1},{1,2},{2,3},{3,4},{4,5},{5,6},{6,7},{7,8},{8,9},{9,10},{10,1... | collective-permute-start | bytes 1916936 | tf_op jit(solution)/shard_map/ppermute | solution.py:195
  4.7 1.1 %slice.6.own_ref = f32[84,4,512]{2,1,0:T(4,128)S(1)} slice(f32[162,4,512]{2,1,0:T(4,128)} %param.7), slice={[0:84], [0:4], [0:512]} | slice | bytes 1376256 | tf_op jit(solution)/shard_map/slice | solution.py:192
  5.8 3.5 %collective-permute-start = (f32[84,4,512]{2,1,0:T(4,128)S(1)}, f32[84,4,512]{2,1,0:T(4,128)S(1)}, u32[]{:S(2)}, u32[]{:S(2)}) collective-permute-start(f32[84,4,512]{2,1,0:T(4,128)S(1)} %slice.6.own_ref), channel_id=1, source_target_pairs={{0,1},{1,2},{2,3},{3,4},{4,5},{5,6},{6,7},{7,8},{8,9},{9,10},{10,1... | collective-permute-start | bytes 2064392 | tf_op jit(solution)/shard_map/ppermute | solution.py:193
  9.4 0.0 copy-done
  9.4 3.5 %collective-permute-start.1 = (s32[4,512]{1,0:T(4,128)S(1)}, s32[4,512]{1,0:T(4,128)S(1)}, u32[]{:S(2)}, u32[]{:S(2)}) collective-permute-start(s32[4,512]{1,0:T(4,128)S(1)} %copy-done), channel_id=1, source_target_pairs={{0,1},{1,2},{2,3},{3,4},{4,5},{5,6},{6,7},{7,8},{8,9},{9,10},{10,1... | collective-permute-start | bytes 24584 | tf_op jit(solution)/shard_map/ppermute | solution.py:194
  13.0 0.8 dynamic_slice.3.coef_ref
  13.8 27.8 %collective-permute-done.1.halo_mask_ref = s32[4,512]{1,0:T(4,128)S(1)} collective-permute-done((s32[4,512]{1,0:T(4,128)S(1)}, s32[4,512]{1,0:T(4,128)S(1)}, u32[]{:S(2)}, u32[]{:S(2)}) %collective-permute-start.1) | collective-permute-done | bytes 8224 | tf_op jit(solution)/shard_map/ppermute | solution.py:194
  41.6 0.0 collective-permute-done.2.halo_ref
  41.6 3.1 %propagate_1.1 = f32[8,160,128]{2,1,0:T(8,128)} custom-call(s32[1]{0:T(128)} %bitcast.3.quarter_ref, f32[486]{0:T(512)S(1)} %dynamic_slice.3.coef_ref, f32[78,4,512]{2,1,0:T(4,128)S(1)} %slice.7.own_ref, f32[78,4,512]{2,1,0:T(4,128)S(1)} %collective-permute-done.2.halo_ref, s32[4,512]{1,0:T(4,128)S(1)} %copy-done, ...), custom_call_target="tpu_custom_call" | custom-call | flops 15974400 | bytes 1916928 | tf_op jit(solution)/shard_map/propagate_1/pallas_call | solution.py:207
  44.6 5.5 %all-to-all-start.1 = ((f32[8,160,128]{2,1,0:T(8,128)}), f32[8,160,128]{2,1,0:T(8,128)S(1)}, u32[]{:S(2)}, u32[]{:S(2)}) async-start(f32[8,160,128]{2,1,0:T(8,128)} %propagate_1.1), calls=%async_computation.1 | async-start | bytes 1310720 | tf_op jit(solution)/shard_map/all_to_all | solution.py:216
  50.1 0.0 copy-start.1
  50.1 0.0 copy-start.2
  50.1 0.0 collective-permute-done.halo_ref
  50.1 3.2 %propagate_0.1 = f32[8,168,128]{2,1,0:T(8,128)} custom-call(s32[1]{0:T(128)} %bitcast.3.quarter_ref, f32[486]{0:T(512)S(1)} %dynamic_slice.3.coef_ref, f32[84,4,512]{2,1,0:T(4,128)S(1)} %slice.6.own_ref, f32[84,4,512]{2,1,0:T(4,128)S(1)} %collective-permute-done.halo_ref, s32[4,512]{1,0:T(4,128)S(1)} %copy-done, ...), custom_call_target="tpu_custom_call" | custom-call | flops 17203200 | bytes 2064384 | tf_op jit(solution)/shard_map/propagate_0/pallas_call | solution.py:207
  53.3 0.0 copy-start.3
  53.3 0.0 copy-start.4
  53.3 7.7 %all-to-all-done.1.refs_1_ = f32[8,160,128]{2,1,0:T(8,128)S(1)} async-done(((f32[8,160,128]{2,1,0:T(8,128)}), f32[8,160,128]{2,1,0:T(8,128)S(1)}, u32[]{:S(2)}, u32[]{:S(2)}) %all-to-all-start.1) | async-done | bytes 655392 | tf_op jit(solution)/shard_map/all_to_all | solution.py:216
  61.0 4.3 %all-to-all-start = ((f32[8,168,128]{2,1,0:T(8,128)}), f32[8,168,128]{2,1,0:T(8,128)S(1)}, u32[]{:S(2)}, u32[]{:S(2)}) async-start(f32[8,168,128]{2,1,0:T(8,128)} %propagate_0.1), calls=%async_computation | async-start | bytes 1376256 | tf_op jit(solution)/shard_map/all_to_all | solution.py:216
  65.3 0.0 copy-done.1
  65.4 0.1 reshape.24
  65.5 0.0 copy-done.2
  65.5 0.1 pad_add_fusion
  65.6 0.3 copy.9
  65.9 0.3 reshape.25.bins_ref
  66.2 0.0 copy-done.3
  66.2 0.1 reshape.26
  66.3 0.1 reshape.27.coupling_ref
  66.4 0.0 copy-done.4
  66.4 0.1 reshape.28
  66.5 0.1 reshape.29.growth_ref
  66.6 10.0 %all-to-all-done.refs_0_ = f32[8,168,128]{2,1,0:T(8,128)S(1)} async-done(((f32[8,168,128]{2,1,0:T(8,128)}), f32[8,168,128]{2,1,0:T(8,128)S(1)}, u32[]{:S(2)}, u32[]{:S(2)}) %all-to-all-start) | async-done | bytes 688160 | tf_op jit(solution)/shard_map/all_to_all | solution.py:216
  76.6 12.9 %settle.1 = f32[2624,128]{1,0:T(8,128)S(1)} custom-call(s32[5248]{0:T(1024)S(1)} %reshape.25.bins_ref, f32[1312]{0:T(1024)S(1)} %reshape.27.coupling_ref, f32[1312]{0:T(1024)S(1)} %reshape.29.growth_ref, f32[8,168,128]{2,1,0:T(8,128)S(1)} %all-to-all-done.refs_0_, f32[8,160,128]{2,1,0:T(8,128)S(1)} %all-to-all-done.1.refs_1_), custom_call_target="tpu_custom_call" | custom-call | tf_op jit(solution)/shard_map/settle/pallas_call | solution.py:219
  89.5 22.0 %all_to_all.15.in_ref = f32[8,328,128]{2,1,0:T(8,128)S(1)} all-to-all(f32[8,328,128]{2,1,0:T(8,128)S(1)} %bitcast.10), channel_id=1, replica_groups=mesh['comp'=8,'tile'=64] {'comp'}, dimensions={0} | all-to-all | bytes 2686976 | tf_op jit(solution)/shard_map/all_to_all | solution.py:230
  111.5 1.6 %unpack.1 = f32[162,4,512]{2,1,0:T(4,128)} custom-call(f32[8,328,128]{2,1,0:T(8,128)S(1)} %all_to_all.15.in_ref), custom_call_target="tpu_custom_call" | custom-call | tf_op jit(solution)/shard_map/unpack/pallas_call | solution.py:231
  (5 shorter events, 0.1 us)
Async XLA Ops:
  0.0 9.4 %copy-start = (s32[4,512]{1,0:T(4,128)S(1)}, s32[4,512]{1,0:T(4,128)}, u32[]{:S(2)}) copy-start(s32[4,512]{1,0:T(4,128)} %own_mask_ref.3) | copy-start | bytes 24580
  1.1 40.4 %collective-permute-start.2 = (f32[78,4,512]{2,1,0:T(4,128)S(1)}, f32[78,4,512]{2,1,0:T(4,128)S(1)}, u32[]{:S(2)}, u32[]{:S(2)}) collective-permute-start(f32[78,4,512]{2,1,0:T(4,128)S(1)} %slice.7.own_ref), channel_id=1, source_target_pairs={{0,1},{1,2},{2,3},{3,4},{4,5},{5,6},{6,7},{7,8},{8,9},{9,10},{10,1... | collective-permute-start | bytes 1916936 | tf_op jit(solution)/shard_map/ppermute | solution.py:195
  5.8 44.3 %collective-permute-start = (f32[84,4,512]{2,1,0:T(4,128)S(1)}, f32[84,4,512]{2,1,0:T(4,128)S(1)}, u32[]{:S(2)}, u32[]{:S(2)}) collective-permute-start(f32[84,4,512]{2,1,0:T(4,128)S(1)} %slice.6.own_ref), channel_id=1, source_target_pairs={{0,1},{1,2},{2,3},{3,4},{4,5},{5,6},{6,7},{7,8},{8,9},{9,10},{10,1... | collective-permute-start | bytes 2064392 | tf_op jit(solution)/shard_map/ppermute | solution.py:193
  9.4 32.1 %collective-permute-start.1 = (s32[4,512]{1,0:T(4,128)S(1)}, s32[4,512]{1,0:T(4,128)S(1)}, u32[]{:S(2)}, u32[]{:S(2)}) collective-permute-start(s32[4,512]{1,0:T(4,128)S(1)} %copy-done), channel_id=1, source_target_pairs={{0,1},{1,2},{2,3},{3,4},{4,5},{5,6},{6,7},{7,8},{8,9},{9,10},{10,1... | collective-permute-start | bytes 24584 | tf_op jit(solution)/shard_map/ppermute | solution.py:194
  44.6 16.4 %all-to-all-start.1 = ((f32[8,160,128]{2,1,0:T(8,128)}), f32[8,160,128]{2,1,0:T(8,128)S(1)}, u32[]{:S(2)}, u32[]{:S(2)}) async-start(f32[8,160,128]{2,1,0:T(8,128)} %propagate_1.1), calls=%async_computation.1 | async-start | bytes 1310720 | tf_op jit(solution)/shard_map/all_to_all | solution.py:216
  50.1 15.2 %copy-start.1 = (s32[4,1296]{1,0:T(4,128)S(1)}, s32[4,1296]{1,0:T(4,128)}, u32[]{:S(2)}) copy-start(s32[4,1296]{1,0:T(4,128)} %param.9) | copy-start | bytes 62212
  50.1 15.3 %copy-start.2 = (s32[8,2,4]{1,0,2:T(8,128)S(1)}, s32[8,2,4]{1,0,2:T(8,128)}, u32[]{:S(2)}) copy-start(s32[8,2,4]{1,0,2:T(8,128)} %constant.52.clone) | copy-start | bytes 772
  53.3 12.8 %copy-start.3 = (f32[1296]{0:T(1024)S(1)}, f32[1296]{0:T(1024)}, u32[]{:S(2)}) copy-start(f32[1296]{0:T(1024)} %param.10) | copy-start | bytes 15556
  53.3 13.0 %copy-start.4 = (f32[1296]{0:T(1024)S(1)}, f32[1296]{0:T(1024)}, u32[]{:S(2)}) copy-start(f32[1296]{0:T(1024)} %param.11) | copy-start | bytes 15556
  61.0 15.6 %all-to-all-start = ((f32[8,168,128]{2,1,0:T(8,128)}), f32[8,168,128]{2,1,0:T(8,128)S(1)}, u32[]{:S(2)}, u32[]{:S(2)}) async-start(f32[8,168,128]{2,1,0:T(8,128)} %propagate_0.1), calls=%async_computation | async-start | bytes 1376256 | tf_op jit(solution)/shard_map/all_to_all | solution.py:216

commit v3 on v2

--- a/solution.py
+++ b/solution.py
@@ -54,8 +54,8 @@
     return pl.ds(pl.multiple_of(row, 2), 2)
 
 
-def propagate_kernel(first, quarter_ref, coef_ref, own_ref, halo_ref, own_mask_ref, halo_mask_ref, out_ref):
-    size = own_ref.shape[0]
+def propagate_kernel(first, quarter_ref, coef_ref, own_ref, halo_ref, out_ref):
+    size = own_ref.shape[0] - 1
     side_by_side = max(n for n in range(1, TOGETHER + 1) if size % n == 0)
     quarter = quarter_ref[0]
     lane = lax.broadcasted_iota(jnp.int32, (8, 128), 1)
@@ -69,7 +69,7 @@
             whole = jnp.concatenate([halo, own] if east else [own, halo], axis=0)
             return [whole[:, 128 * i : 128 * (i + 1)] for i in range(ROW_TILES)]
 
-        mask = rows(own_mask_ref[...].astype(jnp.float32), halo_mask_ref[...].astype(jnp.float32))
+        mask = rows(own_ref[size], halo_ref[size])
         edge = lane == (0 if north else 127)
         base = 4 if east else 0
 
@@ -189,10 +189,11 @@
     params = pltpu.CompilerParams(vmem_limit_bytes=VMEM_LIMIT)
 
     starts = [sum(CHUNKS[:i]) for i in range(len(CHUNKS))]
-    owns = [lax.slice_in_dim(spectrum, s, s + n, axis=0) for s, n in zip(starts, CHUNKS)]
-    halos = [lax.ppermute(owns[0], ("comp", "tile"), pairs)]
-    halo_mask = lax.ppermute(sea_mask, ("comp", "tile"), pairs)
-    halos += [lax.ppermute(own, ("comp", "tile"), pairs) for own in owns[1:]]
+    mask = sea_mask.astype(jnp.float32)[None]
+    owns = [
+        jnp.concatenate([lax.slice_in_dim(spectrum, s, s + n, axis=0), mask], axis=0) for s, n in zip(starts, CHUNKS)
+    ]
+    halos = [lax.ppermute(own, ("comp", "tile"), pairs) for own in owns]
 
     spare = group_rows // 2 - comp_dev
     own_rows = np.arange(groups)[:, None] * group_rows + 2 * (comp_dev + np.arange(spare))[None]
@@ -206,13 +207,13 @@
     for i, (start, size) in enumerate(zip(starts, CHUNKS)):
         moved = pl.pallas_call(
             functools.partial(propagate_kernel, start),
-            in_specs=[smem, smem, vmem, vmem, vmem, vmem],
+            in_specs=[smem, smem, vmem, vmem],
             out_specs=vmem,
             out_shape=jax.ShapeDtypeStruct((groups, rows_of(size), 128), jnp.float32),
             compiler_params=params,
             cost_estimate=pl.CostEstimate(flops=100 * size * 2048, bytes_accessed=12 * size * 2048, transcendentals=0),
             name=f"propagate_{i}",
-        )(quarter, table, owns[i], halos[i], sea_mask, halo_mask)
+        )(quarter, table, owns[i], halos[i])
         pieces.append(lax.all_to_all(moved, "comp", split_axis=0, concat_axis=0, tiled=True))
 
     total_rows = groups * group_rows

time: 114 us -> 99.8 us (0.88)
  waiting for transfers between devices: 45.5 us -> 35.3 us
  starting transfers between devices: 20.5 us -> 17.9 us
  local copies, waits for them, and re-layouts: 4.1 us -> 2.15 us
    all_to_all x2, waiting for transfers between devices: 17.7 us -> 12.2 us  [per_device(): lax.all_to_all(moved, 'comp', split_axis=0, concat_axis=0, tiled=True)]
    ppermute x3 -> x2, waiting for transfers between devices: 27.8 us -> 23.1 us  [per_device(): halos = [lax.ppermute(own, ('comp', 'tile'), pairs) for own in owns]]
    ppermute x3 -> x2, starting transfers between devices: 10.6 us -> 7.22 us  [per_device(): halos = [lax.ppermute(own, ('comp', 'tile'), pairs) for own in owns]]
    slice x2 -> x4, local copies, waits for them, and re-layouts: 2.28 us -> 0.34 us  [per_device(): lax.slice_in_dim(spectrum, s, s + n, axis=0)]
  transfers between devices with their start and end apart: 5 -> 4, of which waited for: 3 -> 4; matrix products, arithmetic and copies ran while one was open for 3% -> 2% of each run, Pallas kernels for 6% -> 6%
where the time goes in v3:
time: 99.8 us; the launch traced here: 99.4 us
  waiting for transfers between devices  35.3 us (35%)
  blocking collectives  22 us (22%)
  Pallas kernels  20.7 us (21%)
  starting transfers between devices  17.9 us (18%)
  local copies, waits for them, and re-layouts  2.15 us (2%)
  other arithmetic  1.18 us (1%)
    ppermute x2, waiting for transfers between devices, per_device(): halos = [lax.ppermute(own, ('comp', 'tile'), pairs) for own in owns]  23.1 us
    all_to_all x1, blocking collectives, per_device(): lax.all_to_all(fresh.reshape(groups, group_rows, 128), 'comp', split_axis...  22 us
    pallas_call x1, Pallas kernels, per_device(): pl.pallas_call(settle_kernel, in_specs=[smem, smem, smem] + [pl.BlockSpec...  12.9 us
    all_to_all x2, waiting for transfers between devices, per_device(): lax.all_to_all(moved, 'comp', split_axis=0, concat_axis=0, tiled=True)  12.2 us
    all_to_all x2, starting transfers between devices, per_device(): lax.all_to_all(moved, 'comp', split_axis=0, concat_axis=0, tiled=True)  10.7 us
    ppermute x2, starting transfers between devices, per_device(): halos = [lax.ppermute(own, ('comp', 'tile'), pairs) for own in owns]  7.22 us
    pallas_call x2, Pallas kernels, per_device(): pl.pallas_call(functools.partial(propagate_kernel, start), in_specs=[smem...  6.27 us
  transfers between devices with their start and end apart: 4, of which 4 were waited for; matrix products, arithmetic and copies ran while one was open for 2% of the time, Pallas kernels for 6%

profile of v3, /device:TPU:7, one launch (start us, length us, event | category | flops | bytes accessed | tf_op | source)
XLA Modules:
  0.0 99.4 jit_solution(13158696480373809945)
XLA Ops:
  0.0 0.0 slice-start
  0.0 0.8 convert_bitcast_fusion
  0.8 0.3 slice-done
  1.1 0.0 slice-start.1
  1.1 0.1 pad_maximum_fusion.1.own_ref
  1.2 3.7 %collective-permute-start.1 = (f32[79,4,512]{2,1,0:T(4,128)S(1)}, f32[79,4,512]{2,1,0:T(4,128)S(1)}, u32[]{:S(2)}, u32[]{:S(2)}) collective-permute-start(f32[79,4,512]{2,1,0:T(4,128)S(1)} %pad_maximum_fusion.1.own_ref), channel_id=1, source_target_pairs={{0,1},{1,2},{2,3},{3,4},{4,5},{5,6},{6,7},{7,8},{8,9},{9,10},{10,1... | collective-permute-start | bytes 1941512 | tf_op jit(solution)/shard_map/ppermute | solution.py:196
  4.9 0.0 slice-done.1
  4.9 0.2 pad_maximum_fusion.own_ref
  5.1 3.5 %collective-permute-start = (f32[85,4,512]{2,1,0:T(4,128)S(1)}, f32[85,4,512]{2,1,0:T(4,128)S(1)}, u32[]{:S(2)}, u32[]{:S(2)}) collective-permute-start(f32[85,4,512]{2,1,0:T(4,128)S(1)} %pad_maximum_fusion.own_ref), channel_id=1, source_target_pairs={{0,1},{1,2},{2,3},{3,4},{4,5},{5,6},{6,7},{7,8},{8,9},{9,10},{10,1... | collective-permute-start | bytes 2088968 | tf_op jit(solution)/shard_map/ppermute | solution.py:196
  8.7 0.8 dynamic_slice.3.coef_ref
  9.5 17.6 %collective-permute-done.1.halo_ref = f32[79,4,512]{2,1,0:T(4,128)S(1)} collective-permute-done((f32[79,4,512]{2,1,0:T(4,128)S(1)}, f32[79,4,512]{2,1,0:T(4,128)S(1)}, u32[]{:S(2)}, u32[]{:S(2)}) %collective-permute-start.1) | collective-permute-done | bytes 647200 | tf_op jit(solution)/shard_map/ppermute | solution.py:196
  27.0 3.1 %propagate_1.1 = f32[8,160,128]{2,1,0:T(8,128)} custom-call(s32[1]{0:T(128)} %bitcast.3.quarter_ref, f32[486]{0:T(512)S(1)} %dynamic_slice.3.coef_ref, f32[79,4,512]{2,1,0:T(4,128)S(1)} %pad_maximum_fusion.1.own_ref, f32[79,4,512]{2,1,0:T(4,128)S(1)} %collective-permute-done.1.halo_ref), custom_call_target="tpu_custom_call" | custom-call | flops 15974400 | bytes 1916928 | tf_op jit(solution)/shard_map/propagate_1/pallas_call | solution.py:208
  30.1 6.3 %all-to-all-start.1 = ((f32[8,160,128]{2,1,0:T(8,128)}), f32[8,160,128]{2,1,0:T(8,128)S(1)}, u32[]{:S(2)}, u32[]{:S(2)}) async-start(f32[8,160,128]{2,1,0:T(8,128)} %propagate_1.1), calls=%async_computation.1 | async-start | bytes 1310720 | tf_op jit(solution)/shard_map/all_to_all | solution.py:217
  36.5 0.0 copy-start
  36.5 0.0 copy-start.1
  36.5 5.5 %collective-permute-done.halo_ref = f32[85,4,512]{2,1,0:T(4,128)S(1)} collective-permute-done((f32[85,4,512]{2,1,0:T(4,128)S(1)}, f32[85,4,512]{2,1,0:T(4,128)S(1)}, u32[]{:S(2)}, u32[]{:S(2)}) %collective-permute-start) | collective-permute-done | bytes 696352 | tf_op jit(solution)/shard_map/ppermute | solution.py:196
  42.0 3.2 %propagate_0.1 = f32[8,168,128]{2,1,0:T(8,128)} custom-call(s32[1]{0:T(128)} %bitcast.3.quarter_ref, f32[486]{0:T(512)S(1)} %dynamic_slice.3.coef_ref, f32[85,4,512]{2,1,0:T(4,128)S(1)} %pad_maximum_fusion.own_ref, f32[85,4,512]{2,1,0:T(4,128)S(1)} %collective-permute-done.halo_ref), custom_call_target="tpu_custom_call" | custom-call | flops 17203200 | bytes 2064384 | tf_op jit(solution)/shard_map/propagate_0/pallas_call | solution.py:208
  45.2 0.0 copy-start.2
  45.2 0.0 copy-start.3
  45.2 2.2 %all-to-all-done.1.refs_1_ = f32[8,160,128]{2,1,0:T(8,128)S(1)} async-done(((f32[8,160,128]{2,1,0:T(8,128)}), f32[8,160,128]{2,1,0:T(8,128)S(1)}, u32[]{:S(2)}, u32[]{:S(2)}) %all-to-all-start.1) | async-done | bytes 655392 | tf_op jit(solution)/shard_map/all_to_all | solution.py:217
  47.3 4.3 %all-to-all-start = ((f32[8,168,128]{2,1,0:T(8,128)}), f32[8,168,128]{2,1,0:T(8,128)S(1)}, u32[]{:S(2)}, u32[]{:S(2)}) async-start(f32[8,168,128]{2,1,0:T(8,128)} %propagate_0.1), calls=%async_computation | async-start | bytes 1376256 | tf_op jit(solution)/shard_map/all_to_all | solution.py:217
  51.7 0.0 copy-done
  51.7 0.1 reshape.24
  51.8 0.0 copy-done.1
  51.8 0.1 pad_add_fusion
  51.9 0.3 copy.9
  52.2 0.3 reshape.25.bins_ref
  52.5 0.0 copy-done.2
  52.5 0.1 reshape.26
  52.6 0.1 reshape.27.coupling_ref
  52.7 0.0 copy-done.3
  52.7 0.1 reshape.28
  52.8 0.1 reshape.29.growth_ref
  52.9 10.0 %all-to-all-done.refs_0_ = f32[8,168,128]{2,1,0:T(8,128)S(1)} async-done(((f32[8,168,128]{2,1,0:T(8,128)}), f32[8,168,128]{2,1,0:T(8,128)S(1)}, u32[]{:S(2)}, u32[]{:S(2)}) %all-to-all-start) | async-done | bytes 688160 | tf_op jit(solution)/shard_map/all_to_all | solution.py:217
  62.9 12.9 %settle.1 = f32[2624,128]{1,0:T(8,128)S(1)} custom-call(s32[5248]{0:T(1024)S(1)} %reshape.25.bins_ref, f32[1312]{0:T(1024)S(1)} %reshape.27.coupling_ref, f32[1312]{0:T(1024)S(1)} %reshape.29.growth_ref, f32[8,168,128]{2,1,0:T(8,128)S(1)} %all-to-all-done.refs_0_, f32[8,160,128]{2,1,0:T(8,128)S(1)} %all-to-all-done.1.refs_1_), custom_call_target="tpu_custom_call" | custom-call | tf_op jit(solution)/shard_map/settle/pallas_call | solution.py:220
  75.8 22.0 %all_to_all.15.in_ref = f32[8,328,128]{2,1,0:T(8,128)S(1)} all-to-all(f32[8,328,128]{2,1,0:T(8,128)S(1)} %bitcast.12), channel_id=1, replica_groups=mesh['comp'=8,'tile'=64] {'comp'}, dimensions={0} | all-to-all | bytes 2686976 | tf_op jit(solution)/shard_map/all_to_all | solution.py:231
  97.8 1.6 %unpack.1 = f32[162,4,512]{2,1,0:T(4,128)} custom-call(f32[8,328,128]{2,1,0:T(8,128)S(1)} %all_to_all.15.in_ref), custom_call_target="tpu_custom_call" | custom-call | tf_op jit(solution)/shard_map/unpack/pallas_call | solution.py:232
  (5 shorter events, 0.1 us)
Async XLA Ops:
  0.0 1.1 %slice-start = ((f32[162,4,512]{2,1,0:T(4,128)}), f32[78,4,512]{2,1,0:T(4,128)S(1)}, s32[]{:S(2)}) async-start(f32[162,4,512]{2,1,0:T(4,128)} %param.7), calls=%async_computation.3 | async-start | bytes 1277952 | tf_op jit(solution)/shard_map/slice | solution.py:194
  1.1 3.8 %slice-start.1 = ((f32[162,4,512]{2,1,0:T(4,128)}), f32[84,4,512]{2,1,0:T(4,128)S(1)}, s32[]{:S(2)}) async-start(f32[162,4,512]{2,1,0:T(4,128)} %param.7), calls=%async_computation.4 | async-start | bytes 1376256 | tf_op jit(solution)/shard_map/slice | solution.py:194
  1.2 25.8 %collective-permute-start.1 = (f32[79,4,512]{2,1,0:T(4,128)S(1)}, f32[79,4,512]{2,1,0:T(4,128)S(1)}, u32[]{:S(2)}, u32[]{:S(2)}) collective-permute-start(f32[79,4,512]{2,1,0:T(4,128)S(1)} %pad_maximum_fusion.1.own_ref), channel_id=1, source_target_pairs={{0,1},{1,2},{2,3},{3,4},{4,5},{5,6},{6,7},{7,8},{8,9},{9,10},{10,1... | collective-permute-start | bytes 1941512 | tf_op jit(solution)/shard_map/ppermute | solution.py:196
  5.1 36.9 %collective-permute-start = (f32[85,4,512]{2,1,0:T(4,128)S(1)}, f32[85,4,512]{2,1,0:T(4,128)S(1)}, u32[]{:S(2)}, u32[]{:S(2)}) collective-permute-start(f32[85,4,512]{2,1,0:T(4,128)S(1)} %pad_maximum_fusion.own_ref), channel_id=1, source_target_pairs={{0,1},{1,2},{2,3},{3,4},{4,5},{5,6},{6,7},{7,8},{8,9},{9,10},{10,1... | collective-permute-start | bytes 2088968 | tf_op jit(solution)/shard_map/ppermute | solution.py:196
  30.1 17.2 %all-to-all-start.1 = ((f32[8,160,128]{2,1,0:T(8,128)}), f32[8,160,128]{2,1,0:T(8,128)S(1)}, u32[]{:S(2)}, u32[]{:S(2)}) async-start(f32[8,160,128]{2,1,0:T(8,128)} %propagate_1.1), calls=%async_computation.1 | async-start | bytes 1310720 | tf_op jit(solution)/shard_map/all_to_all | solution.py:217
  36.5 15.2 %copy-start = (s32[4,1296]{1,0:T(4,128)S(1)}, s32[4,1296]{1,0:T(4,128)}, u32[]{:S(2)}) copy-start(s32[4,1296]{1,0:T(4,128)} %param.9) | copy-start | bytes 62212
  36.5 15.3 %copy-start.1 = (s32[8,2,4]{1,0,2:T(8,128)S(1)}, s32[8,2,4]{1,0,2:T(8,128)}, u32[]{:S(2)}) copy-start(s32[8,2,4]{1,0,2:T(8,128)} %constant.52.clone) | copy-start | bytes 772
  45.2 7.3 %copy-start.2 = (f32[1296]{0:T(1024)S(1)}, f32[1296]{0:T(1024)}, u32[]{:S(2)}) copy-start(f32[1296]{0:T(1024)} %param.10) | copy-start | bytes 15556
  45.2 7.5 %copy-start.3 = (f32[1296]{0:T(1024)S(1)}, f32[1296]{0:T(1024)}, u32[]{:S(2)}) copy-start(f32[1296]{0:T(1024)} %param.11) | copy-start | bytes 15556
  47.3 15.6 %all-to-all-start = ((f32[8,168,128]{2,1,0:T(8,128)}), f32[8,168,128]{2,1,0:T(8,128)S(1)}, u32[]{:S(2)}, u32[]{:S(2)}) async-start(f32[8,168,128]{2,1,0:T(8,128)} %propagate_0.1), calls=%async_computation | async-start | bytes 1376256 | tf_op jit(solution)/shard_map/all_to_all | solution.py:217

commit v4 on v3

--- a/solution.py
+++ b/solution.py
@@ -19,7 +19,7 @@
 time_step = 0.5
 
 ROW_TILES = 4
-CHUNKS = (84, 78)
+CHUNKS = (96, 66)
 TOGETHER = 28
 VMEM_LIMIT = 40 << 20
 
@@ -103,58 +103,53 @@
         pl.when(quarter == value)(functools.partial(run, east, north))
 
 
-def settle_kernel(bins_ref, coupling_ref, growth_ref, *refs):
-    pieces, (out_ref, energy_ref, a_ref, b_ref, c_ref, d_ref, sems) = refs[: len(CHUNKS)], refs[len(CHUNKS) :]
-    parts = (a_ref, b_ref, c_ref, d_ref)
+def settle_kernel(bins_ref, strength_ref, kept_ref, *refs):
+    pieces = refs[: len(CHUNKS)]
+    out_ref, energy_ref, *parts = refs[len(CHUNKS) :]
     total_rows = energy_ref.shape[0]
     groups = pieces[0].shape[0]
-    copies = []
-    start = 0
-    for piece in pieces:
-        rows = piece.shape[1]
-        for g in range(groups):
-            place = energy_ref.at[pl.ds(g * (total_rows // groups) + start, rows), :]
-            copies.append(pltpu.make_async_copy(piece.at[g], place, sems.at[len(copies)]))
-        start += rows
-    for copy in copies:
-        copy.start()
 
     def tile_of(t):
         return pl.ds(pl.multiple_of(8 * t, 8), 8)
 
-    def clear(t, carry):
-        for ref in parts:
-            ref[tile_of(t), :] = jnp.zeros((8, 128), jnp.float32)
-        return carry
-
-    lax.fori_loop(0, total_rows // 8, clear, 0, unroll=4)
-    for copy in copies:
-        copy.wait()
+    def take(piece, shift, g, carry):
+        for t in range(piece.shape[1] // 8):
+            here = pl.ds(pl.multiple_of(g * (total_rows // groups) + shift + 8 * t, 8), 8)
+            energy_ref[here, :] = piece[g, 8 * t : 8 * t + 8, :]
+            for ref in parts:
+                ref[here, :] = jnp.zeros((8, 128), jnp.float32)
+        return carry
+
+    shift = 0
+    for piece in pieces:
+        lax.fori_loop(0, groups, functools.partial(take, piece, shift), 0)
+        shift += piece.shape[1]
 
     def one(k, carry):
         rows = [pair_of(bins_ref[4 * k + j]) for j in range(4)]
         here = pair_of(2 * k)
         energy = energy_ref[here, :]
-        scaled = coupling_ref[k] * energy
-        total = growth_ref[k] * energy
+        scaled = strength_ref[k] * energy
+        cross, squared = (2.0 * w_cross) * scaled, scaled * energy
+        squared_plus, squared_minus = w_plus * squared, w_minus * squared
+        deltas = []
         for mirror in range(2):
-            p, q = rows[2 * mirror], rows[2 * mirror + 1]
-            plus, minus = energy_ref[p, :], energy_ref[q, :]
-            delta = scaled * (energy * (w_plus * plus + w_minus * minus) - (2.0 * w_cross) * plus * minus)
-            total = total - 2.0 * delta
-            for ref, row in ((parts[2 * mirror], p), (parts[2 * mirror + 1], q)):
-                ref[row, :] = ref[row, :] + delta
-        out_ref[here, :] = total
+            plus, minus = (energy_ref[row, :] for row in rows[2 * mirror : 2 * mirror + 2])
+            deltas.append(minus * (squared_minus - cross * plus) + squared_plus * plus)
+        for j, row in enumerate(rows):
+            parts[j][row, :] = parts[j][row, :] + deltas[j // 2]
+        out_ref[here, :] = kept_ref[k] * energy - 2.0 * (deltas[0] + deltas[1])
         return carry
 
     lax.fori_loop(0, total_rows // 2, one, 0, unroll=16)
 
     def gather(t, carry):
         s = tile_of(t)
-        out_ref[s, :] = out_ref[s, :] + ((a_ref[s, :] + b_ref[s, :]) + (c_ref[s, :] + d_ref[s, :]))
-        return carry
-
-    lax.fori_loop(0, total_rows // 8, gather, 0, unroll=4)
+        a, b, c, d = (ref[s, :] for ref in parts)
+        out_ref[s, :] = out_ref[s, :] + ((a + b) + (c + d))
+        return carry
+
+    lax.fori_loop(0, total_rows // 8, gather, 0, unroll=8)
 
 
 def unpack_kernel(in_ref, out_ref):
@@ -200,6 +195,7 @@
     where = 2 * quad_bins.T + (group_rows - 2 * comp_dev) * (quad_bins.T // comp_dev)
     fill = jnp.asarray(np.repeat(own_rows[:, :, None], 4, axis=2).astype(np.int32))
     where = jnp.concatenate([where.reshape(groups, comp_dev, 4), fill], axis=1).reshape(-1)
+
     pad = lambda v: jnp.pad(v.reshape(groups, comp_dev), ((0, 0), (0, spare))).reshape(-1)
     strength, kept = pad(time_step * coupling), pad(1.0 + time_step * growth)
 
@@ -219,11 +215,10 @@
     total_rows = groups * group_rows
     fresh = pl.pallas_call(
         settle_kernel,
-        in_specs=[smem, smem, smem] + [pl.BlockSpec(memory_space=pl.ANY)] * len(CHUNKS),
+        in_specs=[smem, smem, smem] + [vmem] * len(CHUNKS),
         out_specs=vmem,
         out_shape=jax.ShapeDtypeStruct((total_rows, 128), jnp.float32),
-        scratch_shapes=[pltpu.VMEM((total_rows, 128), jnp.float32)] * 5
-        + [pltpu.SemaphoreType.DMA((len(CHUNKS) * groups,))],
+        scratch_shapes=[pltpu.VMEM((total_rows, 128), jnp.float32)] * 5,
         compiler_params=params,
         name="settle",
     )(where, strength, kept, *pieces)

time: 99.8 us -> 97.6 us (0.978)
  Pallas kernels: 20.7 us -> 18 us
  starting transfers between devices: 17.9 us -> 19.2 us
    pallas_call x1, Pallas kernels: 12.9 us -> 10.2 us  [per_device(): pl.pallas_call(settle_kernel, in_specs=[smem, smem, smem] + [vmem] * len(...]
    all_to_all x2, starting transfers between devices: 10.7 us -> 12 us  [per_device(): lax.all_to_all(moved, 'comp', split_axis=0, concat_axis=0, tiled=True)]
    all_to_all x2, waiting for transfers between devices: 12.2 us -> 11 us  [per_device(): lax.all_to_all(moved, 'comp', split_axis=0, concat_axis=0, tiled=True)]
  transfers between devices with their start and end apart: 4 -> 4, of which waited for: 4 -> 3; matrix products, arithmetic and copies ran while one was open for 2% -> 2% of each run, Pallas kernels for 6% -> 6%
where the time goes in v4:
time: 97.6 us; the launch traced here: 97.1 us
  waiting for transfers between devices  34.4 us (35%)
  blocking collectives  22 us (23%)
  starting transfers between devices  19.2 us (20%)
  Pallas kernels  18 us (18%)
  local copies, waits for them, and re-layouts  2.12 us (2%)
  other arithmetic  1.18 us (1%)
    ppermute x2, waiting for transfers between devices, per_device(): halos = [lax.ppermute(own, ('comp', 'tile'), pairs) for own in owns]  23.4 us
    all_to_all x1, blocking collectives, per_device(): lax.all_to_all(fresh.reshape(groups, group_rows, 128), 'comp', split_axis...  22 us
    all_to_all x2, starting transfers between devices, per_device(): lax.all_to_all(moved, 'comp', split_axis=0, concat_axis=0, tiled=True)  12 us
    all_to_all x2, waiting for transfers between devices, per_device(): lax.all_to_all(moved, 'comp', split_axis=0, concat_axis=0, tiled=True)  11 us
    pallas_call x1, Pallas kernels, per_device(): pl.pallas_call(settle_kernel, in_specs=[smem, smem, smem] + [vmem] * len(...  10.2 us
    ppermute x2, starting transfers between devices, per_device(): halos = [lax.ppermute(own, ('comp', 'tile'), pairs) for own in owns]  7.22 us
    pallas_call x2, Pallas kernels, per_device(): pl.pallas_call(functools.partial(propagate_kernel, start), in_specs=[smem...  6.21 us
  transfers between devices with their start and end apart: 4, of which 3 were waited for; matrix products, arithmetic and copies ran while one was open for 2% of the time, Pallas kernels for 6%

profile of v4, /device:TPU:7, one launch (start us, length us, event | category | flops | bytes accessed | tf_op | source)
XLA Modules:
  0.0 97.1 jit_solution(12081321009961393094)
XLA Ops:
  0.0 0.0 slice-start
  0.0 0.8 convert_bitcast_fusion
  0.8 0.3 slice-done
  1.1 0.0 slice-start.1
  1.1 0.1 pad_maximum_fusion.1.own_ref
  1.2 3.7 %collective-permute-start.1 = (f32[67,4,512]{2,1,0:T(4,128)S(1)}, f32[67,4,512]{2,1,0:T(4,128)S(1)}, u32[]{:S(2)}, u32[]{:S(2)}) collective-permute-start(f32[67,4,512]{2,1,0:T(4,128)S(1)} %pad_maximum_fusion.1.own_ref), channel_id=1, source_target_pairs={{0,1},{1,2},{2,3},{3,4},{4,5},{5,6},{6,7},{7,8},{8,9},{9,10},{10,1... | collective-permute-start | bytes 1646600 | tf_op jit(solution)/shard_map/ppermute | solution.py:191
  4.9 0.0 slice-done.1
  4.9 0.2 pad_maximum_fusion.own_ref
  5.1 3.5 %collective-permute-start = (f32[97,4,512]{2,1,0:T(4,128)S(1)}, f32[97,4,512]{2,1,0:T(4,128)S(1)}, u32[]{:S(2)}, u32[]{:S(2)}) collective-permute-start(f32[97,4,512]{2,1,0:T(4,128)S(1)} %pad_maximum_fusion.own_ref), channel_id=1, source_target_pairs={{0,1},{1,2},{2,3},{3,4},{4,5},{5,6},{6,7},{7,8},{8,9},{9,10},{10,1... | collective-permute-start | bytes 2383880 | tf_op jit(solution)/shard_map/ppermute | solution.py:191
  8.6 0.8 dynamic_slice.3.coef_ref
  9.4 15.5 %collective-permute-done.1.halo_ref = f32[67,4,512]{2,1,0:T(4,128)S(1)} collective-permute-done((f32[67,4,512]{2,1,0:T(4,128)S(1)}, f32[67,4,512]{2,1,0:T(4,128)S(1)}, u32[]{:S(2)}, u32[]{:S(2)}) %collective-permute-start.1) | collective-permute-done | bytes 548896 | tf_op jit(solution)/shard_map/ppermute | solution.py:191
  24.9 2.8 %propagate_1.1 = f32[8,136,128]{2,1,0:T(8,128)} custom-call(s32[1]{0:T(128)} %bitcast.3.quarter_ref, f32[486]{0:T(512)S(1)} %dynamic_slice.3.coef_ref, f32[67,4,512]{2,1,0:T(4,128)S(1)} %pad_maximum_fusion.1.own_ref, f32[67,4,512]{2,1,0:T(4,128)S(1)} %collective-permute-done.1.halo_ref), custom_call_target="tpu_custom_call" | custom-call | flops 13516800 | bytes 1622016 | tf_op jit(solution)/shard_map/propagate_1/pallas_call | solution.py:204
  27.6 6.3 %all-to-all-start.1 = ((f32[8,136,128]{2,1,0:T(8,128)}), f32[8,136,128]{2,1,0:T(8,128)S(1)}, u32[]{:S(2)}, u32[]{:S(2)}) async-start(f32[8,136,128]{2,1,0:T(8,128)} %propagate_1.1), calls=%async_computation.1 | async-start | bytes 1114112 | tf_op jit(solution)/shard_map/all_to_all | solution.py:213
  34.0 7.9 %collective-permute-done.halo_ref = f32[97,4,512]{2,1,0:T(4,128)S(1)} collective-permute-done((f32[97,4,512]{2,1,0:T(4,128)S(1)}, f32[97,4,512]{2,1,0:T(4,128)S(1)}, u32[]{:S(2)}, u32[]{:S(2)}) %collective-permute-start) | collective-permute-done | bytes 794656 | tf_op jit(solution)/shard_map/ppermute | solution.py:191
  41.9 3.5 %propagate_0.1 = f32[8,192,128]{2,1,0:T(8,128)} custom-call(s32[1]{0:T(128)} %bitcast.3.quarter_ref, f32[486]{0:T(512)S(1)} %dynamic_slice.3.coef_ref, f32[97,4,512]{2,1,0:T(4,128)S(1)} %pad_maximum_fusion.own_ref, f32[97,4,512]{2,1,0:T(4,128)S(1)} %collective-permute-done.halo_ref), custom_call_target="tpu_custom_call" | custom-call | flops 19660800 | bytes 2359296 | tf_op jit(solution)/shard_map/propagate_0/pallas_call | solution.py:204
  45.4 0.0 copy-start
  45.4 0.0 copy-start.1
  45.4 0.0 copy-start.2
  45.4 0.0 copy-start.3
  45.4 0.0 all-to-all-done.1.refs_1_
  45.4 5.7 %all-to-all-start = ((f32[8,192,128]{2,1,0:T(8,128)}), f32[8,192,128]{2,1,0:T(8,128)S(1)}, u32[]{:S(2)}, u32[]{:S(2)}) async-start(f32[8,192,128]{2,1,0:T(8,128)} %propagate_0.1), calls=%async_computation | async-start | bytes 1572864 | tf_op jit(solution)/shard_map/all_to_all | solution.py:213
  51.1 0.0 copy-done
  51.1 0.1 reshape.24
  51.2 0.0 copy-done.1
  51.2 0.1 pad_add_fusion
  51.3 0.3 copy.9
  51.6 0.3 reshape.25.bins_ref
  51.9 0.0 copy-done.2
  51.9 0.1 reshape.26
  52.0 0.1 reshape.27.strength_ref
  52.1 0.0 copy-done.3
  52.1 0.1 reshape.28
  52.2 0.1 reshape.29.kept_ref
  52.3 11.0 %all-to-all-done.refs_0_ = f32[8,192,128]{2,1,0:T(8,128)S(1)} async-done(((f32[8,192,128]{2,1,0:T(8,128)}), f32[8,192,128]{2,1,0:T(8,128)S(1)}, u32[]{:S(2)}, u32[]{:S(2)}) %all-to-all-start) | async-done | bytes 786464 | tf_op jit(solution)/shard_map/all_to_all | solution.py:213
  63.3 10.2 %settle.1 = f32[2624,128]{1,0:T(8,128)S(1)} custom-call(s32[5248]{0:T(1024)S(1)} %reshape.25.bins_ref, f32[1312]{0:T(1024)S(1)} %reshape.27.strength_ref, f32[1312]{0:T(1024)S(1)} %reshape.29.kept_ref, f32[8,192,128]{2,1,0:T(8,128)S(1)} %all-to-all-done.refs_0_, f32[8,136,128]{2,1,0:T(8,128)S(1)} %all-to-all-done.1.refs_1_), custom_call_target="tpu_custom_call" | custom-call | tf_op jit(solution)/shard_map/settle/pallas_call | solution.py:216
  73.6 22.0 %all_to_all.15.in_ref = f32[8,328,128]{2,1,0:T(8,128)S(1)} all-to-all(f32[8,328,128]{2,1,0:T(8,128)S(1)} %bitcast.12), channel_id=1, replica_groups=mesh['comp'=8,'tile'=64] {'comp'}, dimensions={0} | all-to-all | bytes 2686976 | tf_op jit(solution)/shard_map/all_to_all | solution.py:226
  95.6 1.6 %unpack.1 = f32[162,4,512]{2,1,0:T(4,128)} custom-call(f32[8,328,128]{2,1,0:T(8,128)S(1)} %all_to_all.15.in_ref), custom_call_target="tpu_custom_call" | custom-call | tf_op jit(solution)/shard_map/unpack/pallas_call | solution.py:227
  (5 shorter events, 0.1 us)
Async XLA Ops:
  0.0 1.1 %slice-start = ((f32[162,4,512]{2,1,0:T(4,128)}), f32[66,4,512]{2,1,0:T(4,128)S(1)}, s32[]{:S(2)}) async-start(f32[162,4,512]{2,1,0:T(4,128)} %param.7), calls=%async_computation.3 | async-start | bytes 1081344 | tf_op jit(solution)/shard_map/slice | solution.py:189
  1.1 3.8 %slice-start.1 = ((f32[162,4,512]{2,1,0:T(4,128)}), f32[96,4,512]{2,1,0:T(4,128)S(1)}, s32[]{:S(2)}) async-start(f32[162,4,512]{2,1,0:T(4,128)} %param.7), calls=%async_computation.4 | async-start | bytes 1572864 | tf_op jit(solution)/shard_map/slice | solution.py:189
  1.2 23.7 %collective-permute-start.1 = (f32[67,4,512]{2,1,0:T(4,128)S(1)}, f32[67,4,512]{2,1,0:T(4,128)S(1)}, u32[]{:S(2)}, u32[]{:S(2)}) collective-permute-start(f32[67,4,512]{2,1,0:T(4,128)S(1)} %pad_maximum_fusion.1.own_ref), channel_id=1, source_target_pairs={{0,1},{1,2},{2,3},{3,4},{4,5},{5,6},{6,7},{7,8},{8,9},{9,10},{10,1... | collective-permute-start | bytes 1646600 | tf_op jit(solution)/shard_map/ppermute | solution.py:191
  5.1 36.8 %collective-permute-start = (f32[97,4,512]{2,1,0:T(4,128)S(1)}, f32[97,4,512]{2,1,0:T(4,128)S(1)}, u32[]{:S(2)}, u32[]{:S(2)}) collective-permute-start(f32[97,4,512]{2,1,0:T(4,128)S(1)} %pad_maximum_fusion.own_ref), channel_id=1, source_target_pairs={{0,1},{1,2},{2,3},{3,4},{4,5},{5,6},{6,7},{7,8},{8,9},{9,10},{10,1... | collective-permute-start | bytes 2383880 | tf_op jit(solution)/shard_map/ppermute | solution.py:191
  27.6 17.7 %all-to-all-start.1 = ((f32[8,136,128]{2,1,0:T(8,128)}), f32[8,136,128]{2,1,0:T(8,128)S(1)}, u32[]{:S(2)}, u32[]{:S(2)}) async-start(f32[8,136,128]{2,1,0:T(8,128)} %propagate_1.1), calls=%async_computation.1 | async-start | bytes 1114112 | tf_op jit(solution)/shard_map/all_to_all | solution.py:213
  45.4 5.7 %copy-start = (s32[4,1296]{1,0:T(4,128)S(1)}, s32[4,1296]{1,0:T(4,128)}, u32[]{:S(2)}) copy-start(s32[4,1296]{1,0:T(4,128)} %param.9) | copy-start | bytes 62212
  45.4 5.8 %copy-start.1 = (s32[8,2,4]{1,0,2:T(8,128)S(1)}, s32[8,2,4]{1,0,2:T(8,128)}, u32[]{:S(2)}) copy-start(s32[8,2,4]{1,0,2:T(8,128)} %constant.52.clone) | copy-start | bytes 772
  45.4 6.5 %copy-start.2 = (f32[1296]{0:T(1024)S(1)}, f32[1296]{0:T(1024)}, u32[]{:S(2)}) copy-start(f32[1296]{0:T(1024)} %param.10) | copy-start | bytes 15556
  45.4 6.7 %copy-start.3 = (f32[1296]{0:T(1024)S(1)}, f32[1296]{0:T(1024)}, u32[]{:S(2)}) copy-start(f32[1296]{0:T(1024)} %param.11) | copy-start | bytes 15556
  45.4 18.0 %all-to-all-start = ((f32[8,192,128]{2,1,0:T(8,128)}), f32[8,192,128]{2,1,0:T(8,128)S(1)}, u32[]{:S(2)}, u32[]{:S(2)}) async-start(f32[8,192,128]{2,1,0:T(8,128)} %propagate_0.1), calls=%async_computation | async-start | bytes 1572864 | tf_op jit(solution)/shard_map/all_to_all | solution.py:213

commit v5 on v4

v5 whole, which is shorter than its diff:
```python
import functools
import math

import jax
import jax.numpy as jnp
import numpy as np
from jax import lax
from jax.experimental import pallas as pl
from jax.experimental.pallas import tpu as pltpu
from jax.sharding import PartitionSpec as P

NDIR = 36
NFREQ = 36
SUB = 4

w_plus = 0.4096
w_minus = 3.1605
w_cross = 1.2945
time_step = 0.5

ROW_TILES = 4
CHUNKS = (96, 66)
TOGETHER = 28
VMEM_LIMIT = 40 << 20
COST = 200_000


def courant_table():
    d = np.repeat(np.arange(NDIR), NFREQ)
    level = np.tile(np.arange(NFREQ), NDIR)
    angle = 2.0 * math.pi * d / NDIR
    size = 0.7 * 0.93**level
    cos = np.where(d % (NDIR // 2) == NDIR // 4, 0.0, np.cos(angle))
    sin = np.where(d % (NDIR // 2) == 0, 0.0, np.sin(angle))
    along_x, along_y = np.abs(size * cos), np.abs(size * sin)
    return np.stack([1.0 - along_x - along_y, along_x, along_y], axis=1).astype(np.float32)


def is_east(c, groups):
    return c * 4 // groups in (0, 3)


def halo_pairs(groups, tiles, flip):
    pairs = []
    for c in range(groups):
        step = 1 if (c % 2 == 0) != flip else -1
        pairs += [(c * tiles + t, c * tiles + (t + step) % tiles) for t in range(tiles)]
    return pairs


def window_groups(groups, tiles):
    return [[c * tiles + (t if is_east(c, groups) else (t + 1) % tiles) for c in range(groups)] for t in range(tiles)]


def holders(groups):
    east = [c for c in range(groups) if is_east(c, groups)]
    return east, [c for c in range(groups) if c not in east]


def rows_of(size):
    return -(-2 * size // 8) * 8


def pair_of(row):
    return pl.ds(pl.multiple_of(row, 2), 2)


def propagate_kernel(first, place_ref, coef_ref, own_ref, one_ref, other_ref, *refs):
    *before_refs, out_ref = refs
    size = own_ref.shape[0] - 1
    side_by_side = max(n for n in range(1, TOGETHER + 1) if size % n == 0)
    quarter, swapped, at_start, at_end = (place_ref[i] for i in range(4))
    swapped = swapped == 1
    slots = holders(out_ref.shape[0])
    lane = lax.broadcasted_iota(jnp.int32, (8, 128), 1)
    column = lax.broadcasted_iota(jnp.int32, (8, 128), 0)
    extra = out_ref.shape[1] - 2 * (first + size)
    for piece in range(out_ref.shape[0]):
        for ref in before_refs:
            out_ref[piece, : 2 * first, :] = ref[piece]
        if extra:
            out_ref[piece, 2 * (first + size) :, :] = jnp.zeros((extra, 128), jnp.float32)

    def run(east, north):
        def rows(k):
            one, other = one_ref[k], other_ref[k]
            before, after = jnp.where(swapped, other, one), jnp.where(swapped, one, other)
            whole = jnp.concatenate([before, own_ref[k], after], axis=0)
            return [whole[:, 128 * i : 128 * (i + 1)] for i in range(ROW_TILES)]

        mask = rows(size)
        closed = jnp.where(at_start == 1, 2 if east else 1, jnp.where(at_end == 1, 6 if east else 5, -1))
        open_side = jnp.where(column == closed, 0.0, 1.0)
        edge = lane == (0 if north else 127)
        base = 4 if east else 0

        def several(step, carry):
            which = [step * side_by_side + u for u in range(side_by_side)]
            coefs = [[coef_ref[3 * (first + k) + i] for i in range(3)] for k in which]
            fields = [rows(k) for k in which]
            sides = [side * open_side for _, side, _ in coefs]
            for _ in range(SUB):
                turned = [[pltpu.roll(v, 1 if north else 127, 1) for v in field] for field in fields]
                cols = [[pltpu.roll(v, 1 if east else 7, 0) for v in field] for field in fields]
                fresh = []
                for u, (stay, _, along) in enumerate(coefs):
                    field = []
                    for i in range(ROW_TILES):
                        j = i - 1 if north else i + 1
                        over = turned[u][j] if 0 <= j < ROW_TILES else 0.0
                        upwind_row = jnp.where(edge, over, turned[u][i])
                        field.append(mask[i] * (stay * fields[u][i] + sides[u] * cols[u][i] + along * upwind_row))
                    fresh.append(field)
                fields = fresh
            for u, k in enumerate(which):
                for i, v in enumerate(fields[u]):
                    for pair in range(2):
                        at = base + 2 * pair
                        out_ref[slots[pair][i], pair_of(2 * (first + k)), :] = v[at : at + 2, :]
            return carry

        lax.fori_loop(0, size // side_by_side, several, 0)

    for value, (east, north) in enumerate(((True, True), (False, True), (False, False), (True, False))):
        pl.when(quarter == value)(functools.partial(run, east, north))


def settle_kernel(bins_ref, strength_ref, kept_ref, energy_ref, out_ref, *parts):
    total_rows = energy_ref.shape[0]

    def tile_of(t):
        return pl.ds(pl.multiple_of(8 * t, 8), 8)

    def clear(t, carry):
        for ref in parts:
            ref[tile_of(t), :] = jnp.zeros((8, 128), jnp.float32)
        return carry

    lax.fori_loop(0, total_rows // 8, clear, 0, unroll=8)

    def one(k, carry):
        rows = [pair_of(bins_ref[4 * k + j]) for j in range(4)]
        here = pair_of(2 * k)
        energy = energy_ref[here, :]
        scaled = strength_ref[k] * energy
        cross, squared = (2.0 * w_cross) * scaled, scaled * energy
        squared_plus, squared_minus = w_plus * squared, w_minus * squared
        deltas = []
        for mirror in range(2):
            plus, minus = (energy_ref[row, :] for row in rows[2 * mirror : 2 * mirror + 2])
            deltas.append(minus * (squared_minus - cross * plus) + squared_plus * plus)
        for j, row in enumerate(rows):
            parts[j][row, :] = parts[j][row, :] + deltas[j // 2]
        out_ref[here, :] = kept_ref[k] * energy - 2.0 * (deltas[0] + deltas[1])
        return carry

    lax.fori_loop(0, total_rows // 2, one, 0, unroll=16)

    def gather(t, carry):
        s = tile_of(t)
        a, b, c, d = (ref[s, :] for ref in parts)
        out_ref[s, :] = out_ref[s, :] + ((a + b) + (c + d))
        return carry

    lax.fori_loop(0, total_rows // 8, gather, 0, unroll=8)


def unpack_kernel(in_ref, out_ref):
    step_size = 9
    slots = holders(in_ref.shape[0])[::-1]

    def several(step, carry):
        which = [step * step_size + u for u in range(step_size)]
        both = [
            [[in_ref[slots[pair][i], pair_of(2 * k), :] for pair in range(2)] for i in range(ROW_TILES)]
            for k in which
        ]
        for u, k in enumerate(which):
            for i in range(ROW_TILES):
                out_ref[k, :, 128 * i : 128 * (i + 1)] = jnp.concatenate(both[u][i], axis=0)
        return carry

    lax.fori_loop(0, out_ref.shape[0] // step_size, several, 0)


def per_device(spectrum, sea_mask, quad_bins, coupling, growth):
    comp_dev, width, height = spectrum.shape
    groups, tiles = lax.axis_size("comp"), lax.axis_size("tile")
    mine = lax.axis_index("comp")
    count = comp_dev * groups
    group_rows = rows_of(comp_dev)
    table = lax.dynamic_slice(jnp.asarray(courant_table().reshape(-1)), (3 * mine * comp_dev,), (3 * comp_dev,))
    tile = lax.axis_index("tile")
    odd = mine % 2 == 1
    place = jnp.stack([mine * 4 // groups, mine % 2, tile == 0, tile == tiles - 1]).astype(jnp.int32)

    smem = pl.BlockSpec(memory_space=pltpu.SMEM)
    vmem = pl.BlockSpec(memory_space=pltpu.VMEM)
    params = pltpu.CompilerParams(vmem_limit_bytes=VMEM_LIMIT)

    starts = [sum(CHUNKS[:i]) for i in range(len(CHUNKS))]
    mask = sea_mask.astype(jnp.float32)[None]
    owns = [
        jnp.concatenate([lax.slice_in_dim(spectrum, s, s + n, axis=0), mask], axis=0) for s, n in zip(starts, CHUNKS)
    ]
    half = width // 2
    halos = []
    for own in owns:
        start, end = own[:, :half], own[:, width - half :]
        one = lax.ppermute(jnp.where(odd, start, end), ("comp", "tile"), halo_pairs(groups, tiles, False))
        other = lax.ppermute(jnp.where(odd, end, start), ("comp", "tile"), halo_pairs(groups, tiles, True))
        halos.append((one, other))
    windows = window_groups(groups, tiles)

    spare = group_rows // 2 - comp_dev
    own_rows = np.arange(groups)[:, None] * group_rows + 2 * (comp_dev + np.arange(spare))[None]
    where = 2 * quad_bins.T + (group_rows - 2 * comp_dev) * (quad_bins.T // comp_dev)
    fill = jnp.asarray(np.repeat(own_rows[:, :, None], 4, axis=2).astype(np.int32))
    where = jnp.concatenate([where.reshape(groups, comp_dev, 4), fill], axis=1).reshape(-1)
    pad = lambda v: jnp.pad(v.reshape(groups, comp_dev), ((0, 0), (0, spare))).reshape(-1)
    strength, kept = pad(time_step * coupling), pad(1.0 + time_step * growth)

    moved = []
    for i, (start, size) in enumerate(zip(starts, CHUNKS)):
        moved = [
            pl.pallas_call(
                functools.partial(propagate_kernel, start),
                in_specs=[smem, smem] + [vmem] * (3 + len(moved)),
                out_specs=vmem,
                out_shape=jax.ShapeDtypeStruct((groups, rows_of(start + size), 128), jnp.float32),
                compiler_params=params,
                cost_estimate=pl.CostEstimate(flops=COST * size, bytes_accessed=16384 * size, transcendentals=0),
                name=f"propagate_{i}",
            )(place, table, owns[i], *halos[i], *moved)
        ]
    energy = lax.all_to_all(
        moved[0], ("comp", "tile"), split_axis=0, concat_axis=0, tiled=True, axis_index_groups=windows
    )

    total_rows = groups * group_rows
    fresh = pl.pallas_call(
        settle_kernel,
        in_specs=[smem, smem, smem, vmem],
        out_specs=vmem,
        out_shape=jax.ShapeDtypeStruct((total_rows, 128), jnp.float32),
        scratch_shapes=[pltpu.VMEM((total_rows, 128), jnp.float32)] * 4,
        compiler_params=params,
        name="settle",
    )(where, strength, kept, energy.reshape(total_rows, 128))

    back = lax.all_to_all(fresh.reshape(groups, group_rows, 128), "comp", split_axis=0, concat_axis=0, tiled=True)
    return pl.pallas_call(
        unpack_kernel,
        in_specs=[vmem],
        out_specs=vmem,
        out_shape=jax.ShapeDtypeStruct((comp_dev, width, height), jnp.float32),
        compiler_params=params,
        name="unpack",
    )(back)


def solution(mesh):
    return jax.shard_map(
        per_device,
        mesh=mesh,
        in_specs=(P("comp", "tile", None), P("tile", None), P(), P(), P()),
        out_specs=P("comp", "tile", None),
        check_vma=False,
    )
```

time: 97.6 us -> 102 us (1.045)
  the two profiles are of different devices: /device:TPU:7 before, /device:TPU:1 now
where the time goes in v5:
time: 102 us; the launch traced here: 101 us
  starting transfers between devices  29.2 us (29%)
  blocking collectives  24.7 us (24%)
  waiting for transfers between devices  22.7 us (22%)
  Pallas kernels  17.6 us (17%)
  local copies, waits for them, and re-layouts  4.07 us (4%)
  other arithmetic  2.54 us (2%)
    all_to_all x1, blocking collectives, per_device(): lax.all_to_all(fresh.reshape(groups, group_rows, 128), 'comp', split_axis...  24.7 us
    ppermute x2, starting transfers between devices, per_device(): lax.ppermute(jnp.where(odd, start, end), ('comp', 'tile'), halo_pairs(gro...  20.8 us
    all_to_all x1, waiting for transfers between devices, per_device(): lax.all_to_all(moved[0], ('comp', 'tile'), split_axis=0, concat_axis=0, t...  17.9 us
    pallas_call x1, Pallas kernels, per_device(): pl.pallas_call(settle_kernel, in_specs=[smem, smem, smem, vmem], out_spec...  9.93 us
    pallas_call x2, Pallas kernels, per_device(): pl.pallas_call(functools.partial(propagate_kernel, start), in_specs=[smem...  6.07 us
    ppermute x2, waiting for transfers between devices, per_device(): lax.ppermute(jnp.where(odd, end, start), ('comp', 'tile'), halo_pairs(gro...  4.84 us
    all_to_all x1, starting transfers between devices, per_device(): lax.all_to_all(moved[0], ('comp', 'tile'), split_axis=0, concat_axis=0, t...  4.53 us
    ppermute x2, starting transfers between devices, per_device(): lax.ppermute(jnp.where(odd, end, start), ('comp', 'tile'), halo_pairs(gro...  3.84 us
  transfers between devices with their start and end apart: 5, of which 2 were waited for; matrix products, arithmetic and copies ran while one was open for 4% of the time, Pallas kernels for 3%

profile of v5, /device:TPU:1, one launch (start us, length us, event | category | flops | bytes accessed | tf_op | source)
XLA Modules:
  0.0 101.1 jit_solution(17171478088290486712)
XLA Ops:
  0.0 0.7 convert_bitcast_fusion
  0.7 1.2 %slice.21 = f32[96,4,512]{2,1,0:T(4,128)S(1)} slice(f32[162,4,512]{2,1,0:T(4,128)} %param.7), slice={[0:96], [0:4], [0:512]} | slice | bytes 1572864 | tf_op jit(solution)/shard_map/slice | solution.py:204
  1.9 0.3 broadcast_select_fusion
  2.2 14.1 %collective-permute-start.2 = (f32[97,2,512]{2,1,0:T(2,128)S(1)}, f32[97,2,512]{2,1,0:T(2,128)S(1)}, u32[]{:S(2)}, u32[]{:S(2)}) collective-permute-start(f32[97,2,512]{2,1,0:T(2,128)S(1)} %get-tuple-element.6), channel_id=1, source_target_pairs={{0,1},{1,2},{2,3},{3,4},{4,5},{5,6},{6,7},{7,8},{8,9},{9,10},{10,1... | collective-permute-start | bytes 1191944 | tf_op jit(solution)/shard_map/ppermute | solution.py:210
  16.4 1.9 %collective-permute-start.3 = (f32[97,2,512]{2,1,0:T(2,128)S(1)}, f32[97,2,512]{2,1,0:T(2,128)S(1)}, u32[]{:S(2)}, u32[]{:S(2)}) collective-permute-start(f32[97,2,512]{2,1,0:T(2,128)S(1)} %get-tuple-element.5), channel_id=1, source_target_pairs={{0,63},{1,0},{2,1},{3,2},{4,3},{5,4},{6,5},{7,6},{8,7},{9,8},{10,9... | collective-permute-start | bytes 1191944 | tf_op jit(solution)/shard_map/ppermute | solution.py:211
  18.3 1.1 %slice.18 = f32[66,4,512]{2,1,0:T(4,128)S(1)} slice(f32[162,4,512]{2,1,0:T(4,128)} %param.7), slice={[96:162], [0:4], [0:512]} | slice | bytes 1081344 | tf_op jit(solution)/shard_map/slice | solution.py:204
  19.4 1.0 %broadcast_select_fusion.2 = (f32[67,2,512]{2,1,0:T(2,128)}, f32[67,2,512]{2,1,0:T(2,128)}) fusion(pred[]{:T(512)S(6)} %eq.14, f32[1,4,512]{2,1,0:T(4,128)S(1)} %convert_bitcast_fusion, f32[66,4,512]{2,1,0:T(4,128)S(1)} %slice.18), kind=kLoop, calls=%fused_computation.16 | loop fusion | flops 411648 | bytes 1097729 | tf_op jit(solution)/shard_map/jit(_where)/select_n | solution.py:211
  20.4 6.7 %collective-permute-start = (f32[67,2,512]{2,1,0:T(2,128)}, f32[67,2,512]{2,1,0:T(2,128)S(1)}, u32[]{:S(2)}, u32[]{:S(2)}) collective-permute-start(f32[67,2,512]{2,1,0:T(2,128)} %get-tuple-element.8), channel_id=1, source_target_pairs={{0,1},{1,2},{2,3},{3,4},{4,5},{5,6},{6,7},{7,8},{8,9},{9,10},{10,1... | collective-permute-start | bytes 823304 | tf_op jit(solution)/shard_map/ppermute | solution.py:210
  27.1 1.9 %collective-permute-start.1 = (f32[67,2,512]{2,1,0:T(2,128)}, f32[67,2,512]{2,1,0:T(2,128)S(1)}, u32[]{:S(2)}, u32[]{:S(2)}) collective-permute-start(f32[67,2,512]{2,1,0:T(2,128)} %get-tuple-element.7), channel_id=1, source_target_pairs={{0,63},{1,0},{2,1},{3,2},{4,3},{5,4},{6,5},{7,6},{8,7},{9,8},{10,9... | collective-permute-start | bytes 823304 | tf_op jit(solution)/shard_map/ppermute | solution.py:211
  29.0 0.1 pad_add_fusion.1.place_ref
  29.1 0.8 dynamic_slice.3.coef_ref
  29.9 0.1 pad_maximum_fusion.1.own_ref
  30.0 0.2 pad_maximum_fusion.own_ref
  30.2 0.0 collective-permute-done.2.one_ref
  30.2 0.0 collective-permute-done.3.other_ref
  30.2 2.8 %propagate_0.1.refs_0_ = f32[8,192,128]{2,1,0:T(8,128)S(1)} custom-call(s32[4]{0:T(128)S(1)} %pad_add_fusion.1.place_ref, f32[486]{0:T(512)S(1)} %dynamic_slice.3.coef_ref, f32[97,4,512]{2,1,0:T(4,128)S(1)} %pad_maximum_fusion.own_ref, f32[97,2,512]{2,1,0:T(2,128)S(1)} %collective-permute-done.2.one_ref, f32[97,2,512]{2,1,0:T(2,128)S(1)} %collective-permute-done.3.other_ref), custom_call_target="tpu_custom_call" | custom-call | flops 19200000 | bytes 1572864 | tf_op jit(solution)/shard_map/propagate_0/pallas_call | solution.py:226
  33.0 0.0 collective-permute-done.one_ref
  33.0 4.8 %collective-permute-done.1.other_ref = f32[67,2,512]{2,1,0:T(2,128)S(1)} collective-permute-done((f32[67,2,512]{2,1,0:T(2,128)}, f32[67,2,512]{2,1,0:T(2,128)S(1)}, u32[]{:S(2)}, u32[]{:S(2)}) %collective-permute-start.1) | collective-permute-done | bytes 274464 | tf_op jit(solution)/shard_map/ppermute | solution.py:211
  37.9 3.3 %propagate_1.1 = f32[8,328,128]{2,1,0:T(8,128)} custom-call(s32[4]{0:T(128)S(1)} %pad_add_fusion.1.place_ref, f32[486]{0:T(512)S(1)} %dynamic_slice.3.coef_ref, f32[67,4,512]{2,1,0:T(4,128)S(1)} %pad_maximum_fusion.1.own_ref, f32[67,2,512]{2,1,0:T(2,128)S(1)} %collective-permute-done.one_ref, f32[67,2,512]{2,1,0:T(2,128)S(1)} %collective-permute-done.1.other_ref, ...), custom_call_target="tpu_custom_call" | custom-call | flops 13200000 | bytes 1081344 | tf_op jit(solution)/shard_map/propagate_1/pallas_call | solution.py:226
  41.1 0.0 copy-start
  41.1 0.0 copy-start.1
  41.1 4.5 %all-to-all-start = ((f32[8,328,128]{2,1,0:T(8,128)}), f32[8,328,128]{2,1,0:T(8,128)S(1)}, u32[]{:S(2)}, u32[]{:S(2)}) async-start(f32[8,328,128]{2,1,0:T(8,128)} %propagate_1.1), calls=%async_computation | async-start | bytes 2686976 | tf_op jit(solution)/shard_map/all_to_all | solution.py:236
  45.7 0.0 copy-done
  45.7 0.0 copy-start.2
  45.7 0.0 copy-start.3
  45.7 0.1 reshape.24
  45.8 0.0 copy-done.1
  45.8 0.1 pad_add_fusion
  45.9 0.3 copy.9
  46.2 0.3 reshape.25.bins_ref
  46.5 0.0 copy-done.2
  46.5 0.1 reshape.26
  46.6 0.1 reshape.27.strength_ref
  46.7 0.0 copy-done.3
  46.8 0.1 reshape.28
  46.9 0.1 reshape.29.kept_ref
  46.9 17.9 %all-to-all-done = f32[8,328,128]{2,1,0:T(8,128)S(1)} async-done(((f32[8,328,128]{2,1,0:T(8,128)}), f32[8,328,128]{2,1,0:T(8,128)S(1)}, u32[]{:S(2)}, u32[]{:S(2)}) %all-to-all-start) | async-done | bytes 1343520 | tf_op jit(solution)/shard_map/all_to_all | solution.py:236
  64.8 9.9 %settle.1 = f32[2624,128]{1,0:T(8,128)S(1)} custom-call(s32[5248]{0:T(1024)S(1)} %reshape.25.bins_ref, f32[1312]{0:T(1024)S(1)} %reshape.27.strength_ref, f32[1312]{0:T(1024)S(1)} %reshape.29.kept_ref, f32[2624,128]{1,0:T(8,128)S(1)} %bitcast.16), custom_call_target="tpu_custom_call" | custom-call | tf_op jit(solution)/shard_map/settle/pallas_call | solution.py:241
  74.8 24.7 %all_to_all.10.in_ref = f32[8,328,128]{2,1,0:T(8,128)S(1)} all-to-all(f32[8,328,128]{2,1,0:T(8,128)S(1)} %bitcast.17), channel_id=1, replica_groups=mesh['comp'=8,'tile'=64] {'comp'}, dimensions={0} | all-to-all | bytes 2686976 | tf_op jit(solution)/shard_map/all_to_all | solution.py:251
  99.5 1.6 %unpack.1 = f32[162,4,512]{2,1,0:T(4,128)} custom-call(f32[8,328,128]{2,1,0:T(8,128)S(1)} %all_to_all.10.in_ref), custom_call_target="tpu_custom_call" | custom-call | tf_op jit(solution)/shard_map/unpack/pallas_call | solution.py:252
  (5 shorter events, 0.1 us)
Async XLA Ops:
  2.2 28.0 %collective-permute-start.2 = (f32[97,2,512]{2,1,0:T(2,128)S(1)}, f32[97,2,512]{2,1,0:T(2,128)S(1)}, u32[]{:S(2)}, u32[]{:S(2)}) collective-permute-start(f32[97,2,512]{2,1,0:T(2,128)S(1)} %get-tuple-element.6), channel_id=1, source_target_pairs={{0,1},{1,2},{2,3},{3,4},{4,5},{5,6},{6,7},{7,8},{8,9},{9,10},{10,1... | collective-permute-start | bytes 1191944 | tf_op jit(solution)/shard_map/ppermute | solution.py:210
  16.4 13.8 %collective-permute-start.3 = (f32[97,2,512]{2,1,0:T(2,128)S(1)}, f32[97,2,512]{2,1,0:T(2,128)S(1)}, u32[]{:S(2)}, u32[]{:S(2)}) collective-permute-start(f32[97,2,512]{2,1,0:T(2,128)S(1)} %get-tuple-element.5), channel_id=1, source_target_pairs={{0,63},{1,0},{2,1},{3,2},{4,3},{5,4},{6,5},{7,6},{8,7},{9,8},{10,9... | collective-permute-start | bytes 1191944 | tf_op jit(solution)/shard_map/ppermute | solution.py:211
  20.4 12.6 %collective-permute-start = (f32[67,2,512]{2,1,0:T(2,128)}, f32[67,2,512]{2,1,0:T(2,128)S(1)}, u32[]{:S(2)}, u32[]{:S(2)}) collective-permute-start(f32[67,2,512]{2,1,0:T(2,128)} %get-tuple-element.8), channel_id=1, source_target_pairs={{0,1},{1,2},{2,3},{3,4},{4,5},{5,6},{6,7},{7,8},{8,9},{9,10},{10,1... | collective-permute-start | bytes 823304 | tf_op jit(solution)/shard_map/ppermute | solution.py:210
  27.1 10.8 %collective-permute-start.1 = (f32[67,2,512]{2,1,0:T(2,128)}, f32[67,2,512]{2,1,0:T(2,128)S(1)}, u32[]{:S(2)}, u32[]{:S(2)}) collective-permute-start(f32[67,2,512]{2,1,0:T(2,128)} %get-tuple-element.7), channel_id=1, source_target_pairs={{0,63},{1,0},{2,1},{3,2},{4,3},{5,4},{6,5},{7,6},{8,7},{9,8},{10,9... | collective-permute-start | bytes 823304 | tf_op jit(solution)/shard_map/ppermute | solution.py:211
  41.1 4.5 %copy-start = (s32[4,1296]{1,0:T(4,128)S(1)}, s32[4,1296]{1,0:T(4,128)}, u32[]{:S(2)}) copy-start(s32[4,1296]{1,0:T(4,128)} %param.9) | copy-start | bytes 62212
  41.1 4.7 %copy-start.1 = (s32[8,2,4]{1,0,2:T(8,128)S(1)}, s32[8,2,4]{1,0,2:T(8,128)}, u32[]{:S(2)}) copy-start(s32[8,2,4]{1,0,2:T(8,128)} %constant.70.clone) | copy-start | bytes 772
  41.1 23.7 %all-to-all-start = ((f32[8,328,128]{2,1,0:T(8,128)}), f32[8,328,128]{2,1,0:T(8,128)S(1)}, u32[]{:S(2)}, u32[]{:S(2)}) async-start(f32[8,328,128]{2,1,0:T(8,128)} %propagate_1.1), calls=%async_computation | async-start | bytes 2686976 | tf_op jit(solution)/shard_map/all_to_all | solution.py:236
  45.7 0.8 copy-start.2
  45.7 1.1 %copy-start.3 = (f32[1296]{0:T(1024)S(1)}, f32[1296]{0:T(1024)}, u32[]{:S(2)}) copy-start(f32[1296]{0:T(1024)} %param.11) | copy-start | bytes 15556

commit v6 on v5

--- a/solution.py
+++ b/solution.py
@@ -19,7 +19,7 @@
 time_step = 0.5
 
 ROW_TILES = 4
-CHUNKS = (96, 66)
+CHUNKS = (162,)
 TOGETHER = 28
 VMEM_LIMIT = 40 << 20
 COST = 200_000

time: 102 us -> 101 us (level)
  starting transfers between devices: 29.2 us -> 20.6 us
  waiting for transfers between devices: 22.7 us -> 31.1 us
  other arithmetic: 2.54 us -> 5.56 us
  local copies, waits for them, and re-layouts: 4.07 us -> 1.82 us
    ppermute x2 -> x1, waiting for transfers between devices: 0.01 us -> 9.08 us  [per_device(): lax.ppermute(jnp.where(odd, start, end), ('comp', 'tile'), halo_pairs(gro...]
    ppermute x2 -> x1, starting transfers between devices: 20.8 us -> 14.1 us  [per_device(): lax.ppermute(jnp.where(odd, start, end), ('comp', 'tile'), halo_pairs(gro...]
    select_n x2 -> x1, other arithmetic: 1.35 us -> 4.38 us  [per_device(): jnp.where(odd, end, start)]
    slice x2 -> x0, local copies, waits for them, and re-layouts: 2.27 us -> none  [per_device(): lax.slice_in_dim(spectrum, s, s + n, axis=0)]
    ppermute x2 -> x1, starting transfers between devices: 3.84 us -> 1.92 us  [per_device(): lax.ppermute(jnp.where(odd, end, start), ('comp', 'tile'), halo_pairs(gro...]
    ppermute x2 -> x1, waiting for transfers between devices: 4.84 us -> 4.13 us  [per_device(): lax.ppermute(jnp.where(odd, end, start), ('comp', 'tile'), halo_pairs(gro...]
    pallas_call x2 -> x1, Pallas kernels: 6.07 us -> 5.37 us  [per_device(): pl.pallas_call(functools.partial(propagate_kernel, start), in_specs=[smem...]
  transfers between devices with their start and end apart: 5 -> 3, of which waited for: 2 -> 3; matrix products, arithmetic and copies ran while one was open for 4% -> 2% of each run, Pallas kernels for 3% -> 0%
where the time goes in v6:
time: 101 us
  waiting for transfers between devices  31.1 us (31%)
  blocking collectives  24.7 us (24%)
  starting transfers between devices  20.6 us (20%)
  Pallas kernels  16.9 us (17%)
  other arithmetic  5.56 us (6%)
  local copies, waits for them, and re-layouts  1.82 us (2%)
    all_to_all x1, blocking collectives, per_device(): lax.all_to_all(fresh.reshape(groups, group_rows, 128), 'comp', split_axis...  24.7 us
    all_to_all x1, waiting for transfers between devices, per_device(): lax.all_to_all(moved[0], ('comp', 'tile'), split_axis=0, concat_axis=0, t...  17.9 us
    ppermute x1, starting transfers between devices, per_device(): lax.ppermute(jnp.where(odd, start, end), ('comp', 'tile'), halo_pairs(gro...  14.1 us
    pallas_call x1, Pallas kernels, per_device(): pl.pallas_call(settle_kernel, in_specs=[smem, smem, smem, vmem], out_spec...  9.93 us
    ppermute x1, waiting for transfers between devices, per_device(): lax.ppermute(jnp.where(odd, start, end), ('comp', 'tile'), halo_pairs(gro...  9.08 us
    pallas_call x1, Pallas kernels, per_device(): pl.pallas_call(functools.partial(propagate_kernel, start), in_specs=[smem...  5.37 us
    all_to_all x1, starting transfers between devices, per_device(): lax.all_to_all(moved[0], ('comp', 'tile'), split_axis=0, concat_axis=0, t...  4.53 us
    select_n x1, other arithmetic, per_device(): jnp.where(odd, end, start)  4.38 us
  transfers between devices with their start and end apart: 3, of which 3 were waited for; matrix products, arithmetic and copies ran while one was open for 2% of the time, Pallas kernels for 0%

profile of v6, /device:TPU:1, one launch (start us, length us, event | category | flops | bytes accessed | tf_op | source)
XLA Modules:
  0.0 100.8 jit_solution(7372436182971400129)
XLA Ops:
  0.0 0.7 convert_bitcast_fusion
  0.7 0.0 copy-start
  0.7 4.4 %broadcast_select_fusion = (f32[163,2,512]{2,1,0:T(2,128)S(1)}, f32[163,2,512]{2,1,0:T(2,128)}) fusion(pred[]{:T(512)S(6)} %eq.14, f32[1,4,512]{2,1,0:T(4,128)S(1)} %convert_bitcast_fusion, f32[162,4,512]{2,1,0:T(4,128)} %param.7), kind=kLoop, calls=%fused_computation.7 | loop fusion | flops 1001472 | bytes 2670593 | tf_op jit(solution)/shard_map/jit(_where)/select_n | solution.py:211
  5.1 14.1 %collective-permute-start = (f32[163,2,512]{2,1,0:T(2,128)}, f32[163,2,512]{2,1,0:T(2,128)S(1)}, u32[]{:S(2)}, u32[]{:S(2)}) collective-permute-start(f32[163,2,512]{2,1,0:T(2,128)} %get-tuple-element.6), channel_id=1, source_target_pairs={{0,1},{1,2},{2,3},{3,4},{4,5},{5,6},{6,7},{7,8},{8,9},{9,10},{10,1... | collective-permute-start | bytes 2002952 | tf_op jit(solution)/shard_map/ppermute | solution.py:210
  19.2 1.9 %collective-permute-start.1 = (f32[163,2,512]{2,1,0:T(2,128)S(1)}, f32[163,2,512]{2,1,0:T(2,128)S(1)}, u32[]{:S(2)}, u32[]{:S(2)}) collective-permute-start(f32[163,2,512]{2,1,0:T(2,128)S(1)} %get-tuple-element.5), channel_id=1, source_target_pairs={{0,63},{1,0},{2,1},{3,2},{4,3},{5,4},{6,5},{7,6},{8,7},{9,8},{10,9... | collective-permute-start | bytes 2002952 | tf_op jit(solution)/shard_map/ppermute | solution.py:211
  21.2 0.8 dynamic_slice.3.coef_ref
  22.0 0.1 pad_add_fusion.1.place_ref
  22.0 0.0 copy-done
  22.0 0.3 pad_maximum_fusion.own_ref
  22.3 9.1 %collective-permute-done.one_ref = f32[163,2,512]{2,1,0:T(2,128)S(1)} collective-permute-done((f32[163,2,512]{2,1,0:T(2,128)}, f32[163,2,512]{2,1,0:T(2,128)S(1)}, u32[]{:S(2)}, u32[]{:S(2)}) %collective-permute-start) | collective-permute-done | bytes 667680 | tf_op jit(solution)/shard_map/ppermute | solution.py:210
  31.4 4.1 %collective-permute-done.1.other_ref = f32[163,2,512]{2,1,0:T(2,128)S(1)} collective-permute-done((f32[163,2,512]{2,1,0:T(2,128)S(1)}, f32[163,2,512]{2,1,0:T(2,128)S(1)}, u32[]{:S(2)}, u32[]{:S(2)}) %collective-permute-start.1) | collective-permute-done | bytes 667680 | tf_op jit(solution)/shard_map/ppermute | solution.py:211
  35.5 5.4 %propagate_0.1 = f32[8,328,128]{2,1,0:T(8,128)} custom-call(s32[4]{0:T(128)S(1)} %pad_add_fusion.1.place_ref, f32[486]{0:T(512)S(1)} %dynamic_slice.3.coef_ref, f32[163,4,512]{2,1,0:T(4,128)S(1)} %pad_maximum_fusion.own_ref, f32[163,2,512]{2,1,0:T(2,128)S(1)} %collective-permute-done.one_ref, f32[163,2,512]{2,1,0:T(2,128)S(1)} %collective-permute-done.1.other_ref), custom_call_target="tpu_custom_call" | custom-call | flops 32400000 | bytes 2654208 | tf_op jit(solution)/shard_map/propagate_0/pallas_call | solution.py:226
  40.9 0.0 copy-start.1
  40.9 0.0 copy-start.2
  40.9 4.5 %all-to-all-start = ((f32[8,328,128]{2,1,0:T(8,128)}), f32[8,328,128]{2,1,0:T(8,128)S(1)}, u32[]{:S(2)}, u32[]{:S(2)}) async-start(f32[8,328,128]{2,1,0:T(8,128)} %propagate_0.1), calls=%async_computation | async-start | bytes 2686976 | tf_op jit(solution)/shard_map/all_to_all | solution.py:236
  45.4 0.0 copy-done.1
  45.4 0.0 copy-start.3
  45.4 0.0 copy-start.4
  45.5 0.1 reshape.24
  45.6 0.0 copy-done.2
  45.6 0.1 pad_add_fusion
  45.7 0.3 copy.9
  46.0 0.3 reshape.25.bins_ref
  46.3 0.0 copy-done.3
  46.3 0.1 reshape.26
  46.4 0.1 reshape.27.strength_ref
  46.5 0.0 copy-done.4
  46.5 0.1 reshape.28
  46.6 0.1 reshape.29.kept_ref
  46.7 17.9 %all-to-all-done = f32[8,328,128]{2,1,0:T(8,128)S(1)} async-done(((f32[8,328,128]{2,1,0:T(8,128)}), f32[8,328,128]{2,1,0:T(8,128)S(1)}, u32[]{:S(2)}, u32[]{:S(2)}) %all-to-all-start) | async-done | bytes 1343520 | tf_op jit(solution)/shard_map/all_to_all | solution.py:236
  64.6 9.9 %settle.1 = f32[2624,128]{1,0:T(8,128)S(1)} custom-call(s32[5248]{0:T(1024)S(1)} %reshape.25.bins_ref, f32[1312]{0:T(1024)S(1)} %reshape.27.strength_ref, f32[1312]{0:T(1024)S(1)} %reshape.29.kept_ref, f32[2624,128]{1,0:T(8,128)S(1)} %bitcast.16), custom_call_target="tpu_custom_call" | custom-call | tf_op jit(solution)/shard_map/settle/pallas_call | solution.py:241
  74.5 24.7 %all_to_all.10.in_ref = f32[8,328,128]{2,1,0:T(8,128)S(1)} all-to-all(f32[8,328,128]{2,1,0:T(8,128)S(1)} %bitcast.17), channel_id=1, replica_groups=mesh['comp'=8,'tile'=64] {'comp'}, dimensions={0} | all-to-all | bytes 2686976 | tf_op jit(solution)/shard_map/all_to_all | solution.py:251
  99.3 1.6 %unpack.1 = f32[162,4,512]{2,1,0:T(4,128)} custom-call(f32[8,328,128]{2,1,0:T(8,128)S(1)} %all_to_all.10.in_ref), custom_call_target="tpu_custom_call" | custom-call | tf_op jit(solution)/shard_map/unpack/pallas_call | solution.py:252
  (5 shorter events, 0.1 us)
Async XLA Ops:
  0.7 21.3 %copy-start = (f32[162,4,512]{2,1,0:T(4,128)S(1)}, f32[162,4,512]{2,1,0:T(4,128)}, u32[]{:S(2)}) copy-start(f32[162,4,512]{2,1,0:T(4,128)} %param.7) | copy-start | bytes 3981316
  5.1 26.3 %collective-permute-start = (f32[163,2,512]{2,1,0:T(2,128)}, f32[163,2,512]{2,1,0:T(2,128)S(1)}, u32[]{:S(2)}, u32[]{:S(2)}) collective-permute-start(f32[163,2,512]{2,1,0:T(2,128)} %get-tuple-element.6), channel_id=1, source_target_pairs={{0,1},{1,2},{2,3},{3,4},{4,5},{5,6},{6,7},{7,8},{8,9},{9,10},{10,1... | collective-permute-start | bytes 2002952 | tf_op jit(solution)/shard_map/ppermute | solution.py:210
  19.2 16.3 %collective-permute-start.1 = (f32[163,2,512]{2,1,0:T(2,128)S(1)}, f32[163,2,512]{2,1,0:T(2,128)S(1)}, u32[]{:S(2)}, u32[]{:S(2)}) collective-permute-start(f32[163,2,512]{2,1,0:T(2,128)S(1)} %get-tuple-element.5), channel_id=1, source_target_pairs={{0,63},{1,0},{2,1},{3,2},{4,3},{5,4},{6,5},{7,6},{8,7},{9,8},{10,9... | collective-permute-start | bytes 2002952 | tf_op jit(solution)/shard_map/ppermute | solution.py:211
  40.9 4.5 %copy-start.1 = (s32[4,1296]{1,0:T(4,128)S(1)}, s32[4,1296]{1,0:T(4,128)}, u32[]{:S(2)}) copy-start(s32[4,1296]{1,0:T(4,128)} %param.9) | copy-start | bytes 62212
  40.9 4.7 %copy-start.2 = (s32[8,2,4]{1,0,2:T(8,128)S(1)}, s32[8,2,4]{1,0,2:T(8,128)}, u32[]{:S(2)}) copy-start(s32[8,2,4]{1,0,2:T(8,128)} %constant.70.clone) | copy-start | bytes 772
  40.9 23.7 %all-to-all-start = ((f32[8,328,128]{2,1,0:T(8,128)}), f32[8,328,128]{2,1,0:T(8,128)S(1)}, u32[]{:S(2)}, u32[]{:S(2)}) async-start(f32[8,328,128]{2,1,0:T(8,128)} %propagate_0.1), calls=%async_computation | async-start | bytes 2686976 | tf_op jit(solution)/shard_map/all_to_all | solution.py:236
  45.4 0.8 copy-start.3
  45.4 1.1 %copy-start.4 = (f32[1296]{0:T(1024)S(1)}, f32[1296]{0:T(1024)}, u32[]{:S(2)}) copy-start(f32[1296]{0:T(1024)} %param.11) | copy-start | bytes 15556

commit v7 on v4

--- a/solution.py
+++ b/solution.py
@@ -19,7 +19,8 @@
 time_step = 0.5
 
 ROW_TILES = 4
-CHUNKS = (96, 66)
+SENDS = ((60, 36), (66,))
+CHUNKS = tuple(sum(sizes) for sizes in SENDS)
 TOGETHER = 28
 VMEM_LIMIT = 40 << 20
 
@@ -54,15 +55,18 @@
     return pl.ds(pl.multiple_of(row, 2), 2)
 
 
-def propagate_kernel(first, quarter_ref, coef_ref, own_ref, halo_ref, out_ref):
+def propagate_kernel(first, done, quarter_ref, coef_ref, own_ref, halo_ref, *refs):
+    *before_refs, out_ref = refs
     size = own_ref.shape[0] - 1
     side_by_side = max(n for n in range(1, TOGETHER + 1) if size % n == 0)
     quarter = quarter_ref[0]
     lane = lax.broadcasted_iota(jnp.int32, (8, 128), 1)
-    extra = out_ref.shape[1] - 2 * size
-    if extra:
-        for piece in range(out_ref.shape[0]):
-            out_ref[piece, 2 * size :, :] = jnp.zeros((extra, 128), jnp.float32)
+    extra = out_ref.shape[1] - 2 * (done + size)
+    for piece in range(out_ref.shape[0]):
+        for ref in before_refs:
+            out_ref[piece, : 2 * done, :] = ref[piece]
+        if extra:
+            out_ref[piece, 2 * (done + size) :, :] = jnp.zeros((extra, 128), jnp.float32)
 
     def run(east, north):
         def rows(own, halo):
@@ -94,7 +98,7 @@
                 for i, v in enumerate(fields[u]):
                     for pair in range(2):
                         at = base + 2 * pair
-                        out_ref[pair * ROW_TILES + i, pair_of(2 * k), :] = v[at : at + 2, :]
+                        out_ref[pair * ROW_TILES + i, pair_of(2 * (done + k)), :] = v[at : at + 2, :]
             return carry
 
         lax.fori_loop(0, size // side_by_side, several, 0)
@@ -183,10 +187,11 @@
     vmem = pl.BlockSpec(memory_space=pltpu.VMEM)
     params = pltpu.CompilerParams(vmem_limit_bytes=VMEM_LIMIT)
 
-    starts = [sum(CHUNKS[:i]) for i in range(len(CHUNKS))]
+    sizes = sum(SENDS, ())
+    starts = [sum(sizes[:i]) for i in range(len(sizes))]
     mask = sea_mask.astype(jnp.float32)[None]
     owns = [
-        jnp.concatenate([lax.slice_in_dim(spectrum, s, s + n, axis=0), mask], axis=0) for s, n in zip(starts, CHUNKS)
+        jnp.concatenate([lax.slice_in_dim(spectrum, s, s + n, axis=0), mask], axis=0) for s, n in zip(starts, sizes)
     ]
     halos = [lax.ppermute(own, ("comp", "tile"), pairs) for own in owns]
 
@@ -200,17 +205,26 @@
     strength, kept = pad(time_step * coupling), pad(1.0 + time_step * growth)
 
     pieces = []
-    for i, (start, size) in enumerate(zip(starts, CHUNKS)):
-        moved = pl.pallas_call(
-            functools.partial(propagate_kernel, start),
-            in_specs=[smem, smem, vmem, vmem],
-            out_specs=vmem,
-            out_shape=jax.ShapeDtypeStruct((groups, rows_of(size), 128), jnp.float32),
-            compiler_params=params,
-            cost_estimate=pl.CostEstimate(flops=100 * size * 2048, bytes_accessed=12 * size * 2048, transcendentals=0),
-            name=f"propagate_{i}",
-        )(quarter, table, owns[i], halos[i])
-        pieces.append(lax.all_to_all(moved, "comp", split_axis=0, concat_axis=0, tiled=True))
+    i = 0
+    for together in SENDS:
+        moved, done = [], 0
+        for size in together:
+            moved = [
+                pl.pallas_call(
+                    functools.partial(propagate_kernel, starts[i], done),
+                    in_specs=[smem, smem] + [vmem] * (2 + len(moved)),
+                    out_specs=vmem,
+                    out_shape=jax.ShapeDtypeStruct((groups, rows_of(done + size), 128), jnp.float32),
+                    compiler_params=params,
+                    cost_estimate=pl.CostEstimate(
+                        flops=200_000 * size, bytes_accessed=24_000 * size, transcendentals=0
+                    ),
+                    name=f"propagate_{i}",
+                )(quarter, table, owns[i], halos[i], *moved)
+            ]
+            done += size
+            i += 1
+        pieces.append(lax.all_to_all(moved[0], "comp", split_axis=0, concat_axis=0, tiled=True))
 
     total_rows = groups * group_rows
     fresh = pl.pallas_call(

time: 97.6 us -> 101 us (1.035)
  waiting for transfers between devices: 34.4 us -> 36.3 us
    ppermute x2 -> x3, starting transfers between devices: 7.22 us -> 9.01 us  [per_device(): halos = [lax.ppermute(own, ('comp', 'tile'), pairs) for own in owns]]
    ppermute x2 -> x3, waiting for transfers between devices: 23.4 us -> 25 us  [per_device(): halos = [lax.ppermute(own, ('comp', 'tile'), pairs) for own in owns]]
    pallas_call x2 -> x3, Pallas kernels: 6.21 us -> 6.87 us  [per_device(): pl.pallas_call(functools.partial(propagate_kernel, starts[i], done), in_s...]
  transfers between devices with their start and end apart: 4 -> 5, of which waited for: 3 -> 3; matrix products, arithmetic and copies ran while one was open for 2% -> 2% of each run, Pallas kernels for 6% -> 7%
where the time goes in v7:
time: 101 us
  waiting for transfers between devices  36.3 us (36%)
  blocking collectives  22 us (22%)
  starting transfers between devices  20.2 us (20%)
  Pallas kernels  18.7 us (19%)
  local copies, waits for them, and re-layouts  2.13 us (2%)
  other arithmetic  1.18 us (1%)
    ppermute x3, waiting for transfers between devices, per_device(): halos = [lax.ppermute(own, ('comp', 'tile'), pairs) for own in owns]  25 us
    all_to_all x1, blocking collectives, per_device(): lax.all_to_all(fresh.reshape(groups, group_rows, 128), 'comp', split_axis...  22 us
    all_to_all x2, waiting for transfers between devices, per_device(): lax.all_to_all(moved[0], 'comp', split_axis=0, concat_axis=0, tiled=True)  11.3 us
    all_to_all x2, starting transfers between devices, per_device(): lax.all_to_all(moved[0], 'comp', split_axis=0, concat_axis=0, tiled=True)  11.2 us
    pallas_call x1, Pallas kernels, per_device(): pl.pallas_call(settle_kernel, in_specs=[smem, smem, smem] + [vmem] * len(...  10.2 us
    ppermute x3, starting transfers between devices, per_device(): halos = [lax.ppermute(own, ('comp', 'tile'), pairs) for own in owns]  9.01 us
    pallas_call x3, Pallas kernels, per_device(): pl.pallas_call(functools.partial(propagate_kernel, starts[i], done), in_s...  6.87 us
  transfers between devices with their start and end apart: 5, of which 3 were waited for; matrix products, arithmetic and copies ran while one was open for 2% of the time, Pallas kernels for 7%

profile of v7, /device:TPU:7, one launch (start us, length us, event | category | flops | bytes accessed | tf_op | source)
XLA Modules:
  0.0 100.7 jit_solution(13930902053064887447)
XLA Ops:
  0.0 0.0 slice-start
  0.0 0.8 convert_bitcast_fusion
  0.8 0.0 slice-start.1
  0.8 0.3 slice-done
  1.1 0.1 pad_maximum_fusion.own_ref
  1.2 3.5 %collective-permute-start.2 = (f32[67,4,512]{2,1,0:T(4,128)S(1)}, f32[67,4,512]{2,1,0:T(4,128)S(1)}, u32[]{:S(2)}, u32[]{:S(2)}) collective-permute-start(f32[67,4,512]{2,1,0:T(4,128)S(1)} %pad_maximum_fusion.own_ref), channel_id=1, source_target_pairs={{0,1},{1,2},{2,3},{3,4},{4,5},{5,6},{6,7},{7,8},{8,9},{9,10},{10,1... | collective-permute-start | bytes 1646600 | tf_op jit(solution)/shard_map/ppermute | solution.py:196
  4.7 0.0 slice-done.1
  4.8 0.1 pad_maximum_fusion.1.own_ref
  4.9 3.5 %collective-permute-start.1 = (f32[61,4,512]{2,1,0:T(4,128)S(1)}, f32[61,4,512]{2,1,0:T(4,128)S(1)}, u32[]{:S(2)}, u32[]{:S(2)}) collective-permute-start(f32[61,4,512]{2,1,0:T(4,128)S(1)} %pad_maximum_fusion.1.own_ref), channel_id=1, source_target_pairs={{0,1},{1,2},{2,3},{3,4},{4,5},{5,6},{6,7},{7,8},{8,9},{9,10},{10,1... | collective-permute-start | bytes 1499144 | tf_op jit(solution)/shard_map/ppermute | solution.py:196
  8.4 0.8 dynamic_slice.3.coef_ref
  9.2 15.5 %collective-permute-done.2.halo_ref = f32[67,4,512]{2,1,0:T(4,128)S(1)} collective-permute-done((f32[67,4,512]{2,1,0:T(4,128)S(1)}, f32[67,4,512]{2,1,0:T(4,128)S(1)}, u32[]{:S(2)}, u32[]{:S(2)}) %collective-permute-start.2) | collective-permute-done | bytes 548896 | tf_op jit(solution)/shard_map/ppermute | solution.py:196
  24.7 0.0 slice-start.2
  24.7 2.8 %propagate_2.1 = f32[8,136,128]{2,1,0:T(8,128)} custom-call(s32[1]{0:T(128)} %bitcast.3.quarter_ref, f32[486]{0:T(512)S(1)} %dynamic_slice.3.coef_ref, f32[67,4,512]{2,1,0:T(4,128)S(1)} %pad_maximum_fusion.own_ref, f32[67,4,512]{2,1,0:T(4,128)S(1)} %collective-permute-done.2.halo_ref), custom_call_target="tpu_custom_call" | custom-call | flops 13200000 | bytes 1584000 | tf_op jit(solution)/shard_map/propagate_2/pallas_call | solution.py:213
  27.5 0.0 copy-start.2
  27.5 6.5 %all-to-all-start.1 = ((f32[8,136,128]{2,1,0:T(8,128)}), f32[8,136,128]{2,1,0:T(8,128)S(1)}, u32[]{:S(2)}, u32[]{:S(2)}) async-start(f32[8,136,128]{2,1,0:T(8,128)} %propagate_2.1), calls=%async_computation.1 | async-start | bytes 1114112 | tf_op jit(solution)/shard_map/all_to_all | solution.py:227
  34.0 0.0 slice-done.2
  34.0 0.1 pad_maximum_fusion.2.own_ref
  34.1 1.9 %collective-permute-start = (f32[37,4,512]{2,1,0:T(4,128)S(1)}, f32[37,4,512]{2,1,0:T(4,128)S(1)}, u32[]{:S(2)}, u32[]{:S(2)}) collective-permute-start(f32[37,4,512]{2,1,0:T(4,128)S(1)} %pad_maximum_fusion.2.own_ref), channel_id=1, source_target_pairs={{0,1},{1,2},{2,3},{3,4},{4,5},{5,6},{6,7},{7,8},{8,9},{9,10},{10,1... | collective-permute-start | bytes 909320 | tf_op jit(solution)/shard_map/ppermute | solution.py:196
  36.0 0.0 copy-done.2
  36.0 0.1 reshape.26
  36.1 0.1 reshape.27.strength_ref
  36.2 0.0 collective-permute-done.1.halo_ref
  36.2 1.8 %propagate_0.1.refs_0_ = f32[8,120,128]{2,1,0:T(8,128)S(1)} custom-call(s32[1]{0:T(128)} %bitcast.3.quarter_ref, f32[486]{0:T(512)S(1)} %dynamic_slice.3.coef_ref, f32[61,4,512]{2,1,0:T(4,128)S(1)} %pad_maximum_fusion.1.own_ref, f32[61,4,512]{2,1,0:T(4,128)S(1)} %collective-permute-done.1.halo_ref), custom_call_target="tpu_custom_call" | custom-call | flops 12000000 | bytes 1440000 | tf_op jit(solution)/shard_map/propagate_0/pallas_call | solution.py:213
  38.1 0.0 copy-start.3
  38.1 0.0 copy-start
  38.1 0.0 copy-start.1
  38.1 9.5 %collective-permute-done.halo_ref = f32[37,4,512]{2,1,0:T(4,128)S(1)} collective-permute-done((f32[37,4,512]{2,1,0:T(4,128)S(1)}, f32[37,4,512]{2,1,0:T(4,128)S(1)}, u32[]{:S(2)}, u32[]{:S(2)}) %collective-permute-start) | collective-permute-done | bytes 303136 | tf_op jit(solution)/shard_map/ppermute | solution.py:196
  47.6 2.3 %propagate_1.1 = f32[8,192,128]{2,1,0:T(8,128)} custom-call(s32[1]{0:T(128)} %bitcast.3.quarter_ref, f32[486]{0:T(512)S(1)} %dynamic_slice.3.coef_ref, f32[37,4,512]{2,1,0:T(4,128)S(1)} %pad_maximum_fusion.2.own_ref, f32[37,4,512]{2,1,0:T(4,128)S(1)} %collective-permute-done.halo_ref, f32[8,120,128]{2,1,0:T(8,128)S(1)} %propagate_0.1.refs_0_), custom_call_target="tpu_custom_call" | custom-call | flops 7200000 | bytes 864000 | tf_op jit(solution)/shard_map/propagate_1/pallas_call | solution.py:213
  49.8 0.0 all-to-all-done.1.refs_1_
  49.8 4.7 %all-to-all-start = ((f32[8,192,128]{2,1,0:T(8,128)}), f32[8,192,128]{2,1,0:T(8,128)S(1)}, u32[]{:S(2)}, u32[]{:S(2)}) async-start(f32[8,192,128]{2,1,0:T(8,128)} %propagate_1.1), calls=%async_computation | async-start | bytes 1572864 | tf_op jit(solution)/shard_map/all_to_all | solution.py:227
  54.6 0.0 copy-done.3
  54.6 0.1 reshape.28
  54.7 0.1 reshape.29.kept_ref
  54.8 0.0 copy-done
  54.8 0.1 reshape.24
  54.9 0.0 copy-done.1
  54.9 0.1 pad_add_fusion
  55.0 0.3 copy.9
  55.3 0.3 reshape.25.bins_ref
  55.6 11.2 %all-to-all-done.refs_0_ = f32[8,192,128]{2,1,0:T(8,128)S(1)} async-done(((f32[8,192,128]{2,1,0:T(8,128)}), f32[8,192,128]{2,1,0:T(8,128)S(1)}, u32[]{:S(2)}, u32[]{:S(2)}) %all-to-all-start) | async-done | bytes 786464 | tf_op jit(solution)/shard_map/all_to_all | solution.py:227
  66.9 10.2 %settle.1 = f32[2624,128]{1,0:T(8,128)S(1)} custom-call(s32[5248]{0:T(1024)S(1)} %reshape.25.bins_ref, f32[1312]{0:T(1024)S(1)} %reshape.27.strength_ref, f32[1312]{0:T(1024)S(1)} %reshape.29.kept_ref, f32[8,192,128]{2,1,0:T(8,128)S(1)} %all-to-all-done.refs_0_, f32[8,136,128]{2,1,0:T(8,128)S(1)} %all-to-all-done.1.refs_1_), custom_call_target="tpu_custom_call" | custom-call | tf_op jit(solution)/shard_map/settle/pallas_call | solution.py:230
  77.1 22.0 %all_to_all.15.in_ref = f32[8,328,128]{2,1,0:T(8,128)S(1)} all-to-all(f32[8,328,128]{2,1,0:T(8,128)S(1)} %bitcast.12), channel_id=1, replica_groups=mesh['comp'=8,'tile'=64] {'comp'}, dimensions={0} | all-to-all | bytes 2686976 | tf_op jit(solution)/shard_map/all_to_all | solution.py:240
  99.1 1.6 %unpack.1 = f32[162,4,512]{2,1,0:T(4,128)} custom-call(f32[8,328,128]{2,1,0:T(8,128)S(1)} %all_to_all.15.in_ref), custom_call_target="tpu_custom_call" | custom-call | tf_op jit(solution)/shard_map/unpack/pallas_call | solution.py:241
  (5 shorter events, 0.1 us)
Async XLA Ops:
  0.0 1.1 %slice-start = ((f32[162,4,512]{2,1,0:T(4,128)}), f32[66,4,512]{2,1,0:T(4,128)S(1)}, s32[]{:S(2)}) async-start(f32[162,4,512]{2,1,0:T(4,128)} %param.7), calls=%async_computation.3 | async-start | bytes 1081344 | tf_op jit(solution)/shard_map/slice | solution.py:194
  0.8 4.0 %slice-start.1 = ((f32[162,4,512]{2,1,0:T(4,128)}), f32[60,4,512]{2,1,0:T(4,128)S(1)}, s32[]{:S(2)}) async-start(f32[162,4,512]{2,1,0:T(4,128)} %param.7), calls=%async_computation.4 | async-start | bytes 983040 | tf_op jit(solution)/shard_map/slice | solution.py:194
  1.2 23.6 %collective-permute-start.2 = (f32[67,4,512]{2,1,0:T(4,128)S(1)}, f32[67,4,512]{2,1,0:T(4,128)S(1)}, u32[]{:S(2)}, u32[]{:S(2)}) collective-permute-start(f32[67,4,512]{2,1,0:T(4,128)S(1)} %pad_maximum_fusion.own_ref), channel_id=1, source_target_pairs={{0,1},{1,2},{2,3},{3,4},{4,5},{5,6},{6,7},{7,8},{8,9},{9,10},{10,1... | collective-permute-start | bytes 1646600 | tf_op jit(solution)/shard_map/ppermute | solution.py:196
  4.9 31.3 %collective-permute-start.1 = (f32[61,4,512]{2,1,0:T(4,128)S(1)}, f32[61,4,512]{2,1,0:T(4,128)S(1)}, u32[]{:S(2)}, u32[]{:S(2)}) collective-permute-start(f32[61,4,512]{2,1,0:T(4,128)S(1)} %pad_maximum_fusion.1.own_ref), channel_id=1, source_target_pairs={{0,1},{1,2},{2,3},{3,4},{4,5},{5,6},{6,7},{7,8},{8,9},{9,10},{10,1... | collective-permute-start | bytes 1499144 | tf_op jit(solution)/shard_map/ppermute | solution.py:196
  24.7 9.3 %slice-start.2 = ((f32[162,4,512]{2,1,0:T(4,128)}), f32[36,4,512]{2,1,0:T(4,128)S(1)}, s32[]{:S(2)}) async-start(f32[162,4,512]{2,1,0:T(4,128)} %param.7), calls=%async_computation.5 | async-start | bytes 589824 | tf_op jit(solution)/shard_map/slice | solution.py:194
  27.5 8.5 %copy-start.2 = (f32[1296]{0:T(1024)S(1)}, f32[1296]{0:T(1024)}, u32[]{:S(2)}) copy-start(f32[1296]{0:T(1024)} %param.10) | copy-start | bytes 15556
  27.5 22.3 %all-to-all-start.1 = ((f32[8,136,128]{2,1,0:T(8,128)}), f32[8,136,128]{2,1,0:T(8,128)S(1)}, u32[]{:S(2)}, u32[]{:S(2)}) async-start(f32[8,136,128]{2,1,0:T(8,128)} %propagate_2.1), calls=%async_computation.1 | async-start | bytes 1114112 | tf_op jit(solution)/shard_map/all_to_all | solution.py:227
  34.1 13.5 %collective-permute-start = (f32[37,4,512]{2,1,0:T(4,128)S(1)}, f32[37,4,512]{2,1,0:T(4,128)S(1)}, u32[]{:S(2)}, u32[]{:S(2)}) collective-permute-start(f32[37,4,512]{2,1,0:T(4,128)S(1)} %pad_maximum_fusion.2.own_ref), channel_id=1, source_target_pairs={{0,1},{1,2},{2,3},{3,4},{4,5},{5,6},{6,7},{7,8},{8,9},{9,10},{10,1... | collective-permute-start | bytes 909320 | tf_op jit(solution)/shard_map/ppermute | solution.py:196
  38.1 16.5 %copy-start.3 = (f32[1296]{0:T(1024)S(1)}, f32[1296]{0:T(1024)}, u32[]{:S(2)}) copy-start(f32[1296]{0:T(1024)} %param.11) | copy-start | bytes 15556
  38.1 16.7 %copy-start = (s32[4,1296]{1,0:T(4,128)S(1)}, s32[4,1296]{1,0:T(4,128)}, u32[]{:S(2)}) copy-start(s32[4,1296]{1,0:T(4,128)} %param.9) | copy-start | bytes 62212
  38.1 16.8 %copy-start.1 = (s32[8,2,4]{1,0,2:T(8,128)S(1)}, s32[8,2,4]{1,0,2:T(8,128)}, u32[]{:S(2)}) copy-start(s32[8,2,4]{1,0,2:T(8,128)} %constant.52.clone) | copy-start | bytes 772
  49.8 17.0 %all-to-all-start = ((f32[8,192,128]{2,1,0:T(8,128)}), f32[8,192,128]{2,1,0:T(8,128)S(1)}, u32[]{:S(2)}, u32[]{:S(2)}) async-start(f32[8,192,128]{2,1,0:T(8,128)} %propagate_1.1), calls=%async_computation | async-start | bytes 1572864 | tf_op jit(solution)/shard_map/all_to_all | solution.py:227

commit v8 on v4

--- a/solution.py
+++ b/solution.py
@@ -52,6 +52,14 @@
 
 def pair_of(row):
     return pl.ds(pl.multiple_of(row, 2), 2)
+
+
+def pack_kernel(start, spectrum_ref, mask_ref, out_ref, sem):
+    size = out_ref.shape[0] - 1
+    copy = pltpu.make_async_copy(spectrum_ref.at[pl.ds(start, size)], out_ref.at[pl.ds(0, size)], sem)
+    copy.start()
+    out_ref[size] = mask_ref[...].astype(jnp.float32)
+    copy.wait()
 
 
 def propagate_kernel(first, quarter_ref, coef_ref, own_ref, halo_ref, out_ref):
@@ -141,7 +149,7 @@
         out_ref[here, :] = kept_ref[k] * energy - 2.0 * (deltas[0] + deltas[1])
         return carry
 
-    lax.fori_loop(0, total_rows // 2, one, 0, unroll=16)
+    lax.fori_loop(0, total_rows // 2, one, 0, unroll=32)
 
     def gather(t, carry):
         s = tile_of(t)
@@ -153,12 +161,16 @@
 
 
 def unpack_kernel(in_ref, out_ref):
-    step_size = 9
+    size, together = out_ref.shape[0], 9
+    first = pl.program_id(0) * size
 
     def several(step, carry):
-        which = [step * step_size + u for u in range(step_size)]
+        which = [step * together + u for u in range(together)]
         both = [
-            [[in_ref[pair * ROW_TILES + i, pair_of(2 * k), :] for pair in range(2)] for i in range(ROW_TILES)]
+            [
+                [in_ref[pair * ROW_TILES + i, pair_of(2 * (first + k)), :] for pair in range(2)]
+                for i in range(ROW_TILES)
+            ]
             for k in which
         ]
         for u, k in enumerate(which):
@@ -166,7 +178,7 @@
                 out_ref[k, :, 128 * i : 128 * (i + 1)] = jnp.concatenate(both[u][i], axis=0)
         return carry
 
-    lax.fori_loop(0, out_ref.shape[0] // step_size, several, 0)
+    lax.fori_loop(0, size // together, several, 0)
 
 
 def per_device(spectrum, sea_mask, quad_bins, coupling, growth):
@@ -184,9 +196,16 @@
     params = pltpu.CompilerParams(vmem_limit_bytes=VMEM_LIMIT)
 
     starts = [sum(CHUNKS[:i]) for i in range(len(CHUNKS))]
-    mask = sea_mask.astype(jnp.float32)[None]
     owns = [
-        jnp.concatenate([lax.slice_in_dim(spectrum, s, s + n, axis=0), mask], axis=0) for s, n in zip(starts, CHUNKS)
+        pl.pallas_call(
+            functools.partial(pack_kernel, start),
+            in_specs=[pl.BlockSpec(memory_space=pl.ANY), vmem],
+            out_specs=vmem,
+            out_shape=jax.ShapeDtypeStruct((size + 1, width, height), jnp.float32),
+            scratch_shapes=[pltpu.SemaphoreType.DMA],
+            name=f"pack_{i}",
+        )(spectrum, sea_mask)
+        for i, (start, size) in enumerate(zip(starts, CHUNKS))
     ]
     halos = [lax.ppermute(own, ("comp", "tile"), pairs) for own in owns]
 
@@ -226,8 +245,9 @@
     back = lax.all_to_all(fresh.reshape(groups, group_rows, 128), "comp", split_axis=0, concat_axis=0, tiled=True)
     return pl.pallas_call(
         unpack_kernel,
+        grid=(2,),
         in_specs=[vmem],
-        out_specs=vmem,
+        out_specs=pl.BlockSpec((comp_dev // 2, width, height), lambda i: (i, 0, 0)),
         out_shape=jax.ShapeDtypeStruct((comp_dev, width, height), jnp.float32),
         compiler_params=params,
         name="unpack",

time: 97.6 us -> 98.7 us (1.011)
  Pallas kernels: 18 us -> 22.7 us
  waiting for transfers between devices: 34.4 us -> 32.1 us
  other arithmetic: 1.18 us -> 0.12 us
    pallas_call x1 -> x3, Pallas kernels: 1.56 us -> 6.65 us  [the longest x2 5.28 us: per_device(): pl.pallas_call(functools.partial(pack_kernel, start), in_specs=[pl.BlockS...]
    ppermute x2, waiting for transfers between devices: 23.4 us -> 21.1 us  [per_device(): halos = [lax.ppermute(own, ('comp', 'tile'), pairs) for own in owns]]
  transfers between devices with their start and end apart: 4 -> 4, of which waited for: 3 -> 3; matrix products, arithmetic and copies ran while one was open for 2% -> 2% of each run, Pallas kernels for 6% -> 9%
where the time goes in v8:
time: 98.7 us; the launch traced here: 98.2 us
  waiting for transfers between devices  32.1 us (33%)
  Pallas kernels  22.7 us (23%)
  blocking collectives  22 us (22%)
  starting transfers between devices  19.2 us (19%)
  local copies, waits for them, and re-layouts  1.82 us (2%)
    all_to_all x1, blocking collectives, per_device(): lax.all_to_all(fresh.reshape(groups, group_rows, 128), 'comp', split_axis...  22 us
    ppermute x2, waiting for transfers between devices, per_device(): halos = [lax.ppermute(own, ('comp', 'tile'), pairs) for own in owns]  21.1 us
    all_to_all x2, starting transfers between devices, per_device(): lax.all_to_all(moved, 'comp', split_axis=0, concat_axis=0, tiled=True)  12 us
    all_to_all x2, waiting for transfers between devices, per_device(): lax.all_to_all(moved, 'comp', split_axis=0, concat_axis=0, tiled=True)  11 us
    pallas_call x1, Pallas kernels, per_device(): pl.pallas_call(settle_kernel, in_specs=[smem, smem, smem] + [vmem] * len(...  9.85 us
    ppermute x2, starting transfers between devices, per_device(): halos = [lax.ppermute(own, ('comp', 'tile'), pairs) for own in owns]  7.22 us
    pallas_call x2, Pallas kernels, per_device(): pl.pallas_call(functools.partial(propagate_kernel, start), in_specs=[smem...  6.2 us
    pallas_call x2, Pallas kernels, per_device(): pl.pallas_call(functools.partial(pack_kernel, start), in_specs=[pl.BlockS...  5.28 us
  transfers between devices with their start and end apart: 4, of which 3 were waited for; matrix products, arithmetic and copies ran while one was open for 2% of the time, Pallas kernels for 9%

profile of v8, /device:TPU:7, one launch (start us, length us, event | category | flops | bytes accessed | tf_op | source)
XLA Modules:
  0.0 98.2 jit_solution(3020400017040142876)
XLA Ops:
  0.0 2.6 %pack_1.1.own_ref = f32[67,4,512]{2,1,0:T(4,128)} custom-call(f32[162,4,512]{2,1,0:T(4,128)} %spectrum_ref.3, s32[4,512]{1,0:T(4,128)} %mask_ref.3), custom_call_target="tpu_custom_call" | custom-call | tf_op jit(solution)/shard_map/pack_1/pallas_call | solution.py:200
  2.6 0.0 copy-start.1
  2.6 3.7 %collective-permute-start.1 = (f32[67,4,512]{2,1,0:T(4,128)}, f32[67,4,512]{2,1,0:T(4,128)S(1)}, u32[]{:S(2)}, u32[]{:S(2)}) collective-permute-start(f32[67,4,512]{2,1,0:T(4,128)} %pack_1.1.own_ref), channel_id=1, source_target_pairs={{0,1},{1,2},{2,3},{3,4},{4,5},{5,6},{6,7},{7,8},{8,9},{9,10},{10,1... | collective-permute-start | bytes 1646600 | tf_op jit(solution)/shard_map/ppermute | solution.py:210
  6.3 2.7 %pack_0.1.own_ref = f32[97,4,512]{2,1,0:T(4,128)} custom-call(f32[162,4,512]{2,1,0:T(4,128)} %spectrum_ref.3, s32[4,512]{1,0:T(4,128)} %mask_ref.3), custom_call_target="tpu_custom_call" | custom-call | tf_op jit(solution)/shard_map/pack_0/pallas_call | solution.py:200
  9.0 3.5 %collective-permute-start = (f32[97,4,512]{2,1,0:T(4,128)}, f32[97,4,512]{2,1,0:T(4,128)S(1)}, u32[]{:S(2)}, u32[]{:S(2)}) collective-permute-start(f32[97,4,512]{2,1,0:T(4,128)} %pack_0.1.own_ref), channel_id=1, source_target_pairs={{0,1},{1,2},{2,3},{3,4},{4,5},{5,6},{6,7},{7,8},{8,9},{9,10},{10,1... | collective-permute-start | bytes 2383880 | tf_op jit(solution)/shard_map/ppermute | solution.py:210
  12.6 0.8 dynamic_slice.3.coef_ref
  13.3 13.1 %collective-permute-done.1.halo_ref = f32[67,4,512]{2,1,0:T(4,128)S(1)} collective-permute-done((f32[67,4,512]{2,1,0:T(4,128)}, f32[67,4,512]{2,1,0:T(4,128)S(1)}, u32[]{:S(2)}, u32[]{:S(2)}) %collective-permute-start.1) | collective-permute-done | bytes 548896 | tf_op jit(solution)/shard_map/ppermute | solution.py:210
  26.5 0.0 copy-done.1
  26.5 0.0 copy-start
  26.5 2.7 %propagate_1.1 = f32[8,136,128]{2,1,0:T(8,128)} custom-call(s32[1]{0:T(128)} %bitcast.3.quarter_ref, f32[486]{0:T(512)S(1)} %dynamic_slice.3.coef_ref, f32[67,4,512]{2,1,0:T(4,128)S(1)} %copy-done.1, f32[67,4,512]{2,1,0:T(4,128)S(1)} %collective-permute-done.1.halo_ref), custom_call_target="tpu_custom_call" | custom-call | flops 13516800 | bytes 1622016 | tf_op jit(solution)/shard_map/propagate_1/pallas_call | solution.py:223
  29.2 6.3 %all-to-all-start.1 = ((f32[8,136,128]{2,1,0:T(8,128)}), f32[8,136,128]{2,1,0:T(8,128)S(1)}, u32[]{:S(2)}, u32[]{:S(2)}) async-start(f32[8,136,128]{2,1,0:T(8,128)} %propagate_1.1), calls=%async_computation.1 | async-start | bytes 1114112 | tf_op jit(solution)/shard_map/all_to_all | solution.py:232
  35.6 7.9 %collective-permute-done.halo_ref = f32[97,4,512]{2,1,0:T(4,128)S(1)} collective-permute-done((f32[97,4,512]{2,1,0:T(4,128)}, f32[97,4,512]{2,1,0:T(4,128)S(1)}, u32[]{:S(2)}, u32[]{:S(2)}) %collective-permute-start) | collective-permute-done | bytes 794656 | tf_op jit(solution)/shard_map/ppermute | solution.py:210
  43.5 0.0 copy-done
  43.5 3.5 %propagate_0.1 = f32[8,192,128]{2,1,0:T(8,128)} custom-call(s32[1]{0:T(128)} %bitcast.3.quarter_ref, f32[486]{0:T(512)S(1)} %dynamic_slice.3.coef_ref, f32[97,4,512]{2,1,0:T(4,128)S(1)} %copy-done, f32[97,4,512]{2,1,0:T(4,128)S(1)} %collective-permute-done.halo_ref), custom_call_target="tpu_custom_call" | custom-call | flops 19660800 | bytes 2359296 | tf_op jit(solution)/shard_map/propagate_0/pallas_call | solution.py:223
  47.0 0.0 copy-start.2
  47.0 0.0 copy-start.3
  47.0 0.0 copy-start.4
  47.0 0.0 copy-start.5
  47.0 0.0 all-to-all-done.1.refs_1_
  47.0 5.7 %all-to-all-start = ((f32[8,192,128]{2,1,0:T(8,128)}), f32[8,192,128]{2,1,0:T(8,128)S(1)}, u32[]{:S(2)}, u32[]{:S(2)}) async-start(f32[8,192,128]{2,1,0:T(8,128)} %propagate_0.1), calls=%async_computation | async-start | bytes 1572864 | tf_op jit(solution)/shard_map/all_to_all | solution.py:232
  52.7 0.0 copy-done.2
  52.7 0.1 reshape.24
  52.8 0.0 copy-done.3
  52.8 0.1 pad_add_fusion
  52.9 0.3 copy.9
  53.2 0.3 reshape.25.bins_ref
  53.5 0.0 copy-done.4
  53.5 0.1 reshape.26
  53.6 0.1 reshape.27.strength_ref
  53.7 0.0 copy-done.5
  53.7 0.1 reshape.28
  53.8 0.1 reshape.29.kept_ref
  53.9 11.0 %all-to-all-done.refs_0_ = f32[8,192,128]{2,1,0:T(8,128)S(1)} async-done(((f32[8,192,128]{2,1,0:T(8,128)}), f32[8,192,128]{2,1,0:T(8,128)S(1)}, u32[]{:S(2)}, u32[]{:S(2)}) %all-to-all-start) | async-done | bytes 786464 | tf_op jit(solution)/shard_map/all_to_all | solution.py:232
  64.9 9.9 %settle.1 = f32[2624,128]{1,0:T(8,128)S(1)} custom-call(s32[5248]{0:T(1024)S(1)} %reshape.25.bins_ref, f32[1312]{0:T(1024)S(1)} %reshape.27.strength_ref, f32[1312]{0:T(1024)S(1)} %reshape.29.kept_ref, f32[8,192,128]{2,1,0:T(8,128)S(1)} %all-to-all-done.refs_0_, f32[8,136,128]{2,1,0:T(8,128)S(1)} %all-to-all-done.1.refs_1_), custom_call_target="tpu_custom_call" | custom-call | tf_op jit(solution)/shard_map/settle/pallas_call | solution.py:235
  74.8 22.0 %all_to_all.15.in_ref = f32[8,328,128]{2,1,0:T(8,128)S(1)} all-to-all(f32[8,328,128]{2,1,0:T(8,128)S(1)} %bitcast.10), channel_id=1, replica_groups=mesh['comp'=8,'tile'=64] {'comp'}, dimensions={0} | all-to-all | bytes 2686976 | tf_op jit(solution)/shard_map/all_to_all | solution.py:245
  96.8 1.4 %unpack.1 = f32[162,4,512]{2,1,0:T(4,128)} custom-call(f32[8,328,128]{2,1,0:T(8,128)S(1)} %all_to_all.15.in_ref), custom_call_target="tpu_custom_call" | custom-call | tf_op jit(solution)/shard_map/unpack/pallas_call | solution.py:246
  (5 shorter events, 0.1 us)
Async XLA Ops:
  2.6 23.9 %copy-start.1 = (f32[67,4,512]{2,1,0:T(4,128)S(1)}, f32[67,4,512]{2,1,0:T(4,128)}, u32[]{:S(2)}) copy-start(f32[67,4,512]{2,1,0:T(4,128)} %pack_1.1.own_ref) | copy-start | bytes 1646596
  2.6 23.9 %collective-permute-start.1 = (f32[67,4,512]{2,1,0:T(4,128)}, f32[67,4,512]{2,1,0:T(4,128)S(1)}, u32[]{:S(2)}, u32[]{:S(2)}) collective-permute-start(f32[67,4,512]{2,1,0:T(4,128)} %pack_1.1.own_ref), channel_id=1, source_target_pairs={{0,1},{1,2},{2,3},{3,4},{4,5},{5,6},{6,7},{7,8},{8,9},{9,10},{10,1... | collective-permute-start | bytes 1646600 | tf_op jit(solution)/shard_map/ppermute | solution.py:210
  9.0 34.5 %collective-permute-start = (f32[97,4,512]{2,1,0:T(4,128)}, f32[97,4,512]{2,1,0:T(4,128)S(1)}, u32[]{:S(2)}, u32[]{:S(2)}) collective-permute-start(f32[97,4,512]{2,1,0:T(4,128)} %pack_0.1.own_ref), channel_id=1, source_target_pairs={{0,1},{1,2},{2,3},{3,4},{4,5},{5,6},{6,7},{7,8},{8,9},{9,10},{10,1... | collective-permute-start | bytes 2383880 | tf_op jit(solution)/shard_map/ppermute | solution.py:210
  26.5 17.0 %copy-start = (f32[97,4,512]{2,1,0:T(4,128)S(1)}, f32[97,4,512]{2,1,0:T(4,128)}, u32[]{:S(2)}) copy-start(f32[97,4,512]{2,1,0:T(4,128)} %pack_0.1.own_ref) | copy-start | bytes 2383876
  29.2 17.7 %all-to-all-start.1 = ((f32[8,136,128]{2,1,0:T(8,128)}), f32[8,136,128]{2,1,0:T(8,128)S(1)}, u32[]{:S(2)}, u32[]{:S(2)}) async-start(f32[8,136,128]{2,1,0:T(8,128)} %propagate_1.1), calls=%async_computation.1 | async-start | bytes 1114112 | tf_op jit(solution)/shard_map/all_to_all | solution.py:232
  47.0 5.7 %copy-start.2 = (s32[4,1296]{1,0:T(4,128)S(1)}, s32[4,1296]{1,0:T(4,128)}, u32[]{:S(2)}) copy-start(s32[4,1296]{1,0:T(4,128)} %param.9) | copy-start | bytes 62212
  47.0 5.8 %copy-start.3 = (s32[8,2,4]{1,0,2:T(8,128)S(1)}, s32[8,2,4]{1,0,2:T(8,128)}, u32[]{:S(2)}) copy-start(s32[8,2,4]{1,0,2:T(8,128)} %constant.52.clone) | copy-start | bytes 772
  47.0 6.5 %copy-start.4 = (f32[1296]{0:T(1024)S(1)}, f32[1296]{0:T(1024)}, u32[]{:S(2)}) copy-start(f32[1296]{0:T(1024)} %param.10) | copy-start | bytes 15556
  47.0 6.7 %copy-start.5 = (f32[1296]{0:T(1024)S(1)}, f32[1296]{0:T(1024)}, u32[]{:S(2)}) copy-start(f32[1296]{0:T(1024)} %param.11) | copy-start | bytes 15556
  47.0 18.0 %all-to-all-start = ((f32[8,192,128]{2,1,0:T(8,128)}), f32[8,192,128]{2,1,0:T(8,128)S(1)}, u32[]{:S(2)}, u32[]{:S(2)}) async-start(f32[8,192,128]{2,1,0:T(8,128)} %propagate_0.1), calls=%async_computation | async-start | bytes 1572864 | tf_op jit(solution)/shard_map/all_to_all | solution.py:232

commit v9 on v8

--- a/solution.py
+++ b/solution.py
@@ -19,8 +19,8 @@
 time_step = 0.5
 
 ROW_TILES = 4
-CHUNKS = (96, 66)
-TOGETHER = 28
+CHUNKS = (92, 70)
+TOGETHER = 35
 VMEM_LIMIT = 40 << 20
 
 
@@ -52,14 +52,6 @@
 
 def pair_of(row):
     return pl.ds(pl.multiple_of(row, 2), 2)
-
-
-def pack_kernel(start, spectrum_ref, mask_ref, out_ref, sem):
-    size = out_ref.shape[0] - 1
-    copy = pltpu.make_async_copy(spectrum_ref.at[pl.ds(start, size)], out_ref.at[pl.ds(0, size)], sem)
-    copy.start()
-    out_ref[size] = mask_ref[...].astype(jnp.float32)
-    copy.wait()
 
 
 def propagate_kernel(first, quarter_ref, coef_ref, own_ref, halo_ref, out_ref):
@@ -196,16 +188,9 @@
     params = pltpu.CompilerParams(vmem_limit_bytes=VMEM_LIMIT)
 
     starts = [sum(CHUNKS[:i]) for i in range(len(CHUNKS))]
+    mask = sea_mask.astype(jnp.float32)[None]
     owns = [
-        pl.pallas_call(
-            functools.partial(pack_kernel, start),
-            in_specs=[pl.BlockSpec(memory_space=pl.ANY), vmem],
-            out_specs=vmem,
-            out_shape=jax.ShapeDtypeStruct((size + 1, width, height), jnp.float32),
-            scratch_shapes=[pltpu.SemaphoreType.DMA],
-            name=f"pack_{i}",
-        )(spectrum, sea_mask)
-        for i, (start, size) in enumerate(zip(starts, CHUNKS))
+        jnp.concatenate([lax.slice_in_dim(spectrum, s, s + n, axis=0), mask], axis=0) for s, n in zip(starts, CHUNKS)
     ]
     halos = [lax.ppermute(own, ("comp", "tile"), pairs) for own in owns]
 

time: 98.7 us -> 96.6 us (0.979)
  Pallas kernels: 22.7 us -> 17.5 us
  waiting for transfers between devices: 32.1 us -> 34 us
  other arithmetic: 0.12 us -> 1.18 us
    pallas_call x2 -> x0, Pallas kernels: 5.28 us -> none  [per_device(): pl.pallas_call(functools.partial(pack_kernel, start), in_specs=[pl.BlockS...]
    ppermute x2, waiting for transfers between devices: 21.1 us -> 23.3 us  [per_device(): halos = [lax.ppermute(own, ('comp', 'tile'), pairs) for own in owns]]
  transfers between devices with their start and end apart: 4 -> 4, of which waited for: 3 -> 3; matrix products, arithmetic and copies ran while one was open for 2% -> 2% of each run, Pallas kernels for 9% -> 7%
where the time goes in v9:
time: 96.6 us; the launch traced here: 96.2 us
  waiting for transfers between devices  34 us (35%)
  blocking collectives  22 us (23%)
  starting transfers between devices  19.2 us (20%)
  Pallas kernels  17.5 us (18%)
  local copies, waits for them, and re-layouts  2.13 us (2%)
  other arithmetic  1.18 us (1%)
    ppermute x2, waiting for transfers between devices, per_device(): halos = [lax.ppermute(own, ('comp', 'tile'), pairs) for own in owns]  23.3 us
    all_to_all x1, blocking collectives, per_device(): lax.all_to_all(fresh.reshape(groups, group_rows, 128), 'comp', split_axis...  22 us
    all_to_all x2, starting transfers between devices, per_device(): lax.all_to_all(moved, 'comp', split_axis=0, concat_axis=0, tiled=True)  12 us
    all_to_all x2, waiting for transfers between devices, per_device(): lax.all_to_all(moved, 'comp', split_axis=0, concat_axis=0, tiled=True)  10.7 us
    pallas_call x1, Pallas kernels, per_device(): pl.pallas_call(settle_kernel, in_specs=[smem, smem, smem] + [vmem] * len(...  9.9 us
    ppermute x2, starting transfers between devices, per_device(): halos = [lax.ppermute(own, ('comp', 'tile'), pairs) for own in owns]  7.22 us
    pallas_call x2, Pallas kernels, per_device(): pl.pallas_call(functools.partial(propagate_kernel, start), in_specs=[smem...  6.28 us
  transfers between devices with their start and end apart: 4, of which 3 were waited for; matrix products, arithmetic and copies ran while one was open for 2% of the time, Pallas kernels for 7%

profile of v9, /device:TPU:7, one launch (start us, length us, event | category | flops | bytes accessed | tf_op | source)
XLA Modules:
  0.0 96.2 jit_solution(13496066989561684105)
XLA Ops:
  0.0 0.0 slice-start
  0.0 0.8 convert_bitcast_fusion
  0.8 0.3 slice-done
  1.1 0.0 slice-start.1
  1.1 0.1 pad_maximum_fusion.1.own_ref
  1.2 3.7 %collective-permute-start.1 = (f32[71,4,512]{2,1,0:T(4,128)S(1)}, f32[71,4,512]{2,1,0:T(4,128)S(1)}, u32[]{:S(2)}, u32[]{:S(2)}) collective-permute-start(f32[71,4,512]{2,1,0:T(4,128)S(1)} %pad_maximum_fusion.1.own_ref), channel_id=1, source_target_pairs={{0,1},{1,2},{2,3},{3,4},{4,5},{5,6},{6,7},{7,8},{8,9},{9,10},{10,1... | collective-permute-start | bytes 1744904 | tf_op jit(solution)/shard_map/ppermute | solution.py:195
  4.9 0.0 slice-done.1
  4.9 0.2 pad_maximum_fusion.own_ref
  5.1 3.5 %collective-permute-start = (f32[93,4,512]{2,1,0:T(4,128)S(1)}, f32[93,4,512]{2,1,0:T(4,128)S(1)}, u32[]{:S(2)}, u32[]{:S(2)}) collective-permute-start(f32[93,4,512]{2,1,0:T(4,128)S(1)} %pad_maximum_fusion.own_ref), channel_id=1, source_target_pairs={{0,1},{1,2},{2,3},{3,4},{4,5},{5,6},{6,7},{7,8},{8,9},{9,10},{10,1... | collective-permute-start | bytes 2285576 | tf_op jit(solution)/shard_map/ppermute | solution.py:195
  8.6 0.8 dynamic_slice.3.coef_ref
  9.4 16.2 %collective-permute-done.1.halo_ref = f32[71,4,512]{2,1,0:T(4,128)S(1)} collective-permute-done((f32[71,4,512]{2,1,0:T(4,128)S(1)}, f32[71,4,512]{2,1,0:T(4,128)S(1)}, u32[]{:S(2)}, u32[]{:S(2)}) %collective-permute-start.1) | collective-permute-done | bytes 581664 | tf_op jit(solution)/shard_map/ppermute | solution.py:195
  25.6 2.9 %propagate_1.1 = f32[8,144,128]{2,1,0:T(8,128)} custom-call(s32[1]{0:T(128)} %bitcast.3.quarter_ref, f32[486]{0:T(512)S(1)} %dynamic_slice.3.coef_ref, f32[71,4,512]{2,1,0:T(4,128)S(1)} %pad_maximum_fusion.1.own_ref, f32[71,4,512]{2,1,0:T(4,128)S(1)} %collective-permute-done.1.halo_ref), custom_call_target="tpu_custom_call" | custom-call | flops 14336000 | bytes 1720320 | tf_op jit(solution)/shard_map/propagate_1/pallas_call | solution.py:208
  28.5 6.3 %all-to-all-start.1 = ((f32[8,144,128]{2,1,0:T(8,128)}), f32[8,144,128]{2,1,0:T(8,128)S(1)}, u32[]{:S(2)}, u32[]{:S(2)}) async-start(f32[8,144,128]{2,1,0:T(8,128)} %propagate_1.1), calls=%async_computation.1 | async-start | bytes 1179648 | tf_op jit(solution)/shard_map/all_to_all | solution.py:217
  34.8 0.0 copy-start
  34.8 7.1 %collective-permute-done.halo_ref = f32[93,4,512]{2,1,0:T(4,128)S(1)} collective-permute-done((f32[93,4,512]{2,1,0:T(4,128)S(1)}, f32[93,4,512]{2,1,0:T(4,128)S(1)}, u32[]{:S(2)}, u32[]{:S(2)}) %collective-permute-start) | collective-permute-done | bytes 761888 | tf_op jit(solution)/shard_map/ppermute | solution.py:195
  41.9 3.4 %propagate_0.1 = f32[8,184,128]{2,1,0:T(8,128)} custom-call(s32[1]{0:T(128)} %bitcast.3.quarter_ref, f32[486]{0:T(512)S(1)} %dynamic_slice.3.coef_ref, f32[93,4,512]{2,1,0:T(4,128)S(1)} %pad_maximum_fusion.own_ref, f32[93,4,512]{2,1,0:T(4,128)S(1)} %collective-permute-done.halo_ref), custom_call_target="tpu_custom_call" | custom-call | flops 18841600 | bytes 2260992 | tf_op jit(solution)/shard_map/propagate_0/pallas_call | solution.py:208
  45.3 0.0 copy-start.1
  45.3 0.0 copy-start.2
  45.3 0.0 copy-start.3
  45.3 0.0 all-to-all-done.1.refs_1_
  45.3 5.7 %all-to-all-start = ((f32[8,184,128]{2,1,0:T(8,128)}), f32[8,184,128]{2,1,0:T(8,128)S(1)}, u32[]{:S(2)}, u32[]{:S(2)}) async-start(f32[8,184,128]{2,1,0:T(8,128)} %propagate_0.1), calls=%async_computation | async-start | bytes 1507328 | tf_op jit(solution)/shard_map/all_to_all | solution.py:217
  51.0 0.0 copy-done
  51.0 0.1 reshape.24
  51.1 0.0 copy-done.1
  51.1 0.1 pad_add_fusion
  51.2 0.3 copy.9
  51.5 0.3 reshape.25.bins_ref
  51.8 0.0 copy-done.2
  51.8 0.1 reshape.26
  51.9 0.1 reshape.27.strength_ref
  52.0 0.0 copy-done.3
  52.0 0.1 reshape.28
  52.1 0.1 reshape.29.kept_ref
  52.2 10.7 %all-to-all-done.refs_0_ = f32[8,184,128]{2,1,0:T(8,128)S(1)} async-done(((f32[8,184,128]{2,1,0:T(8,128)}), f32[8,184,128]{2,1,0:T(8,128)S(1)}, u32[]{:S(2)}, u32[]{:S(2)}) %all-to-all-start) | async-done | bytes 753696 | tf_op jit(solution)/shard_map/all_to_all | solution.py:217
  62.9 9.9 %settle.1 = f32[2624,128]{1,0:T(8,128)S(1)} custom-call(s32[5248]{0:T(1024)S(1)} %reshape.25.bins_ref, f32[1312]{0:T(1024)S(1)} %reshape.27.strength_ref, f32[1312]{0:T(1024)S(1)} %reshape.29.kept_ref, f32[8,184,128]{2,1,0:T(8,128)S(1)} %all-to-all-done.refs_0_, f32[8,144,128]{2,1,0:T(8,128)S(1)} %all-to-all-done.1.refs_1_), custom_call_target="tpu_custom_call" | custom-call | tf_op jit(solution)/shard_map/settle/pallas_call | solution.py:220
  72.8 22.0 %all_to_all.15.in_ref = f32[8,328,128]{2,1,0:T(8,128)S(1)} all-to-all(f32[8,328,128]{2,1,0:T(8,128)S(1)} %bitcast.12), channel_id=1, replica_groups=mesh['comp'=8,'tile'=64] {'comp'}, dimensions={0} | all-to-all | bytes 2686976 | tf_op jit(solution)/shard_map/all_to_all | solution.py:230
  94.8 1.4 %unpack.1 = f32[162,4,512]{2,1,0:T(4,128)} custom-call(f32[8,328,128]{2,1,0:T(8,128)S(1)} %all_to_all.15.in_ref), custom_call_target="tpu_custom_call" | custom-call | tf_op jit(solution)/shard_map/unpack/pallas_call | solution.py:231
  (5 shorter events, 0.1 us)
Async XLA Ops:
  0.0 1.1 %slice-start = ((f32[162,4,512]{2,1,0:T(4,128)}), f32[70,4,512]{2,1,0:T(4,128)S(1)}, s32[]{:S(2)}) async-start(f32[162,4,512]{2,1,0:T(4,128)} %param.7), calls=%async_computation.3 | async-start | bytes 1146880 | tf_op jit(solution)/shard_map/slice | solution.py:193
  1.1 3.8 %slice-start.1 = ((f32[162,4,512]{2,1,0:T(4,128)}), f32[92,4,512]{2,1,0:T(4,128)S(1)}, s32[]{:S(2)}) async-start(f32[162,4,512]{2,1,0:T(4,128)} %param.7), calls=%async_computation.4 | async-start | bytes 1507328 | tf_op jit(solution)/shard_map/slice | solution.py:193
  1.2 24.4 %collective-permute-start.1 = (f32[71,4,512]{2,1,0:T(4,128)S(1)}, f32[71,4,512]{2,1,0:T(4,128)S(1)}, u32[]{:S(2)}, u32[]{:S(2)}) collective-permute-start(f32[71,4,512]{2,1,0:T(4,128)S(1)} %pad_maximum_fusion.1.own_ref), channel_id=1, source_target_pairs={{0,1},{1,2},{2,3},{3,4},{4,5},{5,6},{6,7},{7,8},{8,9},{9,10},{10,1... | collective-permute-start | bytes 1744904 | tf_op jit(solution)/shard_map/ppermute | solution.py:195
  5.1 36.8 %collective-permute-start = (f32[93,4,512]{2,1,0:T(4,128)S(1)}, f32[93,4,512]{2,1,0:T(4,128)S(1)}, u32[]{:S(2)}, u32[]{:S(2)}) collective-permute-start(f32[93,4,512]{2,1,0:T(4,128)S(1)} %pad_maximum_fusion.own_ref), channel_id=1, source_target_pairs={{0,1},{1,2},{2,3},{3,4},{4,5},{5,6},{6,7},{7,8},{8,9},{9,10},{10,1... | collective-permute-start | bytes 2285576 | tf_op jit(solution)/shard_map/ppermute | solution.py:195
  28.5 16.8 %all-to-all-start.1 = ((f32[8,144,128]{2,1,0:T(8,128)}), f32[8,144,128]{2,1,0:T(8,128)S(1)}, u32[]{:S(2)}, u32[]{:S(2)}) async-start(f32[8,144,128]{2,1,0:T(8,128)} %propagate_1.1), calls=%async_computation.1 | async-start | bytes 1179648 | tf_op jit(solution)/shard_map/all_to_all | solution.py:217
  34.8 16.2 %copy-start = (s32[4,1296]{1,0:T(4,128)S(1)}, s32[4,1296]{1,0:T(4,128)}, u32[]{:S(2)}) copy-start(s32[4,1296]{1,0:T(4,128)} %param.9) | copy-start | bytes 62212
  45.3 5.8 %copy-start.1 = (s32[8,2,4]{1,0,2:T(8,128)S(1)}, s32[8,2,4]{1,0,2:T(8,128)}, u32[]{:S(2)}) copy-start(s32[8,2,4]{1,0,2:T(8,128)} %constant.52.clone) | copy-start | bytes 772
  45.3 6.5 %copy-start.2 = (f32[1296]{0:T(1024)S(1)}, f32[1296]{0:T(1024)}, u32[]{:S(2)}) copy-start(f32[1296]{0:T(1024)} %param.10) | copy-start | bytes 15556
  45.3 6.7 %copy-start.3 = (f32[1296]{0:T(1024)S(1)}, f32[1296]{0:T(1024)}, u32[]{:S(2)}) copy-start(f32[1296]{0:T(1024)} %param.11) | copy-start | bytes 15556
  45.3 17.6 %all-to-all-start = ((f32[8,184,128]{2,1,0:T(8,128)}), f32[8,184,128]{2,1,0:T(8,128)S(1)}, u32[]{:S(2)}, u32[]{:S(2)}) async-start(f32[8,184,128]{2,1,0:T(8,128)} %propagate_0.1), calls=%async_computation | async-start | bytes 1507328 | tf_op jit(solution)/shard_map/all_to_all | solution.py:217

commit v10 on v9

--- a/solution.py
+++ b/solution.py
@@ -19,7 +19,7 @@
 time_step = 0.5
 
 ROW_TILES = 4
-CHUNKS = (92, 70)
+CHUNKS = (84, 78)
 TOGETHER = 35
 VMEM_LIMIT = 40 << 20
 
@@ -54,9 +54,14 @@
     return pl.ds(pl.multiple_of(row, 2), 2)
 
 
-def propagate_kernel(first, quarter_ref, coef_ref, own_ref, halo_ref, out_ref):
+def together(size):
+    return max(n for n in range(1, TOGETHER + 1) if size % n == 0)
+
+
+def propagate_kernel(first, quarter_ref, coef_ref, own_ref, halo_ref, target_ref, *scratch):
+    out_ref, sems = scratch or (target_ref, None)
     size = own_ref.shape[0] - 1
-    side_by_side = max(n for n in range(1, TOGETHER + 1) if size % n == 0)
+    side_by_side = together(size)
     quarter = quarter_ref[0]
     lane = lax.broadcasted_iota(jnp.int32, (8, 128), 1)
     extra = out_ref.shape[1] - 2 * size
@@ -97,7 +102,18 @@
                         out_ref[pair * ROW_TILES + i, pair_of(2 * k), :] = v[at : at + 2, :]
             return carry
 
-        lax.fori_loop(0, size // side_by_side, several, 0)
+        def leave(step):
+            rows = pl.ds(pl.multiple_of(2 * side_by_side * step, 8), 2 * side_by_side)
+            return pltpu.make_async_copy(out_ref.at[:, rows, :], target_ref.at[:, rows, :], sems.at[step])
+
+        if sems is None:
+            lax.fori_loop(0, size // side_by_side, several, 0)
+            return
+        for step in range(size // side_by_side):
+            several(step, 0)
+            leave(step).start()
+        for step in range(size // side_by_side):
+            leave(step).wait()
 
     for value, (east, north) in enumerate(((True, True), (False, True), (False, False), (True, False))):
         pl.when(quarter == value)(functools.partial(run, east, north))
@@ -153,11 +169,11 @@
 
 
 def unpack_kernel(in_ref, out_ref):
-    size, together = out_ref.shape[0], 9
+    size, several_at_once = out_ref.shape[0], 9
     first = pl.program_id(0) * size
 
     def several(step, carry):
-        which = [step * together + u for u in range(together)]
+        which = [step * several_at_once + u for u in range(several_at_once)]
         both = [
             [
                 [in_ref[pair * ROW_TILES + i, pair_of(2 * (first + k)), :] for pair in range(2)]
@@ -170,7 +186,7 @@
                 out_ref[k, :, 128 * i : 128 * (i + 1)] = jnp.concatenate(both[u][i], axis=0)
         return carry
 
-    lax.fori_loop(0, size // together, several, 0)
+    lax.fori_loop(0, size // several_at_once, several, 0)
 
 
 def per_device(spectrum, sea_mask, quad_bins, coupling, growth):
@@ -205,11 +221,15 @@
 
     pieces = []
     for i, (start, size) in enumerate(zip(starts, CHUNKS)):
+        shape = (groups, rows_of(size), 128)
+        steps = size // together(size)
+        early = 2 * together(size) % 8 == 0
         moved = pl.pallas_call(
             functools.partial(propagate_kernel, start),
             in_specs=[smem, smem, vmem, vmem],
-            out_specs=vmem,
-            out_shape=jax.ShapeDtypeStruct((groups, rows_of(size), 128), jnp.float32),
+            out_specs=pl.BlockSpec(memory_space=pl.ANY) if early else vmem,
+            out_shape=jax.ShapeDtypeStruct(shape, jnp.float32),
+            scratch_shapes=[pltpu.VMEM(shape, jnp.float32), pltpu.SemaphoreType.DMA((steps,))] if early else [],
             compiler_params=params,
             cost_estimate=pl.CostEstimate(flops=100 * size * 2048, bytes_accessed=12 * size * 2048, transcendentals=0),
             name=f"propagate_{i}",

time: 96.6 us -> 96.6 us (level)
  waiting for transfers between devices: 34 us -> 35.5 us
  starting transfers between devices: 19.2 us -> 17.9 us
    all_to_all x2, waiting for transfers between devices: 10.7 us -> 12.4 us  [per_device(): lax.all_to_all(moved, 'comp', split_axis=0, concat_axis=0, tiled=True)]
    all_to_all x2, starting transfers between devices: 12 us -> 10.7 us  [per_device(): lax.all_to_all(moved, 'comp', split_axis=0, concat_axis=0, tiled=True)]
  transfers between devices with their start and end apart: 4 -> 4, of which waited for: 3 -> 4; matrix products, arithmetic and copies ran while one was open for 2% -> 2% of each run, Pallas kernels for 7% -> 6%
where the time goes in v10:
time: 96.6 us; the launch traced here: 96.2 us
  waiting for transfers between devices  35.5 us (37%)
  blocking collectives  22 us (23%)
  starting transfers between devices  17.9 us (19%)
  Pallas kernels  17.3 us (18%)
  local copies, waits for them, and re-layouts  2.15 us (2%)
  other arithmetic  1.18 us (1%)
    ppermute x2, waiting for transfers between devices, per_device(): halos = [lax.ppermute(own, ('comp', 'tile'), pairs) for own in owns]  23.1 us
    all_to_all x1, blocking collectives, per_device(): lax.all_to_all(fresh.reshape(groups, group_rows, 128), 'comp', split_axis...  22 us
    all_to_all x2, waiting for transfers between devices, per_device(): lax.all_to_all(moved, 'comp', split_axis=0, concat_axis=0, tiled=True)  12.4 us
    all_to_all x2, starting transfers between devices, per_device(): lax.all_to_all(moved, 'comp', split_axis=0, concat_axis=0, tiled=True)  10.7 us
    pallas_call x1, Pallas kernels, per_device(): pl.pallas_call(settle_kernel, in_specs=[smem, smem, smem] + [vmem] * len(...  9.9 us
    ppermute x2, starting transfers between devices, per_device(): halos = [lax.ppermute(own, ('comp', 'tile'), pairs) for own in owns]  7.22 us
    pallas_call x2, Pallas kernels, per_device(): pl.pallas_call(functools.partial(propagate_kernel, start), in_specs=[smem...  6.06 us
  transfers between devices with their start and end apart: 4, of which 4 were waited for; matrix products, arithmetic and copies ran while one was open for 2% of the time, Pallas kernels for 6%

profile of v10, /device:TPU:7, one launch (start us, length us, event | category | flops | bytes accessed | tf_op | source)
XLA Modules:
  0.0 96.2 jit_solution(6578626737317419327)
XLA Ops:
  0.0 0.0 slice-start
  0.0 0.8 convert_bitcast_fusion
  0.8 0.3 slice-done
  1.1 0.0 slice-start.1
  1.1 0.1 pad_maximum_fusion.1.own_ref
  1.2 3.7 %collective-permute-start.1 = (f32[79,4,512]{2,1,0:T(4,128)S(1)}, f32[79,4,512]{2,1,0:T(4,128)S(1)}, u32[]{:S(2)}, u32[]{:S(2)}) collective-permute-start(f32[79,4,512]{2,1,0:T(4,128)S(1)} %pad_maximum_fusion.1.own_ref), channel_id=1, source_target_pairs={{0,1},{1,2},{2,3},{3,4},{4,5},{5,6},{6,7},{7,8},{8,9},{9,10},{10,1... | collective-permute-start | bytes 1941512 | tf_op jit(solution)/shard_map/ppermute | solution.py:211
  4.9 0.0 slice-done.1
  4.9 0.2 pad_maximum_fusion.own_ref
  5.1 3.5 %collective-permute-start = (f32[85,4,512]{2,1,0:T(4,128)S(1)}, f32[85,4,512]{2,1,0:T(4,128)S(1)}, u32[]{:S(2)}, u32[]{:S(2)}) collective-permute-start(f32[85,4,512]{2,1,0:T(4,128)S(1)} %pad_maximum_fusion.own_ref), channel_id=1, source_target_pairs={{0,1},{1,2},{2,3},{3,4},{4,5},{5,6},{6,7},{7,8},{8,9},{9,10},{10,1... | collective-permute-start | bytes 2088968 | tf_op jit(solution)/shard_map/ppermute | solution.py:211
  8.7 0.8 dynamic_slice.3.coef_ref
  9.5 17.6 %collective-permute-done.1.halo_ref = f32[79,4,512]{2,1,0:T(4,128)S(1)} collective-permute-done((f32[79,4,512]{2,1,0:T(4,128)S(1)}, f32[79,4,512]{2,1,0:T(4,128)S(1)}, u32[]{:S(2)}, u32[]{:S(2)}) %collective-permute-start.1) | collective-permute-done | bytes 647200 | tf_op jit(solution)/shard_map/ppermute | solution.py:211
  27.0 3.1 %propagate_1.1 = f32[8,160,128]{2,1,0:T(8,128)} custom-call(s32[1]{0:T(128)} %bitcast.3.quarter_ref, f32[486]{0:T(512)S(1)} %dynamic_slice.3.coef_ref, f32[79,4,512]{2,1,0:T(4,128)S(1)} %pad_maximum_fusion.1.own_ref, f32[79,4,512]{2,1,0:T(4,128)S(1)} %collective-permute-done.1.halo_ref), custom_call_target="tpu_custom_call" | custom-call | flops 15974400 | bytes 1916928 | tf_op jit(solution)/shard_map/propagate_1/pallas_call | solution.py:227
  30.1 6.3 %all-to-all-start.1 = ((f32[8,160,128]{2,1,0:T(8,128)}), f32[8,160,128]{2,1,0:T(8,128)S(1)}, u32[]{:S(2)}, u32[]{:S(2)}) async-start(f32[8,160,128]{2,1,0:T(8,128)} %propagate_1.1), calls=%async_computation.1 | async-start | bytes 1310720 | tf_op jit(solution)/shard_map/all_to_all | solution.py:237
  36.5 0.0 copy-start
  36.5 0.0 copy-start.1
  36.5 5.5 %collective-permute-done.halo_ref = f32[85,4,512]{2,1,0:T(4,128)S(1)} collective-permute-done((f32[85,4,512]{2,1,0:T(4,128)S(1)}, f32[85,4,512]{2,1,0:T(4,128)S(1)}, u32[]{:S(2)}, u32[]{:S(2)}) %collective-permute-start) | collective-permute-done | bytes 696352 | tf_op jit(solution)/shard_map/ppermute | solution.py:211
  42.0 3.0 %propagate_0.1 = f32[8,168,128]{2,1,0:T(8,128)} custom-call(s32[1]{0:T(128)} %bitcast.3.quarter_ref, f32[486]{0:T(512)S(1)} %dynamic_slice.3.coef_ref, f32[85,4,512]{2,1,0:T(4,128)S(1)} %pad_maximum_fusion.own_ref, f32[85,4,512]{2,1,0:T(4,128)S(1)} %collective-permute-done.halo_ref), custom_call_target="tpu_custom_call" | custom-call | flops 17203200 | bytes 2064384 | tf_op jit(solution)/shard_map/propagate_0/pallas_call | solution.py:227
  45.0 0.0 copy-start.2
  45.0 0.0 copy-start.3
  45.0 2.4 %all-to-all-done.1.refs_1_ = f32[8,160,128]{2,1,0:T(8,128)S(1)} async-done(((f32[8,160,128]{2,1,0:T(8,128)}), f32[8,160,128]{2,1,0:T(8,128)S(1)}, u32[]{:S(2)}, u32[]{:S(2)}) %all-to-all-start.1) | async-done | bytes 655392 | tf_op jit(solution)/shard_map/all_to_all | solution.py:237
  47.3 4.3 %all-to-all-start = ((f32[8,168,128]{2,1,0:T(8,128)}), f32[8,168,128]{2,1,0:T(8,128)S(1)}, u32[]{:S(2)}, u32[]{:S(2)}) async-start(f32[8,168,128]{2,1,0:T(8,128)} %propagate_0.1), calls=%async_computation | async-start | bytes 1376256 | tf_op jit(solution)/shard_map/all_to_all | solution.py:237
  51.7 0.0 copy-done
  51.7 0.1 reshape.24
  51.8 0.0 copy-done.1
  51.8 0.1 pad_add_fusion
  51.9 0.3 copy.9
  52.2 0.3 reshape.25.bins_ref
  52.5 0.0 copy-done.2
  52.5 0.1 reshape.26
  52.6 0.1 reshape.27.strength_ref
  52.7 0.0 copy-done.3
  52.7 0.1 reshape.28
  52.8 0.1 reshape.29.kept_ref
  52.9 10.0 %all-to-all-done.refs_0_ = f32[8,168,128]{2,1,0:T(8,128)S(1)} async-done(((f32[8,168,128]{2,1,0:T(8,128)}), f32[8,168,128]{2,1,0:T(8,128)S(1)}, u32[]{:S(2)}, u32[]{:S(2)}) %all-to-all-start) | async-done | bytes 688160 | tf_op jit(solution)/shard_map/all_to_all | solution.py:237
  62.9 9.9 %settle.1 = f32[2624,128]{1,0:T(8,128)S(1)} custom-call(s32[5248]{0:T(1024)S(1)} %reshape.25.bins_ref, f32[1312]{0:T(1024)S(1)} %reshape.27.strength_ref, f32[1312]{0:T(1024)S(1)} %reshape.29.kept_ref, f32[8,168,128]{2,1,0:T(8,128)S(1)} %all-to-all-done.refs_0_, f32[8,160,128]{2,1,0:T(8,128)S(1)} %all-to-all-done.1.refs_1_), custom_call_target="tpu_custom_call" | custom-call | tf_op jit(solution)/shard_map/settle/pallas_call | solution.py:240
  72.8 22.0 %all_to_all.15.in_ref = f32[8,328,128]{2,1,0:T(8,128)S(1)} all-to-all(f32[8,328,128]{2,1,0:T(8,128)S(1)} %bitcast.12), channel_id=1, replica_groups=mesh['comp'=8,'tile'=64] {'comp'}, dimensions={0} | all-to-all | bytes 2686976 | tf_op jit(solution)/shard_map/all_to_all | solution.py:250
  94.8 1.4 %unpack.1 = f32[162,4,512]{2,1,0:T(4,128)} custom-call(f32[8,328,128]{2,1,0:T(8,128)S(1)} %all_to_all.15.in_ref), custom_call_target="tpu_custom_call" | custom-call | tf_op jit(solution)/shard_map/unpack/pallas_call | solution.py:251
  (5 shorter events, 0.1 us)
Async XLA Ops:
  0.0 1.1 %slice-start = ((f32[162,4,512]{2,1,0:T(4,128)}), f32[78,4,512]{2,1,0:T(4,128)S(1)}, s32[]{:S(2)}) async-start(f32[162,4,512]{2,1,0:T(4,128)} %param.7), calls=%async_computation.3 | async-start | bytes 1277952 | tf_op jit(solution)/shard_map/slice | solution.py:209
  1.1 3.8 %slice-start.1 = ((f32[162,4,512]{2,1,0:T(4,128)}), f32[84,4,512]{2,1,0:T(4,128)S(1)}, s32[]{:S(2)}) async-start(f32[162,4,512]{2,1,0:T(4,128)} %param.7), calls=%async_computation.4 | async-start | bytes 1376256 | tf_op jit(solution)/shard_map/slice | solution.py:209
  1.2 25.8 %collective-permute-start.1 = (f32[79,4,512]{2,1,0:T(4,128)S(1)}, f32[79,4,512]{2,1,0:T(4,128)S(1)}, u32[]{:S(2)}, u32[]{:S(2)}) collective-permute-start(f32[79,4,512]{2,1,0:T(4,128)S(1)} %pad_maximum_fusion.1.own_ref), channel_id=1, source_target_pairs={{0,1},{1,2},{2,3},{3,4},{4,5},{5,6},{6,7},{7,8},{8,9},{9,10},{10,1... | collective-permute-start | bytes 1941512 | tf_op jit(solution)/shard_map/ppermute | solution.py:211
  5.1 36.9 %collective-permute-start = (f32[85,4,512]{2,1,0:T(4,128)S(1)}, f32[85,4,512]{2,1,0:T(4,128)S(1)}, u32[]{:S(2)}, u32[]{:S(2)}) collective-permute-start(f32[85,4,512]{2,1,0:T(4,128)S(1)} %pad_maximum_fusion.own_ref), channel_id=1, source_target_pairs={{0,1},{1,2},{2,3},{3,4},{4,5},{5,6},{6,7},{7,8},{8,9},{9,10},{10,1... | collective-permute-start | bytes 2088968 | tf_op jit(solution)/shard_map/ppermute | solution.py:211
  30.1 17.2 %all-to-all-start.1 = ((f32[8,160,128]{2,1,0:T(8,128)}), f32[8,160,128]{2,1,0:T(8,128)S(1)}, u32[]{:S(2)}, u32[]{:S(2)}) async-start(f32[8,160,128]{2,1,0:T(8,128)} %propagate_1.1), calls=%async_computation.1 | async-start | bytes 1310720 | tf_op jit(solution)/shard_map/all_to_all | solution.py:237
  36.5 15.2 %copy-start = (s32[4,1296]{1,0:T(4,128)S(1)}, s32[4,1296]{1,0:T(4,128)}, u32[]{:S(2)}) copy-start(s32[4,1296]{1,0:T(4,128)} %param.9) | copy-start | bytes 62212
  36.5 15.3 %copy-start.1 = (s32[8,2,4]{1,0,2:T(8,128)S(1)}, s32[8,2,4]{1,0,2:T(8,128)}, u32[]{:S(2)}) copy-start(s32[8,2,4]{1,0,2:T(8,128)} %constant.52.clone) | copy-start | bytes 772
  45.0 7.5 %copy-start.2 = (f32[1296]{0:T(1024)S(1)}, f32[1296]{0:T(1024)}, u32[]{:S(2)}) copy-start(f32[1296]{0:T(1024)} %param.10) | copy-start | bytes 15556
  45.0 7.7 %copy-start.3 = (f32[1296]{0:T(1024)S(1)}, f32[1296]{0:T(1024)}, u32[]{:S(2)}) copy-start(f32[1296]{0:T(1024)} %param.11) | copy-start | bytes 15556
  47.3 15.6 %all-to-all-start = ((f32[8,168,128]{2,1,0:T(8,128)}), f32[8,168,128]{2,1,0:T(8,128)S(1)}, u32[]{:S(2)}, u32[]{:S(2)}) async-start(f32[8,168,128]{2,1,0:T(8,128)} %propagate_0.1), calls=%async_computation | async-start | bytes 1376256 | tf_op jit(solution)/shard_map/all_to_all | solution.py:237
